TPU v7x, 32 devices: a whole 2x2x4 slice. The times are simulated.
32 devices in a mesh: parts: 2 (over x), seq: 16 (over z, y, core).
Axes of the slice: x: 2, y: 2, z: 4, core: 2. Of those that a mesh axis runs over, the one named last changes fastest.
Arguments:
- x_state: bfloat16 [32, 64, 384], P(('parts', 'seq')), parts along dimension 0, may hold values from -6 to 6
- noise_field: bfloat16 [32, 64, 384], P(('parts', 'seq')), parts along dimension 0, may hold values from -6 to 6
- rotations: float32 [9, 32, 64], P(None, ('parts', 'seq')), parts along dimension 1, may hold values from -1 to 1, as said below
- translations: float32 [3, 32, 64], P(None, ('parts', 'seq')), parts along dimension 1, may hold values from -15 to 15
- residue_types: int32 [128], P('parts'), parts along dimension 0, may hold values from 0 to 20
- pocket_mask: int32 [128], P('parts'), parts along dimension 0, may hold values 0 or 1
- type_table: bfloat16 [21, 384], replicated, may hold values from -3 to 3
- null_embed: bfloat16 [384], replicated, may hold values from -3 to 3
- spatial_gain: float32 [384], replicated, may hold values from 0.25 to 1.75
- spatial_proj: bfloat16 [384, 1152], replicated, may hold values from -0.3125 to 0.3125
- spatial_points: bfloat16 [384, 288], replicated, may hold values from -0.3125 to 0.3125
- spatial_gamma: float32 [12], replicated, may hold values from 0.2 to 2
- spatial_out: bfloat16 [384, 384], replicated, may hold values from -0.3125 to 0.3125
- temporal_gain: float32 [384], replicated, may hold values from 0.25 to 1.75
- temporal_proj: bfloat16 [384, 1152], replicated, may hold values from -0.3125 to 0.3125
- temporal_out: bfloat16 [384, 384], replicated, may hold values from -0.3125 to 0.3125
- hidden_gain: float32 [384], replicated, may hold values from 0.25 to 1.75
- hidden_in: bfloat16 [384, 1536], replicated, may hold values from -0.3125 to 0.3125
- hidden_out: bfloat16 [1536, 384], replicated, may hold values from -0.15625 to 0.15625
- head_gain: float32 [384], replicated, may hold values from 0.25 to 1.75
- head_out: bfloat16 [384, 384], replicated, may hold values from -0.3125 to 0.3125
Outputs:
- x_next: bfloat16 [32, 64, 384], P(('parts', 'seq')), parts along dimension 0
- velocity: bfloat16 [32, 64, 384], P(('parts', 'seq')), parts along dimension 0
There are 2 independent parts, one for each index of `parts`. A program takes and returns all parts, laid end to end along the dimension named above; an argument that names none is the same for every part. Nothing has to cross between parts.
Inputs may be any that keep to these rules, and one draw needn't show every extreme that they name: `rotations`: each column over the first dimension is a proper rotation matrix, row-major.
All inputs are finite; a program needn't handle non-finite values.
Results may differ from a plain program's by a relative error of at most 0.015.
Values may be sent and summed in bfloat16 or wider, within the bound.
No kernel may reach another device: no remote copies, remote signals or barrier semaphores. Data moves between devices by JAX's collectives and lax.ppermute only.
A program may use at most 64 MiB of HBM per device.

v0:
```python
import jax
import jax.numpy as jnp
from jax import lax
from jax.sharding import PartitionSpec as P

THEADS = 6


WEIGHT_LOGIT = 0.7071067811865476
WEIGHT_POINT = 0.23570226039551584
GUIDE = 2.0
STEP_SIZE = 0.25
NOISE_SCALE = 0.2
EPSILON = 1e-05


def layer_norm(values, scale_gain):
    average = jnp.mean(values, axis=-1, keepdims=True)
    centered = values - average
    spread = jnp.mean(centered * centered, axis=-1, keepdims=True)
    return centered * lax.rsqrt(spread + EPSILON) * scale_gain


def softmax_rows(logits):
    row_max = jnp.max(logits, axis=-1, keepdims=True)
    powers = jnp.exp(logits - row_max)
    return powers / jnp.sum(powers, axis=-1, keepdims=True)


def branch_embed(residue_types, type_table, null_embed):
    count = type_table.shape[0]
    onehot = (residue_types[:, None] == jnp.arange(count, dtype=jnp.int32)[None, :]).astype(
        jnp.bfloat16
    )
    conditional = jnp.dot(onehot, type_table, preferred_element_type=jnp.float32)
    empty = jnp.broadcast_to(null_embed.astype(jnp.float32)[None, :], conditional.shape)
    return jnp.stack([conditional, empty])


def spatial_frame(state, rotation, translation, embedding, allowed, weights):
    spatial_gain, spatial_proj, spatial_points, spatial_gamma, spatial_out = weights
    branches, residues, model_width = embedding.shape
    head_count = spatial_gamma.shape[0]
    head_dim = model_width // head_count
    initial = state.astype(jnp.float32)[None] + embedding
    normed = (
        layer_norm(initial, spatial_gain)
        .astype(jnp.bfloat16)
        .reshape(branches * residues, model_width)
    )
    projected = jnp.dot(normed, spatial_proj, preferred_element_type=jnp.float32).astype(
        jnp.bfloat16
    )
    projected = projected.reshape(branches, residues, 3, head_count, head_dim)
    points = jnp.dot(normed, spatial_points, preferred_element_type=jnp.float32)
    points = points.reshape(branches, residues, 2, head_count, -1, 3)
    centred = translation - jnp.mean(translation, axis=1, keepdims=True)
    turned = jnp.einsum(
        "der,brshpe->bshpdr",
        rotation.reshape(3, 3, residues),
        points,
        precision=lax.Precision.HIGHEST,
    )
    placed = turned + centred
    query_points = placed[:, 0].reshape(branches, head_count, -1, residues)
    key_points = placed[:, 1].reshape(branches, head_count, -1, residues)
    pairwise = jnp.einsum(
        "bhcr,bhcs->bhrs", query_points, key_points, precision=lax.Precision.HIGHEST
    )
    query_norm = jnp.sum(query_points * query_points, axis=2)
    key_norm = jnp.sum(key_points * key_points, axis=2)
    distance = query_norm[..., :, None] + key_norm[..., None, :] - 2.0 * pairwise
    scalar = jnp.einsum(
        "brhc,bshc->bhrs",
        projected[:, :, 0],
        projected[:, :, 1],
        preferred_element_type=jnp.float32,
    )
    logits = (
        WEIGHT_LOGIT * scalar / jnp.sqrt(jnp.float32(head_dim))
        - 0.5 * WEIGHT_LOGIT * WEIGHT_POINT * spatial_gamma[None, :, None, None] * distance
    )
    logits = jnp.where(allowed[None, None], logits, -jnp.inf)
    attend = softmax_rows(logits).astype(jnp.bfloat16)
    context = jnp.einsum(
        "bhrs,bshc->brhc", attend, projected[:, :, 2], preferred_element_type=jnp.float32
    ).astype(jnp.bfloat16)
    update = jnp.dot(
        context.reshape(branches * residues, model_width),
        spatial_out,
        preferred_element_type=jnp.float32,
    )
    return (initial + update.reshape(branches, residues, model_width)).astype(jnp.bfloat16)


def temporal_block(states, weights):
    temporal_gain, temporal_proj, temporal_out, hidden_gain, hidden_in, hidden_out = weights
    frames, branches, residues, model_width = states.shape
    head_dim = model_width // THEADS
    initial = states.astype(jnp.float32)
    normed = layer_norm(initial, temporal_gain).astype(jnp.bfloat16).reshape(-1, model_width)
    projected = jnp.dot(normed, temporal_proj, preferred_element_type=jnp.float32).astype(
        jnp.bfloat16
    )
    projected = projected.reshape(frames, branches, residues, 3, THEADS, head_dim)
    scores = jnp.einsum(
        "qbrhc,kbrhc->brhqk",
        projected[:, :, :, 0],
        projected[:, :, :, 1],
        preferred_element_type=jnp.float32,
    ) / jnp.sqrt(jnp.float32(head_dim))
    attend = softmax_rows(scores).astype(jnp.bfloat16)
    context = jnp.einsum(
        "brhqk,kbrhc->qbrhc", attend, projected[:, :, :, 2], preferred_element_type=jnp.float32
    ).astype(jnp.bfloat16)
    after_time = initial + jnp.dot(
        context.reshape(-1, model_width), temporal_out, preferred_element_type=jnp.float32
    ).reshape(states.shape)
    second = layer_norm(after_time, hidden_gain).astype(jnp.bfloat16).reshape(-1, model_width)
    feed_hidden = jax.nn.gelu(
        jnp.dot(second, hidden_in, preferred_element_type=jnp.float32)
    ).astype(jnp.bfloat16)
    result = after_time + jnp.dot(
        feed_hidden, hidden_out, preferred_element_type=jnp.float32
    ).reshape(states.shape)
    return result.astype(jnp.bfloat16)


def velocity_head(states, head_gain, head_out):
    model_width = states.shape[-1]
    normed = (
        layer_norm(states.astype(jnp.float32), head_gain)
        .astype(jnp.bfloat16)
        .reshape(-1, model_width)
    )
    branch_velocity = jnp.dot(normed, head_out, preferred_element_type=jnp.float32).reshape(
        states.shape
    )
    guided = branch_velocity[:, 1] + GUIDE * (branch_velocity[:, 0] - branch_velocity[:, 1])
    return guided.astype(jnp.bfloat16)


def body(
    x_state,
    noise_field,
    rotations,
    translations,
    residue_types,
    pocket_mask,
    type_table,
    null_embed,
    spatial_gain,
    spatial_proj,
    spatial_points,
    spatial_gamma,
    spatial_out,
    temporal_gain,
    temporal_proj,
    temporal_out,
    hidden_gain,
    hidden_in,
    hidden_out,
    head_gain,
    head_out,
):
    embedding = branch_embed(residue_types, type_table, null_embed)
    residues = x_state.shape[1]
    allowed = (pocket_mask[None, :] == 1) | jnp.eye(residues, dtype=bool)
    spatial_weights = (spatial_gain, spatial_proj, spatial_points, spatial_gamma, spatial_out)
    time_weights = (temporal_gain, temporal_proj, temporal_out, hidden_gain, hidden_in, hidden_out)

    def one_frame(pieces):
        return spatial_frame(pieces[0], pieces[1], pieces[2], embedding, allowed, spatial_weights)

    spatial = lax.map(
        one_frame, (x_state, jnp.moveaxis(rotations, 1, 0), jnp.moveaxis(translations, 1, 0))
    )
    mixed = temporal_block(
        lax.all_to_all(spatial, "seq", split_axis=2, concat_axis=0, tiled=True), time_weights
    )
    guided_part = velocity_head(mixed, head_gain, head_out)
    velocity = lax.all_to_all(guided_part, "seq", split_axis=0, concat_axis=1, tiled=True)
    x_next = (
        x_state.astype(jnp.float32)
        + STEP_SIZE * velocity.astype(jnp.float32)
        + NOISE_SCALE * noise_field.astype(jnp.float32)
    ).astype(jnp.bfloat16)
    return (x_next, velocity)


def solution(mesh):
    return jax.shard_map(
        body,
        mesh=mesh,
        in_specs=(
            P(("parts", "seq"), None, None),
            P(("parts", "seq"), None, None),
            P(None, ("parts", "seq"), None),
            P(None, ("parts", "seq"), None),
            P("parts"),
            P("parts"),
            P(),
            P(),
            P(),
            P(),
            P(),
            P(),
            P(),
            P(),
            P(),
            P(),
            P(),
            P(),
            P(),
            P(),
            P(),
        ),
        out_specs=(P(("parts", "seq"), None, None), P(("parts", "seq"), None, None)),
        check_vma=False,
    )
```

profile of v0, /device:TPU:0, one launch (start us, length us, event | category | flops | bytes accessed | tf_op | source)
XLA Modules:
  0.0 59.1 jit_solution(8017859791696662702)
XLA Ops:
  0.6 0.0 copy-start
  0.6 0.9 %convert_bitcast_fusion = f32[64,384]{1,0:T(8,128)S(1)} fusion(bf16[1,64,384]{2,1,0:T(8,128)(2,1)} %param.21), kind=kLoop, calls=%fused_computation.82 | loop fusion | flops 24576 | bytes 147456 | tf_op jit(solution)/shard_map/while/body/eval_jaxpr/add | solution.py:45
  1.5 0.9 %convolution_bitcast_fusion = f32[1,64,384]{2,1,0:T(8,128)S(1)} fusion(bf16[21,384]{1,0:T(8,128)(2,1)} %param.27, s32[64]{0:T(128)} %param.25), kind=kOutput, calls=%fused_computation.24 | convolution fusion | flops 1033536 | bytes 114688 | tf_op jit(solution)/shard_map/dot_general | solution.py:35
  2.5 0.7 %stack_broadcast_in_dim.2 = f32[1,64,384]{2,1,0:T(8,128)S(1)} broadcast(bf16[384]{0:T(512)(128)(2,1)} %param.28), dimensions={2} | broadcast | bytes 99072 | tf_op jit(solution)/shard_map/stack;broadcast_in_dim | solution.py:37
  3.2 0.1 fusion.76
  3.3 0.2 multiply_reduce_fusion.3
  3.5 0.1 div.67
  3.6 0.1 rsqrt.41
  3.6 0.8 %fusion.43 = bf16[128,384]{1,0:T(8,128)(2,1)S(1)} fusion(f32[2,64,384]{2,1,0:T(8,128)S(1)} %get-tuple-element.51, f32[384]{0:T(512)} %param.29, f32[128]{0:T(128)S(1)} %rsqrt.41, f32[128]{0:T(128)S(1)} %div.67), kind=kLoop, calls=%fused_computation.69 | loop fusion | flops 196608 | bytes 297472 | tf_op jit(solution)/shard_map/while/body/eval_jaxpr/convert_element_type | solution.py:48
  4.5 1.5 %convolution_convert_fusion.1 = bf16[128,1152]{1,0:T(8,128)(2,1)S(1)} fusion(bf16[128,384]{1,0:T(8,128)(2,1)S(1)} %fusion.43, bf16[384,1152]{1,0:T(8,128)(2,1)} %param.30), kind=kOutput, calls=%fused_computation.3 | convolution fusion | flops 113393664 | bytes 1277952 | tf_op jit(solution)/shard_map/while/body/eval_jaxpr/dot_general | solution.py:51
  6.0 0.2 copy.97
  6.2 0.3 reshape.240
  6.5 1.3 %fusion.79 = (bf16[2,64,1,12,32]{1,0,4,3,2:T(2,128)(2,1)}, bf16[2,64,1,12,32]{1,0,4,3,2:T(2,128)(2,1)}, bf16[2,64,1,12,32]{1,0,4,3,2:T(2,128)(2,1)}) fusion(bf16[2,64,3,12,32]{1,0,4,3,2:T(2,128)(2,1)S(1)} %reshape.240), kind=kLoop, calls=%fused_computation.127 | loop fusion | bytes 589824 | tf_op jit(solution)/shard_map/while/body/eval_jaxpr/slice | solution.py:86
  7.8 0.1 dot_general.64
  7.9 1.1 %fusion.31 = f32[2,64,2,12,4,3]{1,3,5,4,2,0:T(8,128)} fusion(bf16[2,12,4,3,384]{4,3,2,1,0:T(4,128)(2,1)S(1)} %dot_general.64, f32[384]{0:T(512)S(1)} %copy-done.12, f32[2,64]{1,0:T(2,128)S(1)} %add_rsqrt_fusion.3, f32[2,64]{1,0:T(2,128)S(1)} %broadcast_multiply_fusion.3, f32[1,64,384]{2,1,0:T(8,128)S(1)} %stack_broadcast_in_dim.2, ...), kind=kOutput, calls=%fused_computation.46 | convolution fusion | flops 28606464 | bytes 666112 | tf_op jit(solution)/shard_map/while/body/eval_jaxpr/dot_general | solution.py:55
  9.0 3.2 %copy.102 = f32[2,64,2,12,4,3]{3,5,4,2,0,1:T(4,128)S(1)} copy(f32[2,64,2,12,4,3]{1,3,5,4,2,0:T(8,128)} %fusion.31) | data formatting | bytes 294912 | tf_op jit(solution)/shard_map/while/body/eval_jaxpr/dot_general | solution.py:55
  12.3 0.8 %copy.127 = f32[3,3,64,1,1,1]{1,0,5,4,3,2:T(4,128)} copy(f32[3,3,64,1,1,1]{2,1,0,5,4,3:T(4,128)S(1)} %bitcast.132) | data formatting | bytes 4608 | tf_op jit(solution)/shard_map/while/body/eval_jaxpr/reshape | solution.py:60
  13.1 0.1 reduce_sum.125
  13.2 0.1 bitcast_subtract_fusion.2
  13.3 0.1 copy.104
  13.4 4.8 %bitcast_add_fusion = f32[2,2,12,4,3,64]{2,4,3,1,0,5:T(4,128)S(1)} fusion(f32[2,64,2,12,4,3]{3,5,4,2,0,1:T(4,128)S(1)} %copy.102, f32[3,3,64,1,1,1]{1,0,5,4,3,2:T(4,128)} %copy.127, f32[3,64]{0,1:T(8,128)S(1)} %copy.104), kind=kOutput, calls=%fused_computation.4 | convolution fusion | flops 1363968 | bytes 297984 | tf_op jit(solution)/shard_map/while/body/eval_jaxpr/der,brshpe->bshpdr/dot_general | solution.py:58
  18.2 2.0 %multiply_reduce_fusion.1 = (f32[2,12,64]{1,0,2:T(2,128)}, f32[2,12,64]{1,0,2:T(2,128)S(1)}, f32[2,1,12,4,3,64]{2,4,3,1,0,5:T(4,128)S(1)}, f32[2,1,12,4,3,64]{2,4,3,1,0,5:T(4,128)S(1)}) fusion(f32[2,2,12,4,3,64]{2,4,3,1,0,5:T(4,128)S(1)} %bitcast_add_fusion), kind=kLoop, calls=%fused_computation.26 | loop fusion | flops 70656 | bytes 307200 | tf_op jit(solution)/shard_map/while/body/eval_jaxpr/reduce_sum | solution.py:70
  20.2 1.4 %copy.107 = f32[2,1,12,4,3,64]{5,0,4,3,2,1:T(2,128)} copy(f32[2,1,12,4,3,64]{2,4,3,1,0,5:T(4,128)S(1)} %get-tuple-element.30) | data formatting | bytes 147456 | tf_op jit(solution)/shard_map/while/body/eval_jaxpr/slice | solution.py:65
  21.6 0.7 %copy.108 = f32[2,1,12,4,3,64]{5,0,4,3,2,1:T(2,128)S(1)} copy(f32[2,1,12,4,3,64]{2,4,3,1,0,5:T(4,128)S(1)} %get-tuple-element.31) | data formatting | bytes 147456 | tf_op jit(solution)/shard_map/while/body/eval_jaxpr/slice | solution.py:66
  22.3 1.0 %copy.105 = f32[2,12,64]{2,1,0:T(8,128)S(1)} copy(f32[2,12,64]{1,0,2:T(2,128)} %get-tuple-element.26) | data formatting | bytes 12288 | tf_op jit(solution)/shard_map/while/body/eval_jaxpr/reduce_sum | solution.py:70
  23.3 0.1 copy.106
  23.4 0.1 fusion.66
  23.5 1.3 %convolution_multiply_fusion.1 = f32[2,12,64,64]{2,3,1,0:T(8,128)S(1)} fusion(bf16[2,64,1,12,32]{1,0,4,3,2:T(2,128)(2,1)} %get-tuple-element.49, bf16[2,64,1,12,32]{1,0,4,3,2:T(2,128)(2,1)} %get-tuple-element.48), kind=kOutput, calls=%fused_computation.11 | convolution fusion | flops 6389760 | bytes 589824 | tf_op jit(solution)/shard_map/while/body/eval_jaxpr/brhc,bshc->bhrs/dot_general | solution.py:73
  24.8 1.5 %fusion.7 = f32[2,12,64,64]{2,3,1,0:T(8,128)S(1)} fusion(f32[2,12,64,64]{2,3,1,0:T(8,128)S(1)} %convolution_multiply_fusion.1, f32[2,12,64]{2,1,0:T(8,128)S(1)} %copy.106, f32[2,12,64]{2,1,0:T(8,128)S(1)} %copy.105, f32[12]{0:T(128)S(1)} %broadcast_multiply_fusion.5, pred[64,64]{0,1:T(8,128)(4,1)S(1)} %fusion.66, f32[2,12,12,64]{3,0,2,1:T(2,128)S(1)} %bitcast.128, ...), kind=kOutput, calls=%fused_computation.12 | convolution fusion | flops 14745600 | bytes 950320 | tf_op jit(solution)/shard_map/while/body/eval_jaxpr/bhcr,bhcs->bhrs/dot_general | solution.py:67
  26.4 0.2 fusion.80
  26.6 0.3 convolution_convert_fusion.3
  26.9 0.3 copy-done.2
  27.2 1.2 %fusion.12 = bf16[1,2,64,384]{3,2,1,0:T(8,128)(2,1)S(1)} fusion(bf16[2,64,384]{1,2,0:T(8,128)(2,1)S(1)} %bitcast.131, bf16[384,384]{1,0:T(8,128)(2,1)} %param.33, f32[1,64,384]{2,1,0:T(8,128)S(1)} %copy-done.2, f32[1,64,384]{2,1,0:T(8,128)S(1)} %convolution_bitcast_fusion, f32[64,384]{1,0:T(8,128)S(1)} %convert_bitcast_fusion), kind=kOutput, calls=%fused_computation.23 | convolution fusion | flops 37945344 | bytes 786432 | tf_op jit(solution)/shard_map/while/body/eval_jaxpr/dot_general | solution.py:88
  28.5 0.1 copy.113
  28.6 14.6 %all_to_all.21 = bf16[1,2,64,384]{3,1,0,2:T(2,128)(2,1)S(1)} all-to-all(bf16[1,2,64,384]{3,1,0,2:T(2,128)(2,1)S(1)} %copy.113), channel_id=1, replica_groups=mesh['parts'=2,'seq'=16] {'seq'}, dimensions={2} | all-to-all | bytes 196608 | tf_op jit(solution)/shard_map/all_to_all | solution.py:179
  43.2 0.1 convert.5
  43.3 0.1 fusion.75
  43.4 0.2 fusion.40
  43.6 0.1 copy.116
  43.7 0.1 copy.117
  43.8 0.1 rsqrt.43
  43.9 0.1 copy.115
  44.0 0.1 reshape.245
  44.1 0.1 div.75
  44.2 0.4 convolution_convert_fusion
  44.6 0.4 reshape.242
  45.0 0.2 fusion.78
  45.3 0.3 convolution_multiply_fusion.2
  45.6 0.4 fusion.81
  46.0 0.3 fusion.10
  46.4 0.1 copy.122
  46.5 0.2 dot_general.74
  46.7 0.3 fusion.82
  47.0 0.2 multiply_reduce_fusion.2
  47.2 0.1 multiply_convert_fusion
  47.4 0.3 copy-done.18
  47.7 0.7 %fusion.21 = f32[128,384]{1,0:T(8,128)S(1)} fusion(bf16[1536,384]{1,0:T(8,128)(2,1)S(1)} %copy-done, bf16[128,384]{1,0:T(8,128)(2,1)S(1)} %reshape.243, bf16[384,1536]{1,0:T(8,128)(2,1)S(1)} %copy-done.18), kind=kOutput, calls=%fused_computation.36 | convolution fusion | flops 303759360 | bytes 2654208 | tf_op jit(solution)/shard_map/dot_general | solution.py:123
  48.4 0.1 reshape.244
  48.4 0.1 convert_reduce_fusion
  48.6 0.2 fusion.36
  48.8 0.3 fusion.27
  49.1 9.3 %all_to_all.22 = bf16[16,4,384]{2,1,0:T(4,128)(2,1)S(1)} all-to-all(bf16[16,4,384]{2,1,0:T(4,128)(2,1)S(1)} %copy.125), channel_id=1, replica_groups=mesh['parts'=2,'seq'=16] {'seq'}, dimensions={0} | all-to-all | bytes 98304 | tf_op jit(solution)/shard_map/all_to_all | solution.py:182
  58.5 0.0 copy-start.9
  58.5 0.6 %fusion.49 = bf16[1,64,384]{2,1,0:T(8,128)(2,1)} fusion(bf16[1,64,384]{2,1,0:T(8,128)(2,1)S(1)} %copy-done.10, bf16[1,64,384]{2,1,0:T(8,128)(2,1)S(1)} %copy-done.11, bf16[1,64,384]{2,1,0:T(8,128)(2,1)S(1)} %all_to_all.8), kind=kLoop, calls=%fused_computation.84 | loop fusion | flops 196608 | bytes 196608 | tf_op jit(solution)/shard_map/convert_element_type | solution.py:187
  (57 shorter events, 0.3 us)
Async XLA Ops:
  0.6 46.8 %copy-start = (bf16[1536,384]{1,0:T(8,128)(2,1)S(1)}, bf16[1536,384]{1,0:T(8,128)(2,1)}, u32[]{:S(2)}) copy-start(bf16[1536,384]{1,0:T(8,128)(2,1)} %param.39) | copy-start | bytes 3538948
  3.2 4.7 %copy-start.1 = (f32[1,64,384]{2,1,0:T(8,128)}, f32[1,64,384]{2,1,0:T(8,128)S(1)}, u32[]{:S(2)}) copy-start(f32[1,64,384]{2,1,0:T(8,128)S(1)} %stack_broadcast_in_dim.2) | copy-start | bytes 294916
  3.6 4.2 %copy-start.7 = (bf16[384,288]{0,1:T(8,128)(2,1)S(1)}, bf16[384,288]{0,1:T(8,128)(2,1)}, u32[]{:S(2)}) copy-start(bf16[384,288]{0,1:T(8,128)(2,1)} %param.31) | copy-start | bytes 663556
  4.5 3.4 %copy-start.12 = (f32[384]{0:T(512)S(1)}, f32[384]{0:T(512)}, u32[]{:S(2)}) copy-start(f32[384]{0:T(512)} %param.29) | copy-start | bytes 4612
  7.8 4.5 %copy-start.14 = (f32[9,1,64]{2,1,0:T(1,128)S(1)}, f32[9,1,64]{2,1,0:T(1,128)}, u32[]{:S(2)}) copy-start(f32[9,1,64]{2,1,0:T(1,128)} %param.23) | copy-start | bytes 6916
  7.8 5.3 %copy-start.13 = (f32[3,1,64]{2,1,0:T(1,128)S(1)}, f32[3,1,64]{2,1,0:T(1,128)}, u32[]{:S(2)}) copy-start(f32[3,1,64]{2,1,0:T(1,128)} %param.24) | copy-start | bytes 2308
  20.2 3.2 %copy-start.19 = (s32[64]{0:T(128)S(1)}, s32[64]{0:T(128)}, u32[]{:S(2)}) copy-start(s32[64]{0:T(128)} %param.26) | copy-start | bytes 772
  20.2 3.3 %copy-start.20 = (f32[12]{0:T(128)S(1)}, f32[12]{0:T(128)}, u32[]{:S(2)}) copy-start(f32[12]{0:T(128)} %param.32) | copy-start | bytes 148
  21.6 3.3 %copy-start.4 = (f32[2,1,12,4,3,64]{5,0,4,3,2,1:T(2,128)S(1)}, f32[2,1,12,4,3,64]{5,0,4,3,2,1:T(2,128)}, u32[]{:S(2)}) copy-start(f32[2,1,12,4,3,64]{5,0,4,3,2,1:T(2,128)} %copy.107) | copy-start | bytes 221188
  22.3 4.3 %copy-start.8 = (bf16[2,64,1,12,32]{1,0,4,3,2:T(2,128)(2,1)S(1)}, bf16[2,64,1,12,32]{1,0,4,3,2:T(2,128)(2,1)}, u32[]{:S(2)}) copy-start(bf16[2,64,1,12,32]{1,0,4,3,2:T(2,128)(2,1)} %get-tuple-element.35) | copy-start | bytes 294916
  26.4 0.9 %copy-start.2 = (f32[1,64,384]{2,1,0:T(8,128)S(1)}, f32[1,64,384]{2,1,0:T(8,128)}, u32[]{:S(2)}) copy-start(f32[1,64,384]{2,1,0:T(8,128)} %copy-done.1) | copy-start | bytes 294916
  26.9 17.3 %copy-start.3 = (bf16[384,1152]{1,0:T(8,128)(2,1)S(1)}, bf16[384,1152]{1,0:T(8,128)(2,1)}, u32[]{:S(2)}) copy-start(bf16[384,1152]{1,0:T(8,128)(2,1)} %param.35) | copy-start | bytes 2654212
  26.9 17.3 %copy-start.15 = (f32[384]{0:T(512)S(1)}, f32[384]{0:T(512)}, u32[]{:S(2)}) copy-start(f32[384]{0:T(512)} %param.34) | copy-start | bytes 4612
  45.6 1.1 %copy-start.5 = (bf16[384,384]{1,0:T(8,128)(2,1)S(1)}, bf16[384,384]{1,0:T(8,128)(2,1)}, u32[]{:S(2)}) copy-start(bf16[384,384]{1,0:T(8,128)(2,1)} %param.36) | copy-start | bytes 884740
  46.0 1.2 %copy-start.16 = (f32[384]{0:T(512)S(1)}, f32[384]{0:T(512)}, u32[]{:S(2)}) copy-start(f32[384]{0:T(512)} %param.37) | copy-start | bytes 4612
  46.4 1.3 %copy-start.18 = (bf16[384,1536]{1,0:T(8,128)(2,1)S(1)}, bf16[384,1536]{1,0:T(8,128)(2,1)}, u32[]{:S(2)}) copy-start(bf16[384,1536]{1,0:T(8,128)(2,1)} %param.38) | copy-start | bytes 3538948
  47.6 1.1 %copy-start.6 = (bf16[384,384]{1,0:T(8,128)(2,1)S(1)}, bf16[384,384]{1,0:T(8,128)(2,1)}, u32[]{:S(2)}) copy-start(bf16[384,384]{1,0:T(8,128)(2,1)} %param.41) | copy-start | bytes 884740
  47.6 1.1 %copy-start.17 = (f32[384]{0:T(512)S(1)}, f32[384]{0:T(512)}, u32[]{:S(2)}) copy-start(f32[384]{0:T(512)} %param.40) | copy-start | bytes 4612
  47.6 10.8 %copy-start.10 = (bf16[1,64,384]{2,1,0:T(8,128)(2,1)S(1)}, bf16[1,64,384]{2,1,0:T(8,128)(2,1)}, u32[]{:S(2)}) copy-start(bf16[1,64,384]{2,1,0:T(8,128)(2,1)} %param.21) | copy-start | bytes 147460
  47.6 10.8 %copy-start.11 = (bf16[1,64,384]{2,1,0:T(8,128)(2,1)S(1)}, bf16[1,64,384]{2,1,0:T(8,128)(2,1)}, u32[]{:S(2)}) copy-start(bf16[1,64,384]{2,1,0:T(8,128)(2,1)} %param.22) | copy-start | bytes 147460
  58.5 0.7 %copy-start.9 = (bf16[1,64,384]{2,1,0:T(8,128)(2,1)}, bf16[1,64,384]{2,1,0:T(8,128)(2,1)S(1)}, u32[]{:S(2)}) copy-start(bf16[1,64,384]{2,1,0:T(8,128)(2,1)S(1)} %all_to_all.8) | copy-start | bytes 147460
where the time goes:
time: 59.6 us; the launch traced here: 59.1 us
  blocking collectives  23.9 us (40%)
  matrix products  15.5 us (26%)
  local copies, waits for them, and re-layouts  12.4 us (21%)
  other arithmetic  6.14 us (10%)
  between operations  1.13 us (2%)
    all_to_all x1, blocking collectives, body(): lax.all_to_all(spatial, 'seq', split_axis=2, concat_axis=0, tiled=True)  14.6 us
    all_to_all x1, blocking collectives, body(): lax.all_to_all(guided_part, 'seq', split_axis=0, concat_axis=1, tiled=True)  9.34 us
    dot_general x1, matrix products, spatial_frame(): jnp.einsum('der,brshpe->bshpdr', rotation.reshape(3, 3, residues), points...  4.83 us
    dot_general x2, local copies, waits for them, and re-layouts, spatial_frame(): points = jnp.dot(normed, spatial_points, preferred_element_type=jnp.float32)  3.35 us
    reduce_sum x1, other arithmetic, spatial_frame(): query_norm = jnp.sum(query_points * query_points, axis=2)  1.97 us
    dot_general x1, matrix products, spatial_frame(): jnp.einsum('bhcr,bhcs->bhrs', query_points, key_points, precision=lax.Pre...  1.53 us
    dot_general x1, matrix products, spatial_frame(): jnp.dot(normed, spatial_proj, preferred_element_type=jnp.float32)  1.51 us
    slice x1, local copies, waits for them, and re-layouts, spatial_frame(): query_points = placed[:, 0].reshape(branches, head_count, -1, residues)  1.36 us

commit v1 on v0

v1 whole, which is shorter than its diff:
```python
import functools
import math

import jax
import jax.numpy as jnp
from jax import lax
from jax.experimental import pallas as pl
from jax.experimental.pallas import tpu as pltpu
from jax.sharding import PartitionSpec as P

THEADS = 6
BRANCHES = 2

WEIGHT_LOGIT = 0.7071067811865476
WEIGHT_POINT = 0.23570226039551584
GUIDE = 2.0
STEP_SIZE = 0.25
NOISE_SCALE = 0.2
EPSILON = 1e-05

BF16 = jnp.bfloat16
F32 = jnp.float32
LANES = 128
NT = (((1,), (1,)), ((), ()))


def round_up(value, step):
    return -(-value // step) * step


def layer_norm(values, scale_gain):
    average = jnp.mean(values, axis=-1, keepdims=True)
    centered = values - average
    spread = jnp.mean(centered * centered, axis=-1, keepdims=True)
    return centered * lax.rsqrt(spread + EPSILON) * scale_gain


def matmul(left, right):
    return jnp.dot(left, right, preferred_element_type=F32)


def iota(shape, axis):
    return lax.broadcasted_iota(jnp.int32, shape, axis)


def softmax_down(logits, allowed):
    logits = jnp.where(allowed, logits, -jnp.inf)
    powers = jnp.exp(logits - jnp.max(logits, axis=0, keepdims=True))
    return (powers * (1.0 / jnp.sum(powers, axis=0, keepdims=True))).astype(BF16)


def spatial_kernel(
    groups,
    gamma_ref,
    x_ref,
    rotation_ref,
    translation_ref,
    types_ref,
    mask_ref,
    table_ref,
    null_ref,
    gain_ref,
    proj_ref,
    points_ref,
    spatial_out_ref,
    out_ref,
    columns_ref,
    wide_ref,
    rows_ref,
):
    frames, residues, width = x_ref.shape
    heads = gamma_ref.shape[0]
    head_dim = width // heads
    block_heads = LANES // head_dim
    all_points = points_ref.shape[1]
    half = all_points // 2
    per_head = half // heads
    points_wide = wide_ref.shape[1]
    feature = round_up(half + 2 * heads, LANES)
    share = residues // groups
    fold = max(residues, LANES)
    point_scale = 0.5 * WEIGHT_LOGIT * WEIGHT_POINT

    kinds = table_ref.shape[0]
    onehot = (iota((kinds, residues), 0) == types_ref[...]).astype(F32).T.astype(BF16)
    conditional = matmul(onehot, table_ref[...])
    empty = null_ref[...].astype(F32)

    lane = iota((1, points_wide), 1)
    component = lane % 3
    narrow = iota((1, feature), 1)
    in_points = narrow < half
    in_first = (narrow >= half) & (narrow < half + heads)
    in_second = (narrow >= half + heads) & (narrow < half + 2 * heads)
    member = []
    gamma_lanes = jnp.zeros((1, feature), F32)
    for head in range(heads):
        own = (
            ((narrow >= head * per_head) & (narrow < (head + 1) * per_head))
            | (narrow == half + head)
            | (narrow == half + heads + head)
        )
        member.append(own.astype(F32).astype(BF16))
        gamma_lanes = jnp.where(own, gamma_ref[head], gamma_lanes)
    block_lane = iota((1, LANES), 1)
    block_member = [
        ((block_lane >= part * head_dim) & (block_lane < (part + 1) * head_dim))
        .astype(F32)
        .astype(BF16)
        for part in range(block_heads)
    ]
    row_point = iota((feature, feature), 0)
    column = iota((feature, feature), 1)
    column_head = jnp.where(column >= half + heads, column - half - heads, column - half)
    gather_norm = (
        (
            (column >= half)
            & (column < half + 2 * heads)
            & (row_point >= column_head * per_head)
            & (row_point < (column_head + 1) * per_head)
        )
        .astype(F32)
        .astype(BF16)
    )
    diagonal = iota((LANES, block_heads * residues), 0) // head_dim == (
        iota((LANES, block_heads * residues), 1) // residues
    )

    for frame in range(frames):
        columns_ref[...] = jnp.zeros_like(columns_ref)
        columns_ref[0:9, :] = rotation_ref[:, frame, :]
        moved = translation_ref[:, frame, :]
        columns_ref[9:12, :] = moved - jnp.mean(moved, axis=1, keepdims=True)
        columns_ref[12:13, :] = mask_ref[...].astype(F32)
        columns = columns_ref[...].T
        allowed = (columns[:, 12:13] == 1.0) | (
            iota((residues, residues), 0) == iota((residues, residues), 1)
        )
        allowed = (
            (columns[:, 12:13] == 1.0)
            | (
                iota((residues, block_heads * residues), 0)
                == iota((residues, block_heads * residues), 1) % residues
            )
        )

        state = x_ref[frame].astype(F32)
        initial = jnp.concatenate([state + conditional, state + empty], axis=0)
        normed = layer_norm(initial, gain_ref[...]).astype(BF16)
        projected = matmul(normed, proj_ref[...])
        wide_ref[:, points_wide - LANES :] = jnp.zeros((BRANCHES * residues, LANES), F32)
        wide_ref[:, :all_points] = matmul(normed, points_ref[...])
        points = wide_ref[...]

        placed = None
        for step in range(-2, 3):
            factor = jnp.zeros((residues, points_wide), F32)
            for row in range(3):
                if 0 <= row + step < 3:
                    entry = 3 * row + row + step
                    factor = jnp.where(component == row, columns[:, entry : entry + 1], factor)
            shifted = points if step == 0 else pltpu.roll(points, (-step) % points_wide, 1)
            term = shifted.reshape(BRANCHES, residues, points_wide) * factor[None]
            placed = term if placed is None else placed + term
        anchor = jnp.zeros((residues, points_wide), F32)
        for row in range(3):
            anchor = jnp.where(component == row, columns[:, 9 + row : 10 + row], anchor)
        placed = (placed + anchor[None]).reshape(BRANCHES * residues, points_wide)

        query_points = placed[:, :feature]
        key_points = jnp.where(
            in_points, pltpu.roll(placed, points_wide - half, 1)[:, :feature], 0.0
        )
        query_feature = jnp.where(
            in_points,
            query_points * (gamma_lanes * (2.0 * point_scale)),
            (in_first | in_second).astype(F32),
        )
        query_high = query_feature.astype(BF16)
        query_low = (query_feature - query_high.astype(F32)).astype(BF16)

        square = key_points * key_points
        square_high = square.astype(BF16)
        rest = square - square_high.astype(F32)
        square_middle = rest.astype(BF16)
        square_low = (rest - square_middle.astype(F32)).astype(BF16)
        norm = (
            matmul(square_high, gather_norm)
            + matmul(square_middle, gather_norm)
            + matmul(square_low, gather_norm)
        )
        key_feature = key_points - norm * (gamma_lanes * point_scale)
        high = key_feature.astype(BF16)
        rest = key_feature - high.astype(F32)
        low = rest.astype(BF16)
        last = (rest - low.astype(F32)).astype(BF16)
        key_high = jnp.where(in_second, last, high)
        key_low = jnp.where(in_second, jnp.zeros_like(low), low)

        queries = (
            projected[:, :width].astype(BF16) * jnp.asarray(WEIGHT_LOGIT / math.sqrt(head_dim), BF16)
        )
        keys = projected[:, width : 2 * width].astype(BF16)
        values = projected[:, 2 * width :].astype(BF16).astype(F32)

        contexts = []
        for branch in range(BRANCHES):
            rows = slice(branch * residues, (branch + 1) * residues)
            turned = values[rows].T.astype(BF16)
            pieces = []
            for block in range(width // LANES):
                lanes = slice(block * LANES, (block + 1) * LANES)
                left = jnp.concatenate(
                    [keys[rows, lanes], key_high[rows], key_low[rows], key_high[rows]], axis=1
                )
                stacked = []
                for part in range(block_heads):
                    own = member[block * block_heads + part]
                    upper = query_high[rows] * own
                    stacked.append(
                        jnp.concatenate(
                            [
                                queries[rows, lanes] * block_member[part],
                                upper,
                                upper,
                                query_low[rows] * own,
                            ],
                            axis=1,
                        )
                    )
                logits = lax.dot_general(
                    left, jnp.concatenate(stacked, axis=0), NT, preferred_element_type=F32
                )
                attend = softmax_down(logits, allowed)
                mixed = jnp.where(diagonal, matmul(turned[lanes], attend), 0.0)
                folded = mixed[:, :fold]
                for start in range(fold, block_heads * residues, fold):
                    folded = folded + mixed[:, start : start + fold]
                pieces.append(folded)
            contexts.append(jnp.concatenate(pieces, axis=0).T.astype(BF16))
        update = matmul(jnp.concatenate(contexts, axis=0), spatial_out_ref[...])
        for branch in range(BRANCHES):
            total = initial[branch * residues : (branch + 1) * residues]
            for start in range(0, fold, residues):
                first = branch * fold + start
                total = total + update[first : first + residues]
            place = (frame * BRANCHES + branch) * share
            for group in range(groups):
                rows_ref[group, place : place + share, :] = total[group * share : (group + 1) * share]
    out_ref[...] = rows_ref[...].astype(BF16)


def temporal_kernel(
    period,
    x_ref,
    gain_ref,
    proj_ref,
    temporal_out_ref,
    hidden_gain_ref,
    hidden_in_ref,
    hidden_out_ref,
    head_gain_ref,
    head_out_ref,
    out_ref,
):
    groups, depth, width = x_ref.shape
    rows = groups * depth
    head_dim = width // THEADS
    block_heads = LANES // head_dim
    share = period // BRANCHES

    initial = x_ref[...].astype(F32).reshape(rows, width)
    normed = layer_norm(initial, gain_ref[...]).astype(BF16)
    projected = matmul(normed, proj_ref[...])
    queries = projected[:, :width].astype(BF16) * jnp.asarray(1.0 / math.sqrt(head_dim), BF16)
    keys = projected[:, width : 2 * width].astype(BF16)
    turned = projected[:, 2 * width :].astype(BF16).astype(F32).T.astype(BF16)
    block_lane = iota((1, LANES), 1)
    allowed = (
        iota((rows, block_heads * rows), 0) % period == iota((rows, block_heads * rows), 1) % period
    )
    pieces = []
    for block in range(width // LANES):
        lanes = slice(block * LANES, (block + 1) * LANES)
        stacked = []
        for part in range(block_heads):
            own = (block_lane >= part * head_dim) & (block_lane < (part + 1) * head_dim)
            stacked.append(queries[:, lanes] * own.astype(F32).astype(BF16))
        logits = lax.dot_general(
            keys[:, lanes], jnp.concatenate(stacked, axis=0), NT, preferred_element_type=F32
        )
        attend = softmax_down(logits, allowed)
        mixed = matmul(turned[lanes], attend)
        for part in range(block_heads):
            pieces.append(
                mixed[part * head_dim : (part + 1) * head_dim, part * rows : (part + 1) * rows]
            )
    context = jnp.concatenate(pieces, axis=0).T.astype(BF16)
    after_time = initial + matmul(context, temporal_out_ref[...])
    second = layer_norm(after_time, hidden_gain_ref[...]).astype(BF16)
    hidden = jax.nn.gelu(matmul(second, hidden_in_ref[...])).astype(BF16)
    result = (after_time + matmul(hidden, hidden_out_ref[...])).astype(BF16).astype(F32)
    headed = layer_norm(result, head_gain_ref[...]).astype(BF16)
    branch_velocity = matmul(headed, head_out_ref[...]).reshape(rows // period, period, width)
    conditional = branch_velocity[:, :share]
    empty = branch_velocity[:, share:]
    out_ref[...] = (empty + GUIDE * (conditional - empty)).astype(BF16)


def whole(memory_space=pltpu.VMEM):
    return pl.BlockSpec(memory_space=memory_space)


def body(
    groups,
    x_state,
    noise_field,
    rotations,
    translations,
    residue_types,
    pocket_mask,
    type_table,
    null_embed,
    spatial_gain,
    spatial_proj,
    spatial_points,
    spatial_gamma,
    spatial_out,
    temporal_gain,
    temporal_proj,
    temporal_out,
    hidden_gain,
    hidden_in,
    hidden_out,
    head_gain,
    head_out,
):
    frames, residues, width = x_state.shape
    share = residues // groups
    period = BRANCHES * share
    spatial = pl.pallas_call(
        functools.partial(spatial_kernel, groups),
        out_shape=jax.ShapeDtypeStruct((groups, frames * period, width), BF16),
        in_specs=[whole(pltpu.SMEM)] + [whole()] * 11,
        out_specs=whole(),
        scratch_shapes=[
            pltpu.VMEM((16, residues), F32),
            pltpu.VMEM((BRANCHES * residues, round_up(spatial_points.shape[1], LANES)), F32),
            pltpu.VMEM((groups, frames * period, width), F32),
        ],
        name="spatial",
    )(
        spatial_gamma,
        x_state,
        rotations,
        translations,
        residue_types[None],
        pocket_mask[None],
        type_table,
        null_embed[None],
        spatial_gain[None],
        spatial_proj,
        spatial_points,
        spatial_out,
    )
    arrived = lax.all_to_all(spatial, "seq", split_axis=0, concat_axis=0, tiled=True)
    guided = pl.pallas_call(
        functools.partial(temporal_kernel, period),
        out_shape=jax.ShapeDtypeStruct((groups * frames, share, width), BF16),
        in_specs=[whole()] * 9,
        out_specs=whole(),
        name="temporal",
    )(
        arrived,
        temporal_gain[None],
        temporal_proj,
        temporal_out,
        hidden_gain[None],
        hidden_in,
        hidden_out,
        head_gain[None],
        head_out,
    )
    velocity = lax.all_to_all(guided, "seq", split_axis=0, concat_axis=1, tiled=True)
    x_next = (
        x_state.astype(F32)
        + STEP_SIZE * velocity.astype(F32)
        + NOISE_SCALE * noise_field.astype(F32)
    ).astype(BF16)
    return (x_next, velocity)


def solution(mesh):
    tokens = P(("parts", "seq"), None, None)
    geometry = P(None, ("parts", "seq"), None)
    return jax.shard_map(
        functools.partial(body, mesh.shape["seq"]),
        mesh=mesh,
        in_specs=(tokens, tokens, geometry, geometry, P("parts"), P("parts")) + (P(),) * 15,
        out_specs=(tokens, tokens),
        check_vma=False,
    )
```

time: 59.6 us -> 43.1 us (0.72)
  matrix products: 15.5 us -> 0 us
  blocking collectives: 23.9 us -> 10.2 us
  Pallas kernels: 0 us -> 11.4 us
  starting transfers between devices: 0 us -> 7.39 us
  local copies, waits for them, and re-layouts: 12.4 us -> 6.69 us
  waiting for transfers between devices: 0 us -> 5.7 us
  other arithmetic: 6.14 us -> 0.65 us
    dot_general x14 -> x0, matrix products: 15.1 us -> none  [the longest x1 4.83 us: spatial_frame(): jnp.einsum('der,brshpe->bshpdr', rotation.reshape(3, 3, residues), points...]
    all_to_all x2 -> x1, blocking collectives: 23.9 us -> 10.2 us  [body(): lax.all_to_all(guided, 'seq', split_axis=0, concat_axis=1, tiled=True)]
    pallas_call x0 -> x2, Pallas kernels: none -> 11.4 us  [the longest x1 6.29 us: body(): pl.pallas_call(functools.partial(spatial_kernel, groups), out_shape=jax.S...]
    all_to_all x0 -> x1, starting transfers between devices: none -> 7.39 us  [body(): lax.all_to_all(spatial, 'seq', split_axis=0, concat_axis=0, tiled=True)]
    all_to_all x0 -> x1, waiting for transfers between devices: none -> 5.7 us  [body(): lax.all_to_all(spatial, 'seq', split_axis=0, concat_axis=0, tiled=True)]
    broadcast_in_dim x1 -> x5, local copies, waits for them, and re-layouts: 0.1 us -> 4.17 us  [the longest x1 1.24 us: body(): spatial_gain[None]]
    slice x4 -> x0, local copies, waits for them, and re-layouts: 3.59 us -> none  [the longest x1 1.36 us: spatial_frame(): query_points = placed[:, 0].reshape(branches, head_count, -1, residues)]
    dot_general x3 -> x0, local copies, waits for them, and re-layouts: 3.56 us -> none  [the longest x2 3.35 us: spatial_frame(): points = jnp.dot(normed, spatial_points, preferred_element_type=jnp.float32)]
  transfers between devices with their start and end apart: 0 -> 1, of which waited for: 0 -> 1; matrix products, arithmetic and copies ran while one was open for 0% -> 4% of each run, Pallas kernels for 0% -> 0%
where the time goes in v1:
time: 43.1 us; the launch traced here: 42.7 us
  Pallas kernels  11.4 us (26%)
  blocking collectives  10.2 us (24%)
  starting transfers between devices  7.39 us (17%)
  local copies, waits for them, and re-layouts  6.69 us (16%)
  waiting for transfers between devices  5.7 us (13%)
  between operations  0.7 us (2%)
  other arithmetic  0.65 us (2%)
    all_to_all x1, blocking collectives, body(): lax.all_to_all(guided, 'seq', split_axis=0, concat_axis=1, tiled=True)  10.2 us
    all_to_all x1, starting transfers between devices, body(): lax.all_to_all(spatial, 'seq', split_axis=0, concat_axis=0, tiled=True)  7.39 us
    pallas_call x1, Pallas kernels, body(): pl.pallas_call(functools.partial(spatial_kernel, groups), out_shape=jax.S...  6.29 us
    all_to_all x1, waiting for transfers between devices, body(): lax.all_to_all(spatial, 'seq', split_axis=0, concat_axis=0, tiled=True)  5.7 us
    pallas_call x1, Pallas kernels, body(): pl.pallas_call(functools.partial(temporal_kernel, period), out_shape=jax....  5.1 us
    unnamed x15, local copies, waits for them, and re-layouts  2.5 us
    broadcast_in_dim x1, local copies, waits for them, and re-layouts, body(): spatial_gain[None]  1.24 us
    broadcast_in_dim x1, local copies, waits for them, and re-layouts, body(): null_embed[None]  1.24 us
  transfers between devices with their start and end apart: 1, of which 1 were waited for; matrix products, arithmetic and copies ran while one was open for 4% of the time, Pallas kernels for 0%

profile of v1, /device:TPU:0, one launch (start us, length us, event | category | flops | bytes accessed | tf_op | source)
XLA Modules:
  0.0 42.7 jit_solution(14189037090105961948)
XLA Ops:
  0.6 0.0 copy-start.4
  0.6 0.0 copy-start.5
  0.7 0.0 copy-start.6
  0.7 1.8 %copy.23.points_ref = bf16[384,288]{1,0:T(8,128)(2,1)} copy(bf16[384,288]{0,1:T(8,128)(2,1)} %param.31) | data formatting | bytes 442368 | tf_op args[10]
  2.5 1.2 %broadcast_in_dim.23.null_ref = bf16[1,384]{1,0:T(2,128)(2,1)} reshape(bf16[384]{0:T(512)(128)(2,1)} %param.28) | data formatting | bytes 1536 | tf_op jit(solution)/shard_map/broadcast_in_dim | solution.py:360
  3.7 1.2 %broadcast_in_dim.24.gain_ref = f32[1,384]{1,0:T(1,128)} reshape(f32[384]{0:T(512)} %param.29) | data formatting | bytes 3072 | tf_op jit(solution)/shard_map/broadcast_in_dim | solution.py:361
  5.0 6.3 %spatial.1 = bf16[16,8,384]{2,1,0:T(8,128)(2,1)} custom-call(f32[12]{0:T(128)} %gamma_ref.1, bf16[1,64,384]{2,1,0:T(8,128)(2,1)} %x_ref.1, f32[9,1,64]{2,1,0:T(1,128)} %rotation_ref.1, f32[3,1,64]{2,1,0:T(1,128)} %translation_ref.1, s32[1,64]{1,0:T(1,128)} %bitcast.2, s32[1,64]{1,0:T(1,128)} %bitcast.3, bf16[21,384]{1,0:T(8,128)(2,1)} %table_ref.1, ...), custom_call_target="tpu_custom_call" | custom-call | tf_op jit(solution)/shard_map/spatial/pallas_call | solution.py:341
  11.3 7.4 %all-to-all-start = ((bf16[16,8,384]{2,1,0:T(8,128)(2,1)}), bf16[16,8,384]{2,1,0:T(8,128)(2,1)S(1)}, u32[]{:S(2)}, u32[]{:S(2)}) async-start(bf16[16,8,384]{2,1,0:T(8,128)(2,1)} %spatial.1), calls=%async_computation | async-start | bytes 196608 | tf_op jit(solution)/shard_map/all_to_all | solution.py:366
  18.7 0.0 copy-done.4
  18.7 0.6 %broadcast_in_dim.25.gain_ref = f32[1,384]{1,0:T(1,128)} reshape(f32[384]{0:T(512)S(1)} %copy-done.4) | data formatting | bytes 3072 | tf_op jit(solution)/shard_map/broadcast_in_dim | solution.py:375
  19.3 0.0 copy-done.5
  19.3 0.5 %broadcast_in_dim.26.hidden_gain_ref = f32[1,384]{1,0:T(1,128)} reshape(f32[384]{0:T(512)S(1)} %copy-done.5) | data formatting | bytes 3072 | tf_op jit(solution)/shard_map/broadcast_in_dim | solution.py:378
  19.8 0.0 copy-done.6
  19.8 0.6 %broadcast_in_dim.27.head_gain_ref = f32[1,384]{1,0:T(1,128)} reshape(f32[384]{0:T(512)S(1)} %copy-done.6) | data formatting | bytes 3072 | tf_op jit(solution)/shard_map/broadcast_in_dim | solution.py:381
  20.4 0.0 copy-start.1
  20.4 0.0 copy-start.3
  20.4 5.7 %all-to-all-done.x_ref = bf16[16,8,384]{2,1,0:T(8,128)(2,1)S(1)} async-done(((bf16[16,8,384]{2,1,0:T(8,128)(2,1)}), bf16[16,8,384]{2,1,0:T(8,128)(2,1)S(1)}, u32[]{:S(2)}, u32[]{:S(2)}) %all-to-all-start) | async-done | bytes 98336 | tf_op jit(solution)/shard_map/all_to_all | solution.py:366
  26.1 0.0 copy-start
  26.1 0.6 %copy-done = bf16[16,8,384]{2,1,0:T(8,128)(2,1)} copy-done((bf16[16,8,384]{2,1,0:T(8,128)(2,1)}, bf16[16,8,384]{2,1,0:T(8,128)(2,1)S(1)}, u32[]{:S(2)}) %copy-start) | copy-done | bytes 98328
  26.7 5.1 %temporal.1 = bf16[16,4,384]{2,1,0:T(4,128)(2,1)} custom-call(bf16[16,8,384]{2,1,0:T(8,128)(2,1)} %copy-done, f32[1,384]{1,0:T(1,128)} %broadcast_in_dim.25.gain_ref, bf16[384,1152]{1,0:T(8,128)(2,1)} %proj_ref.3, bf16[384,384]{1,0:T(8,128)(2,1)} %temporal_out_ref.1, f32[1,384]{1,0:T(1,128)} %broadcast_in_dim.26.hidden_gain_ref, ...), custom_call_target="tpu_custom_call" | custom-call | tf_op jit(solution)/shard_map/temporal/pallas_call | solution.py:367
  31.8 10.2 %all_to_all.17 = bf16[16,4,384]{2,1,0:T(4,128)(2,1)S(1)} all-to-all(bf16[16,4,384]{2,1,0:T(4,128)(2,1)} %temporal.1), channel_id=1, replica_groups=mesh['parts'=2,'seq'=16] {'seq'}, dimensions={0} | all-to-all | bytes 98304 | tf_op jit(solution)/shard_map/all_to_all | solution.py:384
  42.1 0.0 copy-done.1
  42.1 0.0 copy-done.3
  42.1 0.0 copy-start.2
  42.1 0.6 %add_convert_fusion = bf16[1,64,384]{2,1,0:T(8,128)(2,1)} fusion(bf16[1,64,384]{2,1,0:T(8,128)(2,1)S(1)} %copy-done.3, bf16[1,64,384]{2,1,0:T(8,128)(2,1)S(1)} %all_to_all.14, bf16[1,64,384]{2,1,0:T(8,128)(2,1)S(1)} %copy-done.1), kind=kLoop, calls=%fused_computation | loop fusion | flops 196608 | bytes 196608 | tf_op jit(solution)/shard_map/convert_element_type | solution.py:389
  42.7 0.0 copy-done.2
  (1 shorter events, 0.0 us)
Async XLA Ops:
  0.6 18.0 %copy-start.4 = (f32[384]{0:T(512)S(1)}, f32[384]{0:T(512)}, u32[]{:S(2)}) copy-start(f32[384]{0:T(512)} %param.34) | copy-start | bytes 4612
  0.6 18.6 %copy-start.5 = (f32[384]{0:T(512)S(1)}, f32[384]{0:T(512)}, u32[]{:S(2)}) copy-start(f32[384]{0:T(512)} %param.37) | copy-start | bytes 4612
  0.7 19.2 %copy-start.6 = (f32[384]{0:T(512)S(1)}, f32[384]{0:T(512)}, u32[]{:S(2)}) copy-start(f32[384]{0:T(512)} %param.40) | copy-start | bytes 4612
  11.3 14.8 %all-to-all-start = ((bf16[16,8,384]{2,1,0:T(8,128)(2,1)}), bf16[16,8,384]{2,1,0:T(8,128)(2,1)S(1)}, u32[]{:S(2)}, u32[]{:S(2)}) async-start(bf16[16,8,384]{2,1,0:T(8,128)(2,1)} %spatial.1), calls=%async_computation | async-start | bytes 196608 | tf_op jit(solution)/shard_map/all_to_all | solution.py:366
  20.4 21.7 %copy-start.1 = (bf16[1,64,384]{2,1,0:T(8,128)(2,1)S(1)}, bf16[1,64,384]{2,1,0:T(8,128)(2,1)}, u32[]{:S(2)}) copy-start(bf16[1,64,384]{2,1,0:T(8,128)(2,1)} %x_ref.1) | copy-start | bytes 147460
  20.4 21.7 %copy-start.3 = (bf16[1,64,384]{2,1,0:T(8,128)(2,1)S(1)}, bf16[1,64,384]{2,1,0:T(8,128)(2,1)}, u32[]{:S(2)}) copy-start(bf16[1,64,384]{2,1,0:T(8,128)(2,1)} %param.22) | copy-start | bytes 147460
  26.1 0.6 %copy-start = (bf16[16,8,384]{2,1,0:T(8,128)(2,1)}, bf16[16,8,384]{2,1,0:T(8,128)(2,1)S(1)}, u32[]{:S(2)}) copy-start(bf16[16,8,384]{2,1,0:T(8,128)(2,1)S(1)} %all-to-all-done.x_ref) | copy-start | bytes 294916
  42.1 0.7 %copy-start.2 = (bf16[1,64,384]{2,1,0:T(8,128)(2,1)}, bf16[1,64,384]{2,1,0:T(8,128)(2,1)S(1)}, u32[]{:S(2)}) copy-start(bf16[1,64,384]{2,1,0:T(8,128)(2,1)S(1)} %all_to_all.14) | copy-start | bytes 147460

commit v2 on v1

--- a/solution.py
+++ b/solution.py
@@ -33,6 +33,10 @@
     centered = values - average
     spread = jnp.mean(centered * centered, axis=-1, keepdims=True)
     return centered * lax.rsqrt(spread + EPSILON) * scale_gain
+
+
+def as_row(ref):
+    return ref[...].reshape(1, ref.shape[0])
 
 
 def matmul(left, right):
@@ -63,16 +67,15 @@
     proj_ref,
     points_ref,
     spatial_out_ref,
-    out_ref,
-    columns_ref,
-    wide_ref,
-    rows_ref,
+    *refs,
 ):
+    out_refs, (columns_ref, wide_ref) = refs[:groups], refs[groups:]
     frames, residues, width = x_ref.shape
+    me = lax.axis_index("seq")
     heads = gamma_ref.shape[0]
     head_dim = width // heads
     block_heads = LANES // head_dim
-    all_points = points_ref.shape[1]
+    all_points = points_ref.shape[0]
     half = all_points // 2
     per_head = half // heads
     points_wide = wide_ref.shape[1]
@@ -84,7 +87,7 @@
     kinds = table_ref.shape[0]
     onehot = (iota((kinds, residues), 0) == types_ref[...]).astype(F32).T.astype(BF16)
     conditional = matmul(onehot, table_ref[...])
-    empty = null_ref[...].astype(F32)
+    empty = as_row(null_ref).astype(F32)
 
     lane = iota((1, points_wide), 1)
     component = lane % 3
@@ -126,6 +129,7 @@
         iota((LANES, block_heads * residues), 1) // residues
     )
 
+    sent = [[] for _ in range(groups)]
     for frame in range(frames):
         columns_ref[...] = jnp.zeros_like(columns_ref)
         columns_ref[0:9, :] = rotation_ref[:, frame, :]
@@ -146,10 +150,12 @@
 
         state = x_ref[frame].astype(F32)
         initial = jnp.concatenate([state + conditional, state + empty], axis=0)
-        normed = layer_norm(initial, gain_ref[...]).astype(BF16)
+        normed = layer_norm(initial, as_row(gain_ref)).astype(BF16)
         projected = matmul(normed, proj_ref[...])
         wide_ref[:, points_wide - LANES :] = jnp.zeros((BRANCHES * residues, LANES), F32)
-        wide_ref[:, :all_points] = matmul(normed, points_ref[...])
+        wide_ref[:, :all_points] = lax.dot_general(
+            normed, points_ref[...], NT, preferred_element_type=F32
+        )
         points = wide_ref[...]
 
         placed = None
@@ -244,33 +250,34 @@
             for start in range(0, fold, residues):
                 first = branch * fold + start
                 total = total + update[first : first + residues]
-            place = (frame * BRANCHES + branch) * share
-            for group in range(groups):
-                rows_ref[group, place : place + share, :] = total[group * share : (group + 1) * share]
-    out_ref[...] = rows_ref[...].astype(BF16)
-
-
-def temporal_kernel(
-    period,
-    x_ref,
-    gain_ref,
-    proj_ref,
-    temporal_out_ref,
-    hidden_gain_ref,
-    hidden_in_ref,
-    hidden_out_ref,
-    head_gain_ref,
-    head_out_ref,
-    out_ref,
-):
-    groups, depth, width = x_ref.shape
+            total = pltpu.roll(total, residues - me * share, 0)
+            for step in range(groups):
+                sent[step].append(total[step * share : (step + 1) * share])
+    for step in range(groups):
+        out_refs[step][...] = jnp.concatenate(sent[step], axis=0).astype(BF16)
+
+
+def temporal_kernel(groups, period, *refs):
+    x_refs, refs = refs[:groups], refs[groups:]
+    (
+        gain_ref,
+        proj_ref,
+        temporal_out_ref,
+        hidden_gain_ref,
+        hidden_in_ref,
+        hidden_out_ref,
+        head_gain_ref,
+        head_out_ref,
+    ) = refs[:8]
+    out_refs = refs[8:]
+    depth, width = x_refs[0].shape
     rows = groups * depth
     head_dim = width // THEADS
     block_heads = LANES // head_dim
     share = period // BRANCHES
 
-    initial = x_ref[...].astype(F32).reshape(rows, width)
-    normed = layer_norm(initial, gain_ref[...]).astype(BF16)
+    initial = jnp.concatenate([x_ref[...].astype(F32) for x_ref in x_refs], axis=0)
+    normed = layer_norm(initial, as_row(gain_ref)).astype(BF16)
     projected = matmul(normed, proj_ref[...])
     queries = projected[:, :width].astype(BF16) * jnp.asarray(1.0 / math.sqrt(head_dim), BF16)
     keys = projected[:, width : 2 * width].astype(BF16)
@@ -297,14 +304,50 @@
             )
     context = jnp.concatenate(pieces, axis=0).T.astype(BF16)
     after_time = initial + matmul(context, temporal_out_ref[...])
-    second = layer_norm(after_time, hidden_gain_ref[...]).astype(BF16)
+    second = layer_norm(after_time, as_row(hidden_gain_ref)).astype(BF16)
     hidden = jax.nn.gelu(matmul(second, hidden_in_ref[...])).astype(BF16)
     result = (after_time + matmul(hidden, hidden_out_ref[...])).astype(BF16).astype(F32)
-    headed = layer_norm(result, head_gain_ref[...]).astype(BF16)
-    branch_velocity = matmul(headed, head_out_ref[...]).reshape(rows // period, period, width)
-    conditional = branch_velocity[:, :share]
-    empty = branch_velocity[:, share:]
-    out_ref[...] = (empty + GUIDE * (conditional - empty)).astype(BF16)
+    headed = layer_norm(result, as_row(head_gain_ref)).astype(BF16)
+    branch_velocity = matmul(headed, head_out_ref[...])
+    for step, out_ref in enumerate(out_refs):
+        for frame in range(depth // period):
+            start = step * depth + frame * period
+            conditional = branch_velocity[start : start + share]
+            empty = branch_velocity[start + share : start + period]
+            out_ref[frame * share : (frame + 1) * share, :] = (
+                empty + GUIDE * (conditional - empty)
+            ).astype(BF16)
+
+
+def update_kernel(groups, x_ref, noise_ref, *refs):
+    parts, (next_ref, velocity_ref, rows_ref) = refs[:groups], refs[groups:]
+    frames, residues, _ = x_ref.shape
+    share = residues // groups
+    me = lax.axis_index("seq")
+    for frame in range(frames):
+        for step, part in enumerate(parts):
+            rows_ref[step * share : (step + 1) * share, :] = part[
+                frame * share : (frame + 1) * share, :
+            ].astype(F32)
+        velocity = pltpu.roll(rows_ref[...], me * share, 0)
+        velocity_ref[frame] = velocity.astype(BF16)
+        next_ref[frame] = (
+            x_ref[frame].astype(F32)
+            + STEP_SIZE * velocity
+            + NOISE_SCALE * noise_ref[frame].astype(F32)
+        ).astype(BF16)
+
+
+def exchange(pieces, direction):
+    count = len(pieces)
+    return [
+        piece
+        if step == 0
+        else lax.ppermute(
+            piece, "seq", [(source, (source + direction * step) % count) for source in range(count)]
+        )
+        for step, piece in enumerate(pieces)
+    ]
 
 
 def whole(memory_space=pltpu.VMEM):
@@ -340,13 +383,12 @@
     period = BRANCHES * share
     spatial = pl.pallas_call(
         functools.partial(spatial_kernel, groups),
-        out_shape=jax.ShapeDtypeStruct((groups, frames * period, width), BF16),
+        out_shape=[jax.ShapeDtypeStruct((frames * period, width), BF16)] * groups,
         in_specs=[whole(pltpu.SMEM)] + [whole()] * 11,
-        out_specs=whole(),
+        out_specs=[whole()] * groups,
         scratch_shapes=[
             pltpu.VMEM((16, residues), F32),
             pltpu.VMEM((BRANCHES * residues, round_up(spatial_points.shape[1], LANES)), F32),
-            pltpu.VMEM((groups, frames * period, width), F32),
         ],
         name="spatial",
     )(
@@ -357,37 +399,39 @@
         residue_types[None],
         pocket_mask[None],
         type_table,
-        null_embed[None],
-        spatial_gain[None],
+        null_embed,
+        spatial_gain,
         spatial_proj,
-        spatial_points,
+        spatial_points.T,
         spatial_out,
     )
-    arrived = lax.all_to_all(spatial, "seq", split_axis=0, concat_axis=0, tiled=True)
     guided = pl.pallas_call(
-        functools.partial(temporal_kernel, period),
-        out_shape=jax.ShapeDtypeStruct((groups * frames, share, width), BF16),
-        in_specs=[whole()] * 9,
-        out_specs=whole(),
+        functools.partial(temporal_kernel, groups, period),
+        out_shape=[jax.ShapeDtypeStruct((frames * share, width), BF16)] * groups,
+        in_specs=[whole()] * (groups + 8),
+        out_specs=[whole()] * groups,
         name="temporal",
     )(
-        arrived,
-        temporal_gain[None],
+        *exchange(spatial, 1),
+        temporal_gain,
         temporal_proj,
         temporal_out,
-        hidden_gain[None],
+        hidden_gain,
         hidden_in,
         hidden_out,
-        head_gain[None],
+        head_gain,
         head_out,
     )
-    velocity = lax.all_to_all(guided, "seq", split_axis=0, concat_axis=1, tiled=True)
-    x_next = (
-        x_state.astype(F32)
-        + STEP_SIZE * velocity.astype(F32)
-        + NOISE_SCALE * noise_field.astype(F32)
-    ).astype(BF16)
-    return (x_next, velocity)
+    return tuple(
+        pl.pallas_call(
+            functools.partial(update_kernel, groups),
+            out_shape=[jax.ShapeDtypeStruct(x_state.shape, BF16)] * 2,
+            in_specs=[whole()] * (groups + 2),
+            out_specs=[whole()] * 2,
+            scratch_shapes=[pltpu.VMEM((residues, width), F32)],
+            name="update",
+        )(x_state, noise_field, *exchange(guided, -1))
+    )
 
 
 def solution(mesh):

time: 43.1 us -> 67.3 us (1.56)
  starting transfers between devices: 7.39 us -> 44.5 us
  blocking collectives: 10.2 us -> 0 us
  local copies, waits for them, and re-layouts: 6.69 us -> 1.05 us
  waiting for transfers between devices: 5.7 us -> 7.47 us
  Pallas kernels: 11.4 us -> 13.1 us
    ppermute x0 -> x30, starting transfers between devices: none -> 44.5 us  [exchange(): lax.ppermute(piece, 'seq', [(source, (source + direction * step) % count)...]
    all_to_all x1 -> x0, blocking collectives: 10.2 us -> none  [body(): lax.all_to_all(guided, 'seq', split_axis=0, concat_axis=1, tiled=True)]
    ppermute x0 -> x30, waiting for transfers between devices: none -> 7.47 us  [exchange(): lax.ppermute(piece, 'seq', [(source, (source + direction * step) % count)...]
    all_to_all x1 -> x0, starting transfers between devices: 7.39 us -> none  [body(): lax.all_to_all(spatial, 'seq', split_axis=0, concat_axis=0, tiled=True)]
    all_to_all x1 -> x0, waiting for transfers between devices: 5.7 us -> none  [body(): lax.all_to_all(spatial, 'seq', split_axis=0, concat_axis=0, tiled=True)]
    broadcast_in_dim x5 -> x0, local copies, waits for them, and re-layouts: 4.17 us -> none  [the longest x1 1.24 us: body(): spatial_gain[None]]
    pallas_call x2 -> x3, Pallas kernels: 11.4 us -> 13.1 us  [the longest x1 6.33 us: body(): pl.pallas_call(functools.partial(spatial_kernel, groups), out_shape=[jax....]
    unnamed x15 -> x60, local copies, waits for them, and re-layouts: 2.5 us -> 1.05 us
  transfers between devices with their start and end apart: 1 -> 30, of which waited for: 1 -> 6; matrix products, arithmetic and copies ran while one was open for 4% -> 0% of each run, Pallas kernels for 0% -> 0%
where the time goes in v2:
time: 67.3 us; the launch traced here: 67.1 us
  starting transfers between devices  44.5 us (66%)
  Pallas kernels  13.1 us (19%)
  waiting for transfers between devices  7.47 us (11%)
  local copies, waits for them, and re-layouts  1.05 us (2%)
  between operations  0.94 us (1%)
    ppermute x30, starting transfers between devices, exchange(): lax.ppermute(piece, 'seq', [(source, (source + direction * step) % count)...  44.5 us
    ppermute x30, waiting for transfers between devices, exchange(): lax.ppermute(piece, 'seq', [(source, (source + direction * step) % count)...  7.47 us
    pallas_call x1, Pallas kernels, body(): pl.pallas_call(functools.partial(spatial_kernel, groups), out_shape=[jax....  6.33 us
    pallas_call x1, Pallas kernels, body(): pl.pallas_call(functools.partial(temporal_kernel, groups, period), out_sh...  5.25 us
    pallas_call x1, Pallas kernels, body(): pl.pallas_call(functools.partial(update_kernel, groups), out_shape=[jax.S...  1.56 us
  transfers between devices with their start and end apart: 30, of which 6 were waited for; matrix products, arithmetic and copies ran while one was open for 0% of the time, Pallas kernels for 0%

profile of v2, /device:TPU:0, one launch (start us, length us, event | category | flops | bytes accessed | tf_op | source)
XLA Modules:
  0.0 67.1 jit_solution(12349102820750655266)
XLA Ops:
  0.6 6.3 %spatial.1 = (bf16[8,384]{1,0:T(8,128)(2,1)}, bf16[8,384]{1,0:T(8,128)(2,1)}, bf16[8,384]{1,0:T(8,128)(2,1)}, bf16[8,384]{1,0:T(8,128)(2,1)}, bf16[8,384]{1,0:T(...) custom-call(f32[12]{0:T(128)} %gamma_ref.1, ...), custom_call_target="tpu_custom_call" | custom-call | tf_op jit(solution)/shard_map/spatial/pallas_call | solution.py:384
  7.0 0.5 collective-permute-start
  7.5 2.6 %collective-permute-start.1 = (bf16[8,384]{1,0:T(8,128)(2,1)}, bf16[8,384]{1,0:T(8,128)(2,1)S(1)}, u32[]{:S(2)}, u32[]{:S(2)}) collective-permute-start(bf16[8,384]{1,0:T(8,128)(2,1)} %get-tuple-element.36), channel_id=1, source_target_pairs={{0,2},{1,3},{2,4},{3,5},{4,6},{5,7},{6,8},{7,9},{8,10},{9,11},{10,... | collective-permute-start | bytes 18440 | tf_op jit(solution)/shard_map/ppermute | solution.py:346
  10.1 2.4 %collective-permute-start.2 = (bf16[8,384]{1,0:T(8,128)(2,1)}, bf16[8,384]{1,0:T(8,128)(2,1)S(1)}, u32[]{:S(2)}, u32[]{:S(2)}) collective-permute-start(bf16[8,384]{1,0:T(8,128)(2,1)} %get-tuple-element.37), channel_id=1, source_target_pairs={{0,3},{1,4},{2,5},{3,6},{4,7},{5,8},{6,9},{7,10},{8,11},{9,12},{10... | collective-permute-start | bytes 18440 | tf_op jit(solution)/shard_map/ppermute | solution.py:346
  12.5 1.6 %collective-permute-start.3 = (bf16[8,384]{1,0:T(8,128)(2,1)}, bf16[8,384]{1,0:T(8,128)(2,1)S(1)}, u32[]{:S(2)}, u32[]{:S(2)}) collective-permute-start(bf16[8,384]{1,0:T(8,128)(2,1)} %get-tuple-element.38), channel_id=1, source_target_pairs={{0,4},{1,5},{2,6},{3,7},{4,8},{5,9},{6,10},{7,11},{8,12},{9,13},{1... | collective-permute-start | bytes 18440 | tf_op jit(solution)/shard_map/ppermute | solution.py:346
  14.0 0.2 collective-permute-start.4
  14.2 0.0 collective-permute-done.refs_1_
  14.2 1.2 %collective-permute-start.5 = (bf16[8,384]{1,0:T(8,128)(2,1)}, bf16[8,384]{1,0:T(8,128)(2,1)S(1)}, u32[]{:S(2)}, u32[]{:S(2)}) collective-permute-start(bf16[8,384]{1,0:T(8,128)(2,1)} %get-tuple-element.40), channel_id=1, source_target_pairs={{0,6},{1,7},{2,8},{3,9},{4,10},{5,11},{6,12},{7,13},{8,14},{9,15},... | collective-permute-start | bytes 18440 | tf_op jit(solution)/shard_map/ppermute | solution.py:346
  15.4 0.0 collective-permute-done.1.refs_2_
  15.4 4.3 %collective-permute-start.6 = (bf16[8,384]{1,0:T(8,128)(2,1)}, bf16[8,384]{1,0:T(8,128)(2,1)S(1)}, u32[]{:S(2)}, u32[]{:S(2)}) collective-permute-start(bf16[8,384]{1,0:T(8,128)(2,1)} %get-tuple-element.41), channel_id=1, source_target_pairs={{0,7},{1,8},{2,9},{3,10},{4,11},{5,12},{6,13},{7,14},{8,15},{9,0},... | collective-permute-start | bytes 18440 | tf_op jit(solution)/shard_map/ppermute | solution.py:346
  19.7 0.0 collective-permute-done.2.refs_3_
  19.7 0.3 collective-permute-start.7
  20.1 0.0 collective-permute-done.3.refs_4_
  20.1 0.3 collective-permute-start.8
  20.4 0.0 collective-permute-done.4.refs_5_
  20.4 2.4 %collective-permute-start.9 = (bf16[8,384]{1,0:T(8,128)(2,1)}, bf16[8,384]{1,0:T(8,128)(2,1)S(1)}, u32[]{:S(2)}, u32[]{:S(2)}) collective-permute-start(bf16[8,384]{1,0:T(8,128)(2,1)} %get-tuple-element.44), channel_id=1, source_target_pairs={{0,10},{1,11},{2,12},{3,13},{4,14},{5,15},{6,0},{7,1},{8,2},{9,3},... | collective-permute-start | bytes 18440 | tf_op jit(solution)/shard_map/ppermute | solution.py:346
  22.8 0.0 collective-permute-done.5.refs_6_
  22.8 2.8 %collective-permute-start.10 = (bf16[8,384]{1,0:T(8,128)(2,1)}, bf16[8,384]{1,0:T(8,128)(2,1)S(1)}, u32[]{:S(2)}, u32[]{:S(2)}) collective-permute-start(bf16[8,384]{1,0:T(8,128)(2,1)} %get-tuple-element.45), channel_id=1, source_target_pairs={{0,11},{1,12},{2,13},{3,14},{4,15},{5,0},{6,1},{7,2},{8,3},{9,4},{... | collective-permute-start | bytes 18440 | tf_op jit(solution)/shard_map/ppermute | solution.py:346
  25.7 0.0 collective-permute-done.6.refs_7_
  25.7 1.8 %collective-permute-start.11 = (bf16[8,384]{1,0:T(8,128)(2,1)}, bf16[8,384]{1,0:T(8,128)(2,1)S(1)}, u32[]{:S(2)}, u32[]{:S(2)}) collective-permute-start(bf16[8,384]{1,0:T(8,128)(2,1)} %get-tuple-element.46), channel_id=1, source_target_pairs={{0,12},{1,13},{2,14},{3,15},{4,0},{5,1},{6,2},{7,3},{8,4},{9,5},{1... | collective-permute-start | bytes 18440 | tf_op jit(solution)/shard_map/ppermute | solution.py:346
  27.5 0.0 collective-permute-done.7.refs_8_
  27.5 0.0 collective-permute-start.12
  27.5 0.0 collective-permute-done.8.refs_9_
  27.5 1.5 %collective-permute-start.13 = (bf16[8,384]{1,0:T(8,128)(2,1)}, bf16[8,384]{1,0:T(8,128)(2,1)S(1)}, u32[]{:S(2)}, u32[]{:S(2)}) collective-permute-start(bf16[8,384]{1,0:T(8,128)(2,1)} %get-tuple-element.48), channel_id=1, source_target_pairs={{0,14},{1,15},{2,0},{3,1},{4,2},{5,3},{6,4},{7,5},{8,6},{9,7},{10,... | collective-permute-start | bytes 18440 | tf_op jit(solution)/shard_map/ppermute | solution.py:346
  29.0 0.0 collective-permute-done.9.refs_10_
  29.0 2.2 %collective-permute-start.14 = (bf16[8,384]{1,0:T(8,128)(2,1)}, bf16[8,384]{1,0:T(8,128)(2,1)S(1)}, u32[]{:S(2)}, u32[]{:S(2)}) collective-permute-start(bf16[8,384]{1,0:T(8,128)(2,1)} %get-tuple-element.49), channel_id=1, source_target_pairs={{0,15},{1,0},{2,1},{3,2},{4,3},{5,4},{6,5},{7,6},{8,7},{9,8},{10,9... | collective-permute-start | bytes 18440 | tf_op jit(solution)/shard_map/ppermute | solution.py:346
  31.2 0.0 collective-permute-done.10.refs_11_
  31.2 0.0 collective-permute-done.11.refs_12_
  31.2 0.0 collective-permute-done.12.refs_13_
  31.2 0.2 collective-permute-done.13.refs_14_
  31.4 1.3 %collective-permute-done.14.refs_15_ = bf16[8,384]{1,0:T(8,128)(2,1)S(1)} collective-permute-done((bf16[8,384]{1,0:T(8,128)(2,1)}, bf16[8,384]{1,0:T(8,128)(2,1)S(1)}, u32[]{:S(2)}, u32[]{:S(2)}) %collective-permute-start.14) | collective-permute-done | bytes 6176 | tf_op jit(solution)/shard_map/ppermute | solution.py:346
  32.8 0.5 copy-done.14
  33.3 5.2 %temporal.1 = (bf16[4,384]{1,0:T(4,128)(2,1)}, bf16[4,384]{1,0:T(4,128)(2,1)}, bf16[4,384]{1,0:T(4,128)(2,1)}, bf16[4,384]{1,0:T(4,128)(2,1)}, bf16[4,384]{1,0:T...) custom-call(bf16[8,384]{1,0:T(8,128)(2,1)} %get-tuple-element.34.ref, ...), custom_call_target="tpu_custom_call" | custom-call | tf_op jit(solution)/shard_map/temporal/pallas_call | solution.py:408
  38.6 4.5 %collective-permute-start.15 = (bf16[4,384]{1,0:T(4,128)(2,1)}, bf16[4,384]{1,0:T(4,128)(2,1)S(1)}, u32[]{:S(2)}, u32[]{:S(2)}) collective-permute-start(bf16[4,384]{1,0:T(4,128)(2,1)} %get-tuple-element.51), channel_id=1, source_target_pairs={{0,15},{1,0},{2,1},{3,2},{4,3},{5,4},{6,5},{7,6},{8,7},{9,8},{10,9... | collective-permute-start | bytes 9224 | tf_op jit(solution)/shard_map/ppermute | solution.py:346
  43.0 0.0 collective-permute-start.16
  43.0 0.0 collective-permute-start.17
  43.0 0.4 collective-permute-start.18
  43.4 1.3 %collective-permute-start.19 = (bf16[4,384]{1,0:T(4,128)(2,1)}, bf16[4,384]{1,0:T(4,128)(2,1)S(1)}, u32[]{:S(2)}, u32[]{:S(2)}) collective-permute-start(bf16[4,384]{1,0:T(4,128)(2,1)} %get-tuple-element.55), channel_id=1, source_target_pairs={{0,11},{1,12},{2,13},{3,14},{4,15},{5,0},{6,1},{7,2},{8,3},{9,4},{... | collective-permute-start | bytes 9224 | tf_op jit(solution)/shard_map/ppermute | solution.py:346
  44.8 0.0 collective-permute-done.15.refs_1_
  44.8 3.8 %collective-permute-start.20 = (bf16[4,384]{1,0:T(4,128)(2,1)}, bf16[4,384]{1,0:T(4,128)(2,1)S(1)}, u32[]{:S(2)}, u32[]{:S(2)}) collective-permute-start(bf16[4,384]{1,0:T(4,128)(2,1)} %get-tuple-element.56), channel_id=1, source_target_pairs={{0,10},{1,11},{2,12},{3,13},{4,14},{5,15},{6,0},{7,1},{8,2},{9,3},... | collective-permute-start | bytes 9224 | tf_op jit(solution)/shard_map/ppermute | solution.py:346
  48.6 0.0 collective-permute-done.16.refs_2_
  48.6 0.0 collective-permute-start.21
  48.6 0.0 collective-permute-done.17.refs_3_
  48.6 1.7 %collective-permute-start.22 = (bf16[4,384]{1,0:T(4,128)(2,1)}, bf16[4,384]{1,0:T(4,128)(2,1)S(1)}, u32[]{:S(2)}, u32[]{:S(2)}) collective-permute-start(bf16[4,384]{1,0:T(4,128)(2,1)} %get-tuple-element.58), channel_id=1, source_target_pairs={{0,8},{1,9},{2,10},{3,11},{4,12},{5,13},{6,14},{7,15},{8,0},{9,1},... | collective-permute-start | bytes 9224 | tf_op jit(solution)/shard_map/ppermute | solution.py:346
  50.4 0.0 collective-permute-done.18.refs_4_
  50.4 1.6 %collective-permute-start.23 = (bf16[4,384]{1,0:T(4,128)(2,1)}, bf16[4,384]{1,0:T(4,128)(2,1)S(1)}, u32[]{:S(2)}, u32[]{:S(2)}) collective-permute-start(bf16[4,384]{1,0:T(4,128)(2,1)} %get-tuple-element.59), channel_id=1, source_target_pairs={{0,7},{1,8},{2,9},{3,10},{4,11},{5,12},{6,13},{7,14},{8,15},{9,0},... | collective-permute-start | bytes 9224 | tf_op jit(solution)/shard_map/ppermute | solution.py:346
  52.0 0.0 collective-permute-done.19.refs_5_
  52.0 1.7 %collective-permute-start.24 = (bf16[4,384]{1,0:T(4,128)(2,1)}, bf16[4,384]{1,0:T(4,128)(2,1)S(1)}, u32[]{:S(2)}, u32[]{:S(2)}) collective-permute-start(bf16[4,384]{1,0:T(4,128)(2,1)} %get-tuple-element.60), channel_id=1, source_target_pairs={{0,6},{1,7},{2,8},{3,9},{4,10},{5,11},{6,12},{7,13},{8,14},{9,15},... | collective-permute-start | bytes 9224 | tf_op jit(solution)/shard_map/ppermute | solution.py:346
  53.7 0.0 collective-permute-done.20.refs_6_
  53.7 0.3 collective-permute-start.25
  54.0 0.0 collective-permute-done.21.refs_7_
  54.0 2.1 %collective-permute-start.26 = (bf16[4,384]{1,0:T(4,128)(2,1)}, bf16[4,384]{1,0:T(4,128)(2,1)S(1)}, u32[]{:S(2)}, u32[]{:S(2)}) collective-permute-start(bf16[4,384]{1,0:T(4,128)(2,1)} %get-tuple-element.62), channel_id=1, source_target_pairs={{0,4},{1,5},{2,6},{3,7},{4,8},{5,9},{6,10},{7,11},{8,12},{9,13},{1... | collective-permute-start | bytes 9224 | tf_op jit(solution)/shard_map/ppermute | solution.py:346
  56.1 0.0 collective-permute-done.22.refs_8_
  56.1 2.1 %collective-permute-start.27 = (bf16[4,384]{1,0:T(4,128)(2,1)}, bf16[4,384]{1,0:T(4,128)(2,1)S(1)}, u32[]{:S(2)}, u32[]{:S(2)}) collective-permute-start(bf16[4,384]{1,0:T(4,128)(2,1)} %get-tuple-element.63), channel_id=1, source_target_pairs={{0,3},{1,4},{2,5},{3,6},{4,7},{5,8},{6,9},{7,10},{8,11},{9,12},{10... | collective-permute-start | bytes 9224 | tf_op jit(solution)/shard_map/ppermute | solution.py:346
  58.2 0.8 %collective-permute-start.28 = (bf16[4,384]{1,0:T(4,128)(2,1)}, bf16[4,384]{1,0:T(4,128)(2,1)S(1)}, u32[]{:S(2)}, u32[]{:S(2)}) collective-permute-start(bf16[4,384]{1,0:T(4,128)(2,1)} %get-tuple-element.64), channel_id=1, source_target_pairs={{0,2},{1,3},{2,4},{3,5},{4,6},{5,7},{6,8},{7,9},{8,10},{9,11},{10,... | collective-permute-start | bytes 9224 | tf_op jit(solution)/shard_map/ppermute | solution.py:346
  59.0 0.0 collective-permute-done.24.refs_10_
  59.0 0.0 collective-permute-start.29
  59.0 0.6 collective-permute-done.26.refs_12_
  59.6 2.7 %collective-permute-done.27.refs_13_ = bf16[4,384]{1,0:T(4,128)(2,1)S(1)} collective-permute-done((bf16[4,384]{1,0:T(4,128)(2,1)}, bf16[4,384]{1,0:T(4,128)(2,1)S(1)}, u32[]{:S(2)}, u32[]{:S(2)}) %collective-permute-start.27) | collective-permute-done | bytes 3104 | tf_op jit(solution)/shard_map/ppermute | solution.py:346
  62.3 2.5 %collective-permute-done.28.refs_14_ = bf16[4,384]{1,0:T(4,128)(2,1)S(1)} collective-permute-done((bf16[4,384]{1,0:T(4,128)(2,1)}, bf16[4,384]{1,0:T(4,128)(2,1)S(1)}, u32[]{:S(2)}, u32[]{:S(2)}) %collective-permute-start.28) | collective-permute-done | bytes 3104 | tf_op jit(solution)/shard_map/ppermute | solution.py:346
  64.7 0.2 collective-permute-done.29.refs_15_
  65.1 0.2 copy-done.28
  65.3 0.2 copy-done.29
  65.5 1.6 %update.1 = (bf16[1,64,384]{2,1,0:T(8,128)(2,1)}, bf16[1,64,384]{2,1,0:T(8,128)(2,1)}) custom-call(bf16[1,64,384]{2,1,0:T(8,128)(2,1)} %x_ref.3, bf16[1,64,384]{2,1,0:T(8,128)(2,1)} %noise_ref.1, bf16[4,384]{1,0:T(4,128)(2,1)} %get-tuple-element.50.refs_0_, bf16[4,384]{1,0:T(4,128)(2,1)} %copy-done.15, bf16[4,384]{1,0:T(4,128)(2,1)} %copy-done.16, ...), custom_call_target="tpu_custom_call" | custom-call | tf_op jit(solution)/shard_map/update/pallas_call | solution.py:426
  (59 shorter events, 0.1 us)
Async XLA Ops:
  7.0 7.3 %collective-permute-start = (bf16[8,384]{1,0:T(8,128)(2,1)}, bf16[8,384]{1,0:T(8,128)(2,1)S(1)}, u32[]{:S(2)}, u32[]{:S(2)}) collective-permute-start(bf16[8,384]{1,0:T(8,128)(2,1)} %get-tuple-element.35), channel_id=1, source_target_pairs={{0,1},{1,2},{2,3},{3,4},{4,5},{5,6},{6,7},{7,8},{8,9},{9,10},{10,1... | collective-permute-start | bytes 18440 | tf_op jit(solution)/shard_map/ppermute | solution.py:346
  7.5 8.0 %collective-permute-start.1 = (bf16[8,384]{1,0:T(8,128)(2,1)}, bf16[8,384]{1,0:T(8,128)(2,1)S(1)}, u32[]{:S(2)}, u32[]{:S(2)}) collective-permute-start(bf16[8,384]{1,0:T(8,128)(2,1)} %get-tuple-element.36), channel_id=1, source_target_pairs={{0,2},{1,3},{2,4},{3,5},{4,6},{5,7},{6,8},{7,9},{8,10},{9,11},{10,... | collective-permute-start | bytes 18440 | tf_op jit(solution)/shard_map/ppermute | solution.py:346
  10.1 9.7 %collective-permute-start.2 = (bf16[8,384]{1,0:T(8,128)(2,1)}, bf16[8,384]{1,0:T(8,128)(2,1)S(1)}, u32[]{:S(2)}, u32[]{:S(2)}) collective-permute-start(bf16[8,384]{1,0:T(8,128)(2,1)} %get-tuple-element.37), channel_id=1, source_target_pairs={{0,3},{1,4},{2,5},{3,6},{4,7},{5,8},{6,9},{7,10},{8,11},{9,12},{10... | collective-permute-start | bytes 18440 | tf_op jit(solution)/shard_map/ppermute | solution.py:346
  12.5 7.6 %collective-permute-start.3 = (bf16[8,384]{1,0:T(8,128)(2,1)}, bf16[8,384]{1,0:T(8,128)(2,1)S(1)}, u32[]{:S(2)}, u32[]{:S(2)}) collective-permute-start(bf16[8,384]{1,0:T(8,128)(2,1)} %get-tuple-element.38), channel_id=1, source_target_pairs={{0,4},{1,5},{2,6},{3,7},{4,8},{5,9},{6,10},{7,11},{8,12},{9,13},{1... | collective-permute-start | bytes 18440 | tf_op jit(solution)/shard_map/ppermute | solution.py:346
  14.0 6.3 %collective-permute-start.4 = (bf16[8,384]{1,0:T(8,128)(2,1)}, bf16[8,384]{1,0:T(8,128)(2,1)S(1)}, u32[]{:S(2)}, u32[]{:S(2)}) collective-permute-start(bf16[8,384]{1,0:T(8,128)(2,1)} %get-tuple-element.39), channel_id=1, source_target_pairs={{0,5},{1,6},{2,7},{3,8},{4,9},{5,10},{6,11},{7,12},{8,13},{9,14},{... | collective-permute-start | bytes 18440 | tf_op jit(solution)/shard_map/ppermute | solution.py:346
  14.2 18.5 %copy-start = (bf16[8,384]{1,0:T(8,128)(2,1)}, bf16[8,384]{1,0:T(8,128)(2,1)S(1)}, u32[]{:S(2)}) copy-start(bf16[8,384]{1,0:T(8,128)(2,1)S(1)} %collective-permute-done.refs_1_) | copy-start | bytes 18436
  14.2 8.6 %collective-permute-start.5 = (bf16[8,384]{1,0:T(8,128)(2,1)}, bf16[8,384]{1,0:T(8,128)(2,1)S(1)}, u32[]{:S(2)}, u32[]{:S(2)}) collective-permute-start(bf16[8,384]{1,0:T(8,128)(2,1)} %get-tuple-element.40), channel_id=1, source_target_pairs={{0,6},{1,7},{2,8},{3,9},{4,10},{5,11},{6,12},{7,13},{8,14},{9,15},... | collective-permute-start | bytes 18440 | tf_op jit(solution)/shard_map/ppermute | solution.py:346
  15.4 17.3 %copy-start.1 = (bf16[8,384]{1,0:T(8,128)(2,1)}, bf16[8,384]{1,0:T(8,128)(2,1)S(1)}, u32[]{:S(2)}) copy-start(bf16[8,384]{1,0:T(8,128)(2,1)S(1)} %collective-permute-done.1.refs_2_) | copy-start | bytes 18436
  15.4 10.2 %collective-permute-start.6 = (bf16[8,384]{1,0:T(8,128)(2,1)}, bf16[8,384]{1,0:T(8,128)(2,1)S(1)}, u32[]{:S(2)}, u32[]{:S(2)}) collective-permute-start(bf16[8,384]{1,0:T(8,128)(2,1)} %get-tuple-element.41), channel_id=1, source_target_pairs={{0,7},{1,8},{2,9},{3,10},{4,11},{5,12},{6,13},{7,14},{8,15},{9,0},... | collective-permute-start | bytes 18440 | tf_op jit(solution)/shard_map/ppermute | solution.py:346
  19.7 13.0 %copy-start.2 = (bf16[8,384]{1,0:T(8,128)(2,1)}, bf16[8,384]{1,0:T(8,128)(2,1)S(1)}, u32[]{:S(2)}) copy-start(bf16[8,384]{1,0:T(8,128)(2,1)S(1)} %collective-permute-done.2.refs_3_) | copy-start | bytes 18436
  19.7 7.7 %collective-permute-start.7 = (bf16[8,384]{1,0:T(8,128)(2,1)}, bf16[8,384]{1,0:T(8,128)(2,1)S(1)}, u32[]{:S(2)}, u32[]{:S(2)}) collective-permute-start(bf16[8,384]{1,0:T(8,128)(2,1)} %get-tuple-element.42), channel_id=1, source_target_pairs={{0,8},{1,9},{2,10},{3,11},{4,12},{5,13},{6,14},{7,15},{8,0},{9,1},... | collective-permute-start | bytes 18440 | tf_op jit(solution)/shard_map/ppermute | solution.py:346
  20.1 12.6 %copy-start.3 = (bf16[8,384]{1,0:T(8,128)(2,1)}, bf16[8,384]{1,0:T(8,128)(2,1)S(1)}, u32[]{:S(2)}) copy-start(bf16[8,384]{1,0:T(8,128)(2,1)S(1)} %collective-permute-done.3.refs_4_) | copy-start | bytes 18436
  20.1 7.4 %collective-permute-start.8 = (bf16[8,384]{1,0:T(8,128)(2,1)}, bf16[8,384]{1,0:T(8,128)(2,1)S(1)}, u32[]{:S(2)}, u32[]{:S(2)}) collective-permute-start(bf16[8,384]{1,0:T(8,128)(2,1)} %get-tuple-element.43), channel_id=1, source_target_pairs={{0,9},{1,10},{2,11},{3,12},{4,13},{5,14},{6,15},{7,0},{8,1},{9,2},... | collective-permute-start | bytes 18440 | tf_op jit(solution)/shard_map/ppermute | solution.py:346
  20.4 12.4 %copy-start.4 = (bf16[8,384]{1,0:T(8,128)(2,1)}, bf16[8,384]{1,0:T(8,128)(2,1)S(1)}, u32[]{:S(2)}) copy-start(bf16[8,384]{1,0:T(8,128)(2,1)S(1)} %collective-permute-done.4.refs_5_) | copy-start | bytes 18436
  20.4 8.6 %collective-permute-start.9 = (bf16[8,384]{1,0:T(8,128)(2,1)}, bf16[8,384]{1,0:T(8,128)(2,1)S(1)}, u32[]{:S(2)}, u32[]{:S(2)}) collective-permute-start(bf16[8,384]{1,0:T(8,128)(2,1)} %get-tuple-element.44), channel_id=1, source_target_pairs={{0,10},{1,11},{2,12},{3,13},{4,14},{5,15},{6,0},{7,1},{8,2},{9,3},... | collective-permute-start | bytes 18440 | tf_op jit(solution)/shard_map/ppermute | solution.py:346
  22.8 9.9 %copy-start.5 = (bf16[8,384]{1,0:T(8,128)(2,1)}, bf16[8,384]{1,0:T(8,128)(2,1)S(1)}, u32[]{:S(2)}) copy-start(bf16[8,384]{1,0:T(8,128)(2,1)S(1)} %collective-permute-done.5.refs_6_) | copy-start | bytes 18436
  22.8 8.3 %collective-permute-start.10 = (bf16[8,384]{1,0:T(8,128)(2,1)}, bf16[8,384]{1,0:T(8,128)(2,1)S(1)}, u32[]{:S(2)}, u32[]{:S(2)}) collective-permute-start(bf16[8,384]{1,0:T(8,128)(2,1)} %get-tuple-element.45), channel_id=1, source_target_pairs={{0,11},{1,12},{2,13},{3,14},{4,15},{5,0},{6,1},{7,2},{8,3},{9,4},{... | collective-permute-start | bytes 18440 | tf_op jit(solution)/shard_map/ppermute | solution.py:346
  25.7 7.1 %copy-start.6 = (bf16[8,384]{1,0:T(8,128)(2,1)}, bf16[8,384]{1,0:T(8,128)(2,1)S(1)}, u32[]{:S(2)}) copy-start(bf16[8,384]{1,0:T(8,128)(2,1)S(1)} %collective-permute-done.6.refs_7_) | copy-start | bytes 18436
  25.7 5.5 %collective-permute-start.11 = (bf16[8,384]{1,0:T(8,128)(2,1)}, bf16[8,384]{1,0:T(8,128)(2,1)S(1)}, u32[]{:S(2)}, u32[]{:S(2)}) collective-permute-start(bf16[8,384]{1,0:T(8,128)(2,1)} %get-tuple-element.46), channel_id=1, source_target_pairs={{0,12},{1,13},{2,14},{3,15},{4,0},{5,1},{6,2},{7,3},{8,4},{9,5},{1... | collective-permute-start | bytes 18440 | tf_op jit(solution)/shard_map/ppermute | solution.py:346
  27.5 5.3 %copy-start.7 = (bf16[8,384]{1,0:T(8,128)(2,1)}, bf16[8,384]{1,0:T(8,128)(2,1)S(1)}, u32[]{:S(2)}) copy-start(bf16[8,384]{1,0:T(8,128)(2,1)S(1)} %collective-permute-done.7.refs_8_) | copy-start | bytes 18436
  27.5 3.7 %collective-permute-start.12 = (bf16[8,384]{1,0:T(8,128)(2,1)}, bf16[8,384]{1,0:T(8,128)(2,1)S(1)}, u32[]{:S(2)}, u32[]{:S(2)}) collective-permute-start(bf16[8,384]{1,0:T(8,128)(2,1)} %get-tuple-element.47), channel_id=1, source_target_pairs={{0,13},{1,14},{2,15},{3,0},{4,1},{5,2},{6,3},{7,4},{8,5},{9,6},{10... | collective-permute-start | bytes 18440 | tf_op jit(solution)/shard_map/ppermute | solution.py:346
  27.5 5.3 %copy-start.8 = (bf16[8,384]{1,0:T(8,128)(2,1)}, bf16[8,384]{1,0:T(8,128)(2,1)S(1)}, u32[]{:S(2)}) copy-start(bf16[8,384]{1,0:T(8,128)(2,1)S(1)} %collective-permute-done.8.refs_9_) | copy-start | bytes 18436
  27.5 3.9 %collective-permute-start.13 = (bf16[8,384]{1,0:T(8,128)(2,1)}, bf16[8,384]{1,0:T(8,128)(2,1)S(1)}, u32[]{:S(2)}, u32[]{:S(2)}) collective-permute-start(bf16[8,384]{1,0:T(8,128)(2,1)} %get-tuple-element.48), channel_id=1, source_target_pairs={{0,14},{1,15},{2,0},{3,1},{4,2},{5,3},{6,4},{7,5},{8,6},{9,7},{10,... | collective-permute-start | bytes 18440 | tf_op jit(solution)/shard_map/ppermute | solution.py:346
  29.0 3.8 %copy-start.9 = (bf16[8,384]{1,0:T(8,128)(2,1)}, bf16[8,384]{1,0:T(8,128)(2,1)S(1)}, u32[]{:S(2)}) copy-start(bf16[8,384]{1,0:T(8,128)(2,1)S(1)} %collective-permute-done.9.refs_10_) | copy-start | bytes 18436
  29.0 3.7 %collective-permute-start.14 = (bf16[8,384]{1,0:T(8,128)(2,1)}, bf16[8,384]{1,0:T(8,128)(2,1)S(1)}, u32[]{:S(2)}, u32[]{:S(2)}) collective-permute-start(bf16[8,384]{1,0:T(8,128)(2,1)} %get-tuple-element.49), channel_id=1, source_target_pairs={{0,15},{1,0},{2,1},{3,2},{4,3},{5,4},{6,5},{7,6},{8,7},{9,8},{10,9... | collective-permute-start | bytes 18440 | tf_op jit(solution)/shard_map/ppermute | solution.py:346
  31.2 1.6 %copy-start.10 = (bf16[8,384]{1,0:T(8,128)(2,1)}, bf16[8,384]{1,0:T(8,128)(2,1)S(1)}, u32[]{:S(2)}) copy-start(bf16[8,384]{1,0:T(8,128)(2,1)S(1)} %collective-permute-done.10.refs_11_) | copy-start | bytes 18436
  31.2 1.6 %copy-start.11 = (bf16[8,384]{1,0:T(8,128)(2,1)}, bf16[8,384]{1,0:T(8,128)(2,1)S(1)}, u32[]{:S(2)}) copy-start(bf16[8,384]{1,0:T(8,128)(2,1)S(1)} %collective-permute-done.11.refs_12_) | copy-start | bytes 18436
  31.2 1.6 %copy-start.12 = (bf16[8,384]{1,0:T(8,128)(2,1)}, bf16[8,384]{1,0:T(8,128)(2,1)S(1)}, u32[]{:S(2)}) copy-start(bf16[8,384]{1,0:T(8,128)(2,1)S(1)} %collective-permute-done.12.refs_13_) | copy-start | bytes 18436
  31.4 1.4 %copy-start.13 = (bf16[8,384]{1,0:T(8,128)(2,1)}, bf16[8,384]{1,0:T(8,128)(2,1)S(1)}, u32[]{:S(2)}) copy-start(bf16[8,384]{1,0:T(8,128)(2,1)S(1)} %collective-permute-done.13.refs_14_) | copy-start | bytes 18436
  32.7 0.6 copy-start.14
  38.6 6.2 %collective-permute-start.15 = (bf16[4,384]{1,0:T(4,128)(2,1)}, bf16[4,384]{1,0:T(4,128)(2,1)S(1)}, u32[]{:S(2)}, u32[]{:S(2)}) collective-permute-start(bf16[4,384]{1,0:T(4,128)(2,1)} %get-tuple-element.51), channel_id=1, source_target_pairs={{0,15},{1,0},{2,1},{3,2},{4,3},{5,4},{6,5},{7,6},{8,7},{9,8},{10,9... | collective-permute-start | bytes 9224 | tf_op jit(solution)/shard_map/ppermute | solution.py:346
  43.0 5.6 %collective-permute-start.16 = (bf16[4,384]{1,0:T(4,128)(2,1)}, bf16[4,384]{1,0:T(4,128)(2,1)S(1)}, u32[]{:S(2)}, u32[]{:S(2)}) collective-permute-start(bf16[4,384]{1,0:T(4,128)(2,1)} %get-tuple-element.52), channel_id=1, source_target_pairs={{0,14},{1,15},{2,0},{3,1},{4,2},{5,3},{6,4},{7,5},{8,6},{9,7},{10,... | collective-permute-start | bytes 9224 | tf_op jit(solution)/shard_map/ppermute | solution.py:346
  43.0 5.6 %collective-permute-start.17 = (bf16[4,384]{1,0:T(4,128)(2,1)}, bf16[4,384]{1,0:T(4,128)(2,1)S(1)}, u32[]{:S(2)}, u32[]{:S(2)}) collective-permute-start(bf16[4,384]{1,0:T(4,128)(2,1)} %get-tuple-element.53), channel_id=1, source_target_pairs={{0,13},{1,14},{2,15},{3,0},{4,1},{5,2},{6,3},{7,4},{8,5},{9,6},{10... | collective-permute-start | bytes 9224 | tf_op jit(solution)/shard_map/ppermute | solution.py:346
  43.0 7.3 %collective-permute-start.18 = (bf16[4,384]{1,0:T(4,128)(2,1)}, bf16[4,384]{1,0:T(4,128)(2,1)S(1)}, u32[]{:S(2)}, u32[]{:S(2)}) collective-permute-start(bf16[4,384]{1,0:T(4,128)(2,1)} %get-tuple-element.54), channel_id=1, source_target_pairs={{0,12},{1,13},{2,14},{3,15},{4,0},{5,1},{6,2},{7,3},{8,4},{9,5},{1... | collective-permute-start | bytes 9224 | tf_op jit(solution)/shard_map/ppermute | solution.py:346
  43.4 8.5 %collective-permute-start.19 = (bf16[4,384]{1,0:T(4,128)(2,1)}, bf16[4,384]{1,0:T(4,128)(2,1)S(1)}, u32[]{:S(2)}, u32[]{:S(2)}) collective-permute-start(bf16[4,384]{1,0:T(4,128)(2,1)} %get-tuple-element.55), channel_id=1, source_target_pairs={{0,11},{1,12},{2,13},{3,14},{4,15},{5,0},{6,1},{7,2},{8,3},{9,4},{... | collective-permute-start | bytes 9224 | tf_op jit(solution)/shard_map/ppermute | solution.py:346
  44.8 20.2 %copy-start.15 = (bf16[4,384]{1,0:T(4,128)(2,1)}, bf16[4,384]{1,0:T(4,128)(2,1)S(1)}, u32[]{:S(2)}) copy-start(bf16[4,384]{1,0:T(4,128)(2,1)S(1)} %collective-permute-done.15.refs_1_) | copy-start | bytes 9220
  44.8 8.9 %collective-permute-start.20 = (bf16[4,384]{1,0:T(4,128)(2,1)}, bf16[4,384]{1,0:T(4,128)(2,1)S(1)}, u32[]{:S(2)}, u32[]{:S(2)}) collective-permute-start(bf16[4,384]{1,0:T(4,128)(2,1)} %get-tuple-element.56), channel_id=1, source_target_pairs={{0,10},{1,11},{2,12},{3,13},{4,14},{5,15},{6,0},{7,1},{8,2},{9,3},... | collective-permute-start | bytes 9224 | tf_op jit(solution)/shard_map/ppermute | solution.py:346
  48.6 16.4 %copy-start.16 = (bf16[4,384]{1,0:T(4,128)(2,1)}, bf16[4,384]{1,0:T(4,128)(2,1)S(1)}, u32[]{:S(2)}) copy-start(bf16[4,384]{1,0:T(4,128)(2,1)S(1)} %collective-permute-done.16.refs_2_) | copy-start | bytes 9220
  48.6 5.4 %collective-permute-start.21 = (bf16[4,384]{1,0:T(4,128)(2,1)}, bf16[4,384]{1,0:T(4,128)(2,1)S(1)}, u32[]{:S(2)}, u32[]{:S(2)}) collective-permute-start(bf16[4,384]{1,0:T(4,128)(2,1)} %get-tuple-element.57), channel_id=1, source_target_pairs={{0,9},{1,10},{2,11},{3,12},{4,13},{5,14},{6,15},{7,0},{8,1},{9,2},... | collective-permute-start | bytes 9224 | tf_op jit(solution)/shard_map/ppermute | solution.py:346
  48.6 16.3 %copy-start.17 = (bf16[4,384]{1,0:T(4,128)(2,1)}, bf16[4,384]{1,0:T(4,128)(2,1)S(1)}, u32[]{:S(2)}) copy-start(bf16[4,384]{1,0:T(4,128)(2,1)S(1)} %collective-permute-done.17.refs_3_) | copy-start | bytes 9220
  48.6 7.5 %collective-permute-start.22 = (bf16[4,384]{1,0:T(4,128)(2,1)}, bf16[4,384]{1,0:T(4,128)(2,1)S(1)}, u32[]{:S(2)}, u32[]{:S(2)}) collective-permute-start(bf16[4,384]{1,0:T(4,128)(2,1)} %get-tuple-element.58), channel_id=1, source_target_pairs={{0,8},{1,9},{2,10},{3,11},{4,12},{5,13},{6,14},{7,15},{8,0},{9,1},... | collective-permute-start | bytes 9224 | tf_op jit(solution)/shard_map/ppermute | solution.py:346
  50.4 14.6 %copy-start.18 = (bf16[4,384]{1,0:T(4,128)(2,1)}, bf16[4,384]{1,0:T(4,128)(2,1)S(1)}, u32[]{:S(2)}) copy-start(bf16[4,384]{1,0:T(4,128)(2,1)S(1)} %collective-permute-done.18.refs_4_) | copy-start | bytes 9220
  50.4 7.8 %collective-permute-start.23 = (bf16[4,384]{1,0:T(4,128)(2,1)}, bf16[4,384]{1,0:T(4,128)(2,1)S(1)}, u32[]{:S(2)}, u32[]{:S(2)}) collective-permute-start(bf16[4,384]{1,0:T(4,128)(2,1)} %get-tuple-element.59), channel_id=1, source_target_pairs={{0,7},{1,8},{2,9},{3,10},{4,11},{5,12},{6,13},{7,14},{8,15},{9,0},... | collective-permute-start | bytes 9224 | tf_op jit(solution)/shard_map/ppermute | solution.py:346
  52.0 13.0 %copy-start.19 = (bf16[4,384]{1,0:T(4,128)(2,1)}, bf16[4,384]{1,0:T(4,128)(2,1)S(1)}, u32[]{:S(2)}) copy-start(bf16[4,384]{1,0:T(4,128)(2,1)S(1)} %collective-permute-done.19.refs_5_) | copy-start | bytes 9220
  52.0 7.1 %collective-permute-start.24 = (bf16[4,384]{1,0:T(4,128)(2,1)}, bf16[4,384]{1,0:T(4,128)(2,1)S(1)}, u32[]{:S(2)}, u32[]{:S(2)}) collective-permute-start(bf16[4,384]{1,0:T(4,128)(2,1)} %get-tuple-element.60), channel_id=1, source_target_pairs={{0,6},{1,7},{2,8},{3,9},{4,10},{5,11},{6,12},{7,13},{8,14},{9,15},... | collective-permute-start | bytes 9224 | tf_op jit(solution)/shard_map/ppermute | solution.py:346
  53.7 11.3 %copy-start.20 = (bf16[4,384]{1,0:T(4,128)(2,1)}, bf16[4,384]{1,0:T(4,128)(2,1)S(1)}, u32[]{:S(2)}) copy-start(bf16[4,384]{1,0:T(4,128)(2,1)S(1)} %collective-permute-done.20.refs_6_) | copy-start | bytes 9220
  53.7 5.3 %collective-permute-start.25 = (bf16[4,384]{1,0:T(4,128)(2,1)}, bf16[4,384]{1,0:T(4,128)(2,1)S(1)}, u32[]{:S(2)}, u32[]{:S(2)}) collective-permute-start(bf16[4,384]{1,0:T(4,128)(2,1)} %get-tuple-element.61), channel_id=1, source_target_pairs={{0,5},{1,6},{2,7},{3,8},{4,9},{5,10},{6,11},{7,12},{8,13},{9,14},{... | collective-permute-start | bytes 9224 | tf_op jit(solution)/shard_map/ppermute | solution.py:346
  54.0 11.0 %copy-start.21 = (bf16[4,384]{1,0:T(4,128)(2,1)}, bf16[4,384]{1,0:T(4,128)(2,1)S(1)}, u32[]{:S(2)}) copy-start(bf16[4,384]{1,0:T(4,128)(2,1)S(1)} %collective-permute-done.21.refs_7_) | copy-start | bytes 9220
  54.0 5.6 %collective-permute-start.26 = (bf16[4,384]{1,0:T(4,128)(2,1)}, bf16[4,384]{1,0:T(4,128)(2,1)S(1)}, u32[]{:S(2)}, u32[]{:S(2)}) collective-permute-start(bf16[4,384]{1,0:T(4,128)(2,1)} %get-tuple-element.62), channel_id=1, source_target_pairs={{0,4},{1,5},{2,6},{3,7},{4,8},{5,9},{6,10},{7,11},{8,12},{9,13},{1... | collective-permute-start | bytes 9224 | tf_op jit(solution)/shard_map/ppermute | solution.py:346
  56.1 8.9 %copy-start.22 = (bf16[4,384]{1,0:T(4,128)(2,1)}, bf16[4,384]{1,0:T(4,128)(2,1)S(1)}, u32[]{:S(2)}) copy-start(bf16[4,384]{1,0:T(4,128)(2,1)S(1)} %collective-permute-done.22.refs_8_) | copy-start | bytes 9220
  56.1 6.1 %collective-permute-start.27 = (bf16[4,384]{1,0:T(4,128)(2,1)}, bf16[4,384]{1,0:T(4,128)(2,1)S(1)}, u32[]{:S(2)}, u32[]{:S(2)}) collective-permute-start(bf16[4,384]{1,0:T(4,128)(2,1)} %get-tuple-element.63), channel_id=1, source_target_pairs={{0,3},{1,4},{2,5},{3,6},{4,7},{5,8},{6,9},{7,10},{8,11},{9,12},{10... | collective-permute-start | bytes 9224 | tf_op jit(solution)/shard_map/ppermute | solution.py:346
  58.2 6.8 %copy-start.23 = (bf16[4,384]{1,0:T(4,128)(2,1)}, bf16[4,384]{1,0:T(4,128)(2,1)S(1)}, u32[]{:S(2)}) copy-start(bf16[4,384]{1,0:T(4,128)(2,1)S(1)} %collective-permute-done.23.refs_9_) | copy-start | bytes 9220
  58.2 6.5 %collective-permute-start.28 = (bf16[4,384]{1,0:T(4,128)(2,1)}, bf16[4,384]{1,0:T(4,128)(2,1)S(1)}, u32[]{:S(2)}, u32[]{:S(2)}) collective-permute-start(bf16[4,384]{1,0:T(4,128)(2,1)} %get-tuple-element.64), channel_id=1, source_target_pairs={{0,2},{1,3},{2,4},{3,5},{4,6},{5,7},{6,8},{7,9},{8,10},{9,11},{10,... | collective-permute-start | bytes 9224 | tf_op jit(solution)/shard_map/ppermute | solution.py:346
  59.0 6.0 %copy-start.24 = (bf16[4,384]{1,0:T(4,128)(2,1)}, bf16[4,384]{1,0:T(4,128)(2,1)S(1)}, u32[]{:S(2)}) copy-start(bf16[4,384]{1,0:T(4,128)(2,1)S(1)} %collective-permute-done.24.refs_10_) | copy-start | bytes 9220
  59.0 5.9 %collective-permute-start.29 = (bf16[4,384]{1,0:T(4,128)(2,1)}, bf16[4,384]{1,0:T(4,128)(2,1)S(1)}, u32[]{:S(2)}, u32[]{:S(2)}) collective-permute-start(bf16[4,384]{1,0:T(4,128)(2,1)} %get-tuple-element.65), channel_id=1, source_target_pairs={{0,1},{1,2},{2,3},{3,4},{4,5},{5,6},{6,7},{7,8},{8,9},{9,10},{10,1... | collective-permute-start | bytes 9224 | tf_op jit(solution)/shard_map/ppermute | solution.py:346
  59.0 6.0 %copy-start.25 = (bf16[4,384]{1,0:T(4,128)(2,1)}, bf16[4,384]{1,0:T(4,128)(2,1)S(1)}, u32[]{:S(2)}) copy-start(bf16[4,384]{1,0:T(4,128)(2,1)S(1)} %collective-permute-done.25.refs_11_) | copy-start | bytes 9220
  59.6 5.4 %copy-start.26 = (bf16[4,384]{1,0:T(4,128)(2,1)}, bf16[4,384]{1,0:T(4,128)(2,1)S(1)}, u32[]{:S(2)}) copy-start(bf16[4,384]{1,0:T(4,128)(2,1)S(1)} %collective-permute-done.26.refs_12_) | copy-start | bytes 9220
  62.3 2.8 %copy-start.27 = (bf16[4,384]{1,0:T(4,128)(2,1)}, bf16[4,384]{1,0:T(4,128)(2,1)S(1)}, u32[]{:S(2)}) copy-start(bf16[4,384]{1,0:T(4,128)(2,1)S(1)} %collective-permute-done.27.refs_13_) | copy-start | bytes 9220
  64.7 0.6 copy-start.28
  64.9 0.6 copy-start.29

commit v3 on v1

--- a/solution.py
+++ b/solution.py
@@ -21,6 +21,8 @@
 BF16 = jnp.bfloat16
 F32 = jnp.float32
 LANES = 128
+SPATIAL_VMEM = 56 * 2**20
+TEMPORAL_VMEM = 40 * 2**20
 NT = (((1,), (1,)), ((), ()))
 
 
@@ -35,6 +37,10 @@
     return centered * lax.rsqrt(spread + EPSILON) * scale_gain
 
 
+def as_row(ref):
+    return ref[...].reshape(1, ref.shape[0])
+
+
 def matmul(left, right):
     return jnp.dot(left, right, preferred_element_type=F32)
 
@@ -49,30 +55,39 @@
     return (powers * (1.0 / jnp.sum(powers, axis=0, keepdims=True))).astype(BF16)
 
 
-def spatial_kernel(
-    groups,
-    gamma_ref,
-    x_ref,
-    rotation_ref,
-    translation_ref,
-    types_ref,
-    mask_ref,
-    table_ref,
-    null_ref,
-    gain_ref,
-    proj_ref,
-    points_ref,
-    spatial_out_ref,
-    out_ref,
-    columns_ref,
-    wide_ref,
-    rows_ref,
-):
+def spatial_kernel(groups, gamma_ref, *refs):
+    sources, refs = refs[:11], refs[11:]
+    later, refs = refs[:5], refs[5:]
+    out_ref, later_out, refs = refs[0], refs[1:6], refs[6:]
+    local, (columns_ref, wide_ref, rows_ref, sems) = refs[:11], refs[11:]
+    copies = [
+        pltpu.make_async_copy(source, target, sems.at[index])
+        for index, (source, target) in enumerate(
+            zip(sources + later, local + tuple(later_out), strict=True)
+        )
+    ]
+    for copy in copies:
+        copy.start()
+    (
+        x_ref,
+        table_ref,
+        types_ref,
+        null_ref,
+        gain_ref,
+        rotation_ref,
+        translation_ref,
+        mask_ref,
+        proj_ref,
+        points_ref,
+        spatial_out_ref,
+    ) = local
+    for copy in copies[:8]:
+        copy.wait()
     frames, residues, width = x_ref.shape
     heads = gamma_ref.shape[0]
     head_dim = width // heads
     block_heads = LANES // head_dim
-    all_points = points_ref.shape[1]
+    all_points = points_ref.shape[0]
     half = all_points // 2
     per_head = half // heads
     points_wide = wide_ref.shape[1]
@@ -84,7 +99,7 @@
     kinds = table_ref.shape[0]
     onehot = (iota((kinds, residues), 0) == types_ref[...]).astype(F32).T.astype(BF16)
     conditional = matmul(onehot, table_ref[...])
-    empty = null_ref[...].astype(F32)
+    empty = as_row(null_ref).astype(F32)
 
     lane = iota((1, points_wide), 1)
     component = lane % 3
@@ -146,10 +161,15 @@
 
         state = x_ref[frame].astype(F32)
         initial = jnp.concatenate([state + conditional, state + empty], axis=0)
-        normed = layer_norm(initial, gain_ref[...]).astype(BF16)
+        normed = layer_norm(initial, as_row(gain_ref)).astype(BF16)
+        if frame == 0:
+            copies[8].wait()
+            copies[9].wait()
         projected = matmul(normed, proj_ref[...])
         wide_ref[:, points_wide - LANES :] = jnp.zeros((BRANCHES * residues, LANES), F32)
-        wide_ref[:, :all_points] = matmul(normed, points_ref[...])
+        wide_ref[:, :all_points] = lax.dot_general(
+            normed, points_ref[...], NT, preferred_element_type=F32
+        )
         points = wide_ref[...]
 
         placed = None
@@ -238,6 +258,8 @@
                     folded = folded + mixed[:, start : start + fold]
                 pieces.append(folded)
             contexts.append(jnp.concatenate(pieces, axis=0).T.astype(BF16))
+        if frame == 0:
+            copies[10].wait()
         update = matmul(jnp.concatenate(contexts, axis=0), spatial_out_ref[...])
         for branch in range(BRANCHES):
             total = initial[branch * residues : (branch + 1) * residues]
@@ -248,6 +270,8 @@
             for group in range(groups):
                 rows_ref[group, place : place + share, :] = total[group * share : (group + 1) * share]
     out_ref[...] = rows_ref[...].astype(BF16)
+    for copy in copies[11:]:
+        copy.wait()
 
 
 def temporal_kernel(
@@ -270,7 +294,7 @@
     share = period // BRANCHES
 
     initial = x_ref[...].astype(F32).reshape(rows, width)
-    normed = layer_norm(initial, gain_ref[...]).astype(BF16)
+    normed = layer_norm(initial, as_row(gain_ref)).astype(BF16)
     projected = matmul(normed, proj_ref[...])
     queries = projected[:, :width].astype(BF16) * jnp.asarray(1.0 / math.sqrt(head_dim), BF16)
     keys = projected[:, width : 2 * width].astype(BF16)
@@ -297,10 +321,10 @@
             )
     context = jnp.concatenate(pieces, axis=0).T.astype(BF16)
     after_time = initial + matmul(context, temporal_out_ref[...])
-    second = layer_norm(after_time, hidden_gain_ref[...]).astype(BF16)
+    second = layer_norm(after_time, as_row(hidden_gain_ref)).astype(BF16)
     hidden = jax.nn.gelu(matmul(second, hidden_in_ref[...])).astype(BF16)
     result = (after_time + matmul(hidden, hidden_out_ref[...])).astype(BF16).astype(F32)
-    headed = layer_norm(result, head_gain_ref[...]).astype(BF16)
+    headed = layer_norm(result, as_row(head_gain_ref)).astype(BF16)
     branch_velocity = matmul(headed, head_out_ref[...]).reshape(rows // period, period, width)
     conditional = branch_velocity[:, :share]
     empty = branch_velocity[:, share:]
@@ -338,48 +362,55 @@
     frames, residues, width = x_state.shape
     share = residues // groups
     period = BRANCHES * share
-    spatial = pl.pallas_call(
+    sources = (
+        x_state,
+        type_table,
+        residue_types[None],
+        null_embed,
+        spatial_gain,
+        rotations,
+        translations,
+        pocket_mask[None],
+        spatial_proj,
+        spatial_points.T,
+        spatial_out,
+    )
+    later = (temporal_proj, temporal_out, hidden_in, hidden_out, head_out)
+    spatial, *later = pl.pallas_call(
         functools.partial(spatial_kernel, groups),
-        out_shape=jax.ShapeDtypeStruct((groups, frames * period, width), BF16),
-        in_specs=[whole(pltpu.SMEM)] + [whole()] * 11,
-        out_specs=whole(),
-        scratch_shapes=[
+        out_shape=[pltpu.VMEM((groups, frames * period, width), BF16)]
+        + [pltpu.VMEM(array.shape, array.dtype) for array in later],
+        in_specs=[whole(pltpu.SMEM)] + [whole(pl.ANY)] * (len(sources) + len(later)),
+        out_specs=[whole()] * (1 + len(later)),
+        scratch_shapes=[pltpu.VMEM(array.shape, array.dtype) for array in sources]
+        + [
             pltpu.VMEM((16, residues), F32),
             pltpu.VMEM((BRANCHES * residues, round_up(spatial_points.shape[1], LANES)), F32),
             pltpu.VMEM((groups, frames * period, width), F32),
+            pltpu.SemaphoreType.DMA((len(sources) + len(later),)),
         ],
+        compiler_params=pltpu.CompilerParams(vmem_limit_bytes=SPATIAL_VMEM),
         name="spatial",
-    )(
-        spatial_gamma,
-        x_state,
-        rotations,
-        translations,
-        residue_types[None],
-        pocket_mask[None],
-        type_table,
-        null_embed[None],
-        spatial_gain[None],
-        spatial_proj,
-        spatial_points,
-        spatial_out,
-    )
+    )(spatial_gamma, *sources, *later)
     arrived = lax.all_to_all(spatial, "seq", split_axis=0, concat_axis=0, tiled=True)
+    proj_local, out_local, in_local, hidden_local, head_local = later
     guided = pl.pallas_call(
         functools.partial(temporal_kernel, period),
-        out_shape=jax.ShapeDtypeStruct((groups * frames, share, width), BF16),
+        out_shape=pltpu.VMEM((groups * frames, share, width), BF16),
         in_specs=[whole()] * 9,
         out_specs=whole(),
+        compiler_params=pltpu.CompilerParams(vmem_limit_bytes=TEMPORAL_VMEM),
         name="temporal",
     )(
         arrived,
-        temporal_gain[None],
-        temporal_proj,
-        temporal_out,
-        hidden_gain[None],
-        hidden_in,
-        hidden_out,
-        head_gain[None],
-        head_out,
+        temporal_gain,
+        proj_local,
+        out_local,
+        hidden_gain,
+        in_local,
+        hidden_local,
+        head_gain,
+        head_local,
     )
     velocity = lax.all_to_all(guided, "seq", split_axis=0, concat_axis=1, tiled=True)
     x_next = (

time: 43.1 us -> 34.2 us (0.79)
  blocking collectives: 10.2 us -> 23.9 us
  starting transfers between devices: 7.39 us -> 0 us
  local copies, waits for them, and re-layouts: 6.69 us -> 0.05 us
  waiting for transfers between devices: 5.7 us -> 0 us
  Pallas kernels: 11.4 us -> 8.66 us
    all_to_all x0 -> x1, blocking collectives: none -> 14.6 us  [body(): lax.all_to_all(spatial, 'seq', split_axis=0, concat_axis=0, tiled=True)]
    all_to_all x1 -> x0, starting transfers between devices: 7.39 us -> none  [body(): lax.all_to_all(spatial, 'seq', split_axis=0, concat_axis=0, tiled=True)]
    all_to_all x1 -> x0, waiting for transfers between devices: 5.7 us -> none  [body(): lax.all_to_all(spatial, 'seq', split_axis=0, concat_axis=0, tiled=True)]
    broadcast_in_dim x5 -> x0, local copies, waits for them, and re-layouts: 4.17 us -> none  [the longest x1 1.24 us: body(): spatial_gain[None]]
    pallas_call x2, Pallas kernels: 11.4 us -> 8.66 us  [the longest x1 6.27 us: body(): pl.pallas_call(functools.partial(spatial_kernel, groups), out_shape=[pltp...]
    unnamed x15 -> x12, local copies, waits for them, and re-layouts: 2.5 us -> 0.03 us
    all_to_all x1, blocking collectives: 10.2 us -> 9.34 us  [body(): lax.all_to_all(guided, 'seq', split_axis=0, concat_axis=1, tiled=True)]
  transfers between devices with their start and end apart: 1 -> 0, of which waited for: 1 -> 0; matrix products, arithmetic and copies ran while one was open for 4% -> 0% of each run, Pallas kernels for 0% -> 0%
where the time goes in v3:
time: 34.2 us; the launch traced here: 34 us
  blocking collectives  23.9 us (70%)
  Pallas kernels  8.66 us (25%)
  between operations  0.72 us (2%)
  other arithmetic  0.65 us (2%)
    all_to_all x1, blocking collectives, body(): lax.all_to_all(spatial, 'seq', split_axis=0, concat_axis=0, tiled=True)  14.6 us
    all_to_all x1, blocking collectives, body(): lax.all_to_all(guided, 'seq', split_axis=0, concat_axis=1, tiled=True)  9.34 us
    pallas_call x1, Pallas kernels, body(): pl.pallas_call(functools.partial(spatial_kernel, groups), out_shape=[pltp...  6.27 us
    pallas_call x1, Pallas kernels, body(): pl.pallas_call(functools.partial(temporal_kernel, period), out_shape=pltp...  2.4 us

profile of v3, /device:TPU:0, one launch (start us, length us, event | category | flops | bytes accessed | tf_op | source)
XLA Modules:
  0.0 34.0 jit_solution(8060766838882418782)
XLA Ops:
  0.6 0.0 copy-start
  0.6 0.0 copy-start.1
  0.7 0.0 copy-start.2
  0.7 6.3 %spatial.1 = (bf16[16,8,384]{2,1,0:T(8,128)(2,1)S(1)}, bf16[384,1152]{1,0:T(8,128)(2,1)S(1)}, bf16[384,384]{1,0:T(8,128)(2,1)S(1)}, bf16[384,1536]{1,0:T(8,128)(...) custom-call(f32[12]{0:T(128)} %gamma_ref.1, bf16[1,64,384]{2,1,0:T(8,128)(2,1)} %refs_0_.1, ...), custom_call_target="tpu_custom_call" | custom-call | tf_op jit(solution)/shard_map/spatial/pallas_call | solution.py:379
  6.9 14.6 %all_to_all.17.x_ref = bf16[16,8,384]{2,1,0:T(8,128)(2,1)S(1)} all-to-all(bf16[16,8,384]{2,1,0:T(8,128)(2,1)S(1)} %get-tuple-element.8), channel_id=1, replica_groups=mesh['parts'=2,'seq'=16] {'seq'}, dimensions={0} | all-to-all | bytes 196608 | tf_op jit(solution)/shard_map/all_to_all | solution.py:395
  21.5 0.0 copy-done
  21.5 0.0 copy-done.1
  21.5 0.0 copy-done.2
  21.6 0.0 copy-start.3
  21.6 0.0 copy-start.5
  21.6 2.4 %temporal.1 = bf16[16,4,384]{2,1,0:T(4,128)(2,1)S(1)} custom-call(bf16[16,8,384]{2,1,0:T(8,128)(2,1)S(1)} %all_to_all.17.x_ref, f32[384]{0:T(512)S(1)} %copy-done, bf16[384,1152]{1,0:T(8,128)(2,1)S(1)} %get-tuple-element.9.proj_ref, bf16[384,384]{1,0:T(8,128)(2,1)S(1)} %get-tuple-element.10.temporal_out_ref, f32[384]{0:T(512)S(1)} %copy-done.1, ...), custom_call_target="tpu_custom_call" | custom-call | tf_op jit(solution)/shard_map/temporal/pallas_call | solution.py:397
  24.0 9.3 %all_to_all.18 = bf16[16,4,384]{2,1,0:T(4,128)(2,1)S(1)} all-to-all(bf16[16,4,384]{2,1,0:T(4,128)(2,1)S(1)} %temporal.1), channel_id=1, replica_groups=mesh['parts'=2,'seq'=16] {'seq'}, dimensions={0} | all-to-all | bytes 98304 | tf_op jit(solution)/shard_map/all_to_all | solution.py:415
  33.3 0.0 copy-done.3
  33.3 0.0 copy-done.5
  33.4 0.0 copy-start.4
  33.4 0.6 %add_convert_fusion = bf16[1,64,384]{2,1,0:T(8,128)(2,1)} fusion(bf16[1,64,384]{2,1,0:T(8,128)(2,1)S(1)} %copy-done.5, bf16[1,64,384]{2,1,0:T(8,128)(2,1)S(1)} %all_to_all.14, bf16[1,64,384]{2,1,0:T(8,128)(2,1)S(1)} %copy-done.3), kind=kLoop, calls=%fused_computation | loop fusion | flops 196608 | bytes 196608 | tf_op jit(solution)/shard_map/convert_element_type | solution.py:420
  34.0 0.0 copy-done.4
  (1 shorter events, 0.0 us)
Async XLA Ops:
  0.6 20.9 %copy-start = (f32[384]{0:T(512)S(1)}, f32[384]{0:T(512)}, u32[]{:S(2)}) copy-start(f32[384]{0:T(512)} %gain_ref.1) | copy-start | bytes 4612
  0.6 20.9 %copy-start.1 = (f32[384]{0:T(512)S(1)}, f32[384]{0:T(512)}, u32[]{:S(2)}) copy-start(f32[384]{0:T(512)} %hidden_gain_ref.1) | copy-start | bytes 4612
  0.7 20.9 %copy-start.2 = (f32[384]{0:T(512)S(1)}, f32[384]{0:T(512)}, u32[]{:S(2)}) copy-start(f32[384]{0:T(512)} %head_gain_ref.1) | copy-start | bytes 4612
  21.6 11.8 %copy-start.3 = (bf16[1,64,384]{2,1,0:T(8,128)(2,1)S(1)}, bf16[1,64,384]{2,1,0:T(8,128)(2,1)}, u32[]{:S(2)}) copy-start(bf16[1,64,384]{2,1,0:T(8,128)(2,1)} %refs_0_.1) | copy-start | bytes 147460
  21.6 11.8 %copy-start.5 = (bf16[1,64,384]{2,1,0:T(8,128)(2,1)S(1)}, bf16[1,64,384]{2,1,0:T(8,128)(2,1)}, u32[]{:S(2)}) copy-start(bf16[1,64,384]{2,1,0:T(8,128)(2,1)} %param.22) | copy-start | bytes 147460
  33.4 0.7 %copy-start.4 = (bf16[1,64,384]{2,1,0:T(8,128)(2,1)}, bf16[1,64,384]{2,1,0:T(8,128)(2,1)S(1)}, u32[]{:S(2)}) copy-start(bf16[1,64,384]{2,1,0:T(8,128)(2,1)S(1)} %all_to_all.14) | copy-start | bytes 147460

commit v4 on v3

--- a/solution.py
+++ b/solution.py
@@ -276,7 +276,7 @@
 
 def temporal_kernel(
     period,
-    x_ref,
+    gathered_ref,
     gain_ref,
     proj_ref,
     temporal_out_ref,
@@ -286,7 +286,12 @@
     head_gain_ref,
     head_out_ref,
     out_ref,
+    x_ref,
+    sem,
 ):
+    copy = pltpu.make_async_copy(gathered_ref.at[:, lax.axis_index("seq")], x_ref, sem)
+    copy.start()
+    copy.wait()
     groups, depth, width = x_ref.shape
     rows = groups * depth
     head_dim = width // THEADS
@@ -392,13 +397,17 @@
         compiler_params=pltpu.CompilerParams(vmem_limit_bytes=SPATIAL_VMEM),
         name="spatial",
     )(spatial_gamma, *sources, *later)
-    arrived = lax.all_to_all(spatial, "seq", split_axis=0, concat_axis=0, tiled=True)
+    arrived = lax.all_gather(spatial, "seq")
     proj_local, out_local, in_local, hidden_local, head_local = later
     guided = pl.pallas_call(
         functools.partial(temporal_kernel, period),
         out_shape=pltpu.VMEM((groups * frames, share, width), BF16),
-        in_specs=[whole()] * 9,
+        in_specs=[whole(pl.ANY)] + [whole()] * 8,
         out_specs=whole(),
+        scratch_shapes=[
+            pltpu.VMEM((groups, frames * period, width), BF16),
+            pltpu.SemaphoreType.DMA,
+        ],
         compiler_params=pltpu.CompilerParams(vmem_limit_bytes=TEMPORAL_VMEM),
         name="temporal",
     )(
@@ -412,7 +421,9 @@
         head_gain,
         head_local,
     )
-    velocity = lax.all_to_all(guided, "seq", split_axis=0, concat_axis=1, tiled=True)
+    gathered = lax.all_gather(guided.reshape(groups, frames * share, width), "seq")
+    velocity = lax.dynamic_index_in_dim(gathered, lax.axis_index("seq"), 1, keepdims=False)
+    velocity = jnp.moveaxis(velocity.reshape(groups, frames, share, width), 0, 1).reshape(x_state.shape)
     x_next = (
         x_state.astype(F32)
         + STEP_SIZE * velocity.astype(F32)

time: 34.2 us -> 92.5 us (2.70)
  waiting for transfers between devices: 0 us -> 42.5 us
  between operations: 0.72 us -> 14.1 us
  local copies, waits for them, and re-layouts: 0.05 us -> 3.77 us
  blocking collectives: 23.9 us -> 21.6 us
    all_gather x0 -> x1, waiting for transfers between devices: none -> 42.5 us  [body(): arrived = lax.all_gather(spatial, 'seq')]
    all_to_all x2 -> x0, blocking collectives: 23.9 us -> none  [the longest x1 14.6 us: body(): lax.all_to_all(spatial, 'seq', split_axis=0, concat_axis=0, tiled=True)]
    all_gather x0 -> x1, blocking collectives: none -> 21.6 us  [body(): lax.all_gather(guided.reshape(groups, frames * share, width), 'seq')]
    unnamed x12 -> x16, local copies, waits for them, and re-layouts: 0.03 us -> 3.73 us
  transfers between devices with their start and end apart: 0 -> 1, of which waited for: 0 -> 1; matrix products, arithmetic and copies ran while one was open for 0% -> 0% of each run, Pallas kernels for 0% -> 0%
where the time goes in v4:
time: 92.5 us; the launch traced here: 92.2 us
  waiting for transfers between devices  42.5 us (46%)
  blocking collectives  21.6 us (23%)
  between operations  14.1 us (15%)
  Pallas kernels  8.7 us (9%)
  local copies, waits for them, and re-layouts  3.77 us (4%)
  other arithmetic  1.49 us (2%)
    all_gather x1, waiting for transfers between devices, body(): arrived = lax.all_gather(spatial, 'seq')  42.5 us
    all_gather x1, blocking collectives, body(): lax.all_gather(guided.reshape(groups, frames * share, width), 'seq')  21.6 us
    pallas_call x1, Pallas kernels, body(): pl.pallas_call(functools.partial(spatial_kernel, groups), out_shape=[pltp...  6.27 us
    unnamed x16, local copies, waits for them, and re-layouts  3.73 us
    pallas_call x1, Pallas kernels, body(): pl.pallas_call(functools.partial(temporal_kernel, period), out_shape=pltp...  2.43 us
  transfers between devices with their start and end apart: 1, of which 1 were waited for; matrix products, arithmetic and copies ran while one was open for 0% of the time, Pallas kernels for 0%

profile of v4, /device:TPU:0, one launch (start us, length us, event | category | flops | bytes accessed | tf_op | source)
XLA Modules:
  0.0 92.2 jit_solution(3811953506717697272)
XLA Ops:
  7.2 0.0 all-gather.4.cloned.1.call-start
  7.2 0.0 copy-start.4
  7.2 0.0 copy-start.5
  7.2 0.0 copy-start.6
  7.2 6.3 %spatial.1 = (bf16[16,8,384]{2,1,0:T(8,128)(2,1)S(1)}, bf16[384,1152]{1,0:T(8,128)(2,1)S(1)}, bf16[384,384]{1,0:T(8,128)(2,1)S(1)}, bf16[384,1536]{1,0:T(8,128)(...) custom-call(f32[12]{0:T(128)} %gamma_ref.1, bf16[1,64,384]{2,1,0:T(8,128)(2,1)} %refs_0_.1, ...), custom_call_target="tpu_custom_call" | custom-call | tf_op jit(solution)/shard_map/spatial/pallas_call | solution.py:384
  13.5 0.0 copy-start.1
  13.5 0.7 copy-done.1
  14.2 0.0 copy-start.3
  14.2 0.6 copy-done.3
  14.9 0.0 all-gather.4.cloned.1.call-update
  14.9 42.5 %all-gather.4.cloned.1.call-done = bf16[256,8,384]{2,1,0:T(8,128)(2,1)} async-done(((bf16[16,8,384]{2,1,0:T(8,128)(2,1)}), bf16[256,8,384]{2,1,0:T(8,128)(2,1)}) %all-gather.4.cloned.1.call-update) | async-done | bytes 1572880 | tf_op jit(solution)/shard_map/all_gather | solution.py:400
  57.4 0.0 copy-done.4
  57.4 0.0 copy-done.5
  57.4 0.0 copy-done.6
  57.4 0.0 copy-start
  57.4 1.4 %copy-done = bf16[256,8,384]{2,1,0:T(8,128)(2,1)S(1)} copy-done((bf16[256,8,384]{2,1,0:T(8,128)(2,1)S(1)}, bf16[256,8,384]{2,1,0:T(8,128)(2,1)}, u32[]{:S(2)}) %copy-start) | copy-done | bytes 1572888
  58.9 0.0 copy-start.2
  58.9 1.0 %copy-done.2 = bf16[384,384]{1,0:T(8,128)(2,1)S(1)} copy-done((bf16[384,384]{1,0:T(8,128)(2,1)S(1)}, bf16[384,384]{1,0:T(8,128)(2,1)}, u32[]{:S(2)}) %copy-start.2) | copy-done | bytes 294936
  59.8 2.4 %temporal.1 = bf16[16,4,384]{2,1,0:T(4,128)(2,1)S(1)} custom-call(bf16[16,16,8,384]{3,2,1,0:T(8,128)(2,1)S(1)} %bitcast.5, f32[384]{0:T(512)S(1)} %copy-done.4, bf16[384,1152]{1,0:T(8,128)(2,1)S(1)} %get-tuple-element.9.proj_ref, bf16[384,384]{1,0:T(8,128)(2,1)S(1)} %get-tuple-element.10.temporal_out_ref, f32[384]{0:T(512)S(1)} %copy-done.5, ...), custom_call_target="tpu_custom_call" | custom-call | tf_op jit(solution)/shard_map/temporal/pallas_call | solution.py:402
  62.3 21.6 %all-gather.1 = bf16[256,4,384]{2,1,0:T(4,128)(2,1)S(1)} all-gather(bf16[16,4,384]{2,1,0:T(4,128)(2,1)S(1)} %temporal.1), channel_id=3, replica_groups=mesh['parts'=2,'seq'=16] {'seq'}, dimensions={0}, use_global_device_ids=true | all-gather | bytes 835584 | tf_op jit(solution)/shard_map/all_gather | solution.py:424
  83.9 0.0 copy-start.7
  83.9 1.5 %add_convert_fusion = bf16[1,64,384]{2,1,0:T(8,128)(2,1)} fusion(bf16[1,64,384]{2,1,0:T(8,128)(2,1)} %param.22, bf16[1,64,384]{2,1,0:T(8,128)(2,1)S(1)} %reshape_transpose_reshape.3, bf16[1,64,384]{2,1,0:T(8,128)(2,1)} %refs_0_.1), kind=kLoop, calls=%fused_computation | loop fusion | flops 196608 | bytes 196608 | tf_op jit(solution)/shard_map/convert_element_type | solution.py:431
  85.4 0.0 copy-done.7
  (2 shorter events, 0.0 us)
Async XLA Ops:
  7.2 50.3 %all-gather.4.cloned.1.call-start = ((), (), s32[]{:S(2)}) async-start(), calls=%async_computation | async-start | bytes 1671168 | tf_op jit(solution)/shard_map/all_gather | solution.py:400
  7.2 50.2 %copy-start.4 = (f32[384]{0:T(512)S(1)}, f32[384]{0:T(512)}, u32[]{:S(2)}) copy-start(f32[384]{0:T(512)} %gain_ref.1) | copy-start | bytes 4612
  7.2 50.2 %copy-start.5 = (f32[384]{0:T(512)S(1)}, f32[384]{0:T(512)}, u32[]{:S(2)}) copy-start(f32[384]{0:T(512)} %hidden_gain_ref.1) | copy-start | bytes 4612
  7.2 50.2 %copy-start.6 = (f32[384]{0:T(512)S(1)}, f32[384]{0:T(512)}, u32[]{:S(2)}) copy-start(f32[384]{0:T(512)} %head_gain_ref.1) | copy-start | bytes 4612
  13.5 0.7 copy-start.1
  14.2 0.6 copy-start.3
  57.4 1.4 %copy-start = (bf16[256,8,384]{2,1,0:T(8,128)(2,1)S(1)}, bf16[256,8,384]{2,1,0:T(8,128)(2,1)}, u32[]{:S(2)}) copy-start(bf16[256,8,384]{2,1,0:T(8,128)(2,1)} %all-gather.4.cloned.1.call-done) | copy-start | bytes 4718596
  58.9 1.0 %copy-start.2 = (bf16[384,384]{1,0:T(8,128)(2,1)S(1)}, bf16[384,384]{1,0:T(8,128)(2,1)}, u32[]{:S(2)}) copy-start(bf16[384,384]{1,0:T(8,128)(2,1)} %copy-done.1) | copy-start | bytes 884740
  83.9 1.5 %copy-start.7 = (bf16[1,64,384]{2,1,0:T(8,128)(2,1)}, bf16[1,64,384]{2,1,0:T(8,128)(2,1)S(1)}, u32[]{:S(2)}) copy-start(bf16[1,64,384]{2,1,0:T(8,128)(2,1)S(1)} %reshape_transpose_reshape.3) | copy-start | bytes 147460
Sparse Core Ops, SparseCore 0:
  15.0 42.3 all-gather.3

commit v5 on v3

v5 whole, which is shorter than its diff:
```python
import functools
import math

import jax
import jax.numpy as jnp
from jax import lax
from jax.experimental import pallas as pl
from jax.experimental.pallas import tpu as pltpu
from jax.sharding import PartitionSpec as P

THEADS = 6
BRANCHES = 2

WEIGHT_LOGIT = 0.7071067811865476
WEIGHT_POINT = 0.23570226039551584
GUIDE = 2.0
STEP_SIZE = 0.25
NOISE_SCALE = 0.2
EPSILON = 1e-05

BF16 = jnp.bfloat16
F32 = jnp.float32
LANES = 128
SLOT = 64
SPATIAL_VMEM = 56 * 2**20
TEMPORAL_VMEM = 40 * 2**20
NT = (((1,), (1,)), ((), ()))


def layer_norm(values, scale_gain):
    average = jnp.mean(values, axis=-1, keepdims=True)
    centered = values - average
    spread = jnp.mean(centered * centered, axis=-1, keepdims=True)
    return centered * lax.rsqrt(spread + EPSILON) * scale_gain


def as_row(ref):
    return ref[...].reshape(1, ref.shape[0])


def matmul(left, right):
    return jnp.dot(left, right, preferred_element_type=F32)


def iota(shape, axis):
    return lax.broadcasted_iota(jnp.int32, shape, axis)


def softmax_down(logits, allowed):
    logits = jnp.where(allowed, logits, -jnp.inf)
    powers = jnp.exp(logits - jnp.max(logits, axis=0, keepdims=True))
    return (powers * (1.0 / jnp.sum(powers, axis=0, keepdims=True))).astype(BF16)


def spatial_kernel(groups, gamma_ref, *refs):
    sources, refs = refs[:11], refs[11:]
    later, refs = refs[:5], refs[5:]
    out_ref, later_out, refs = refs[0], refs[1:6], refs[6:]
    local, (columns_ref, rows_ref, sems) = refs[:11], refs[11:]
    (
        x_ref,
        table_ref,
        types_ref,
        null_ref,
        gain_ref,
        rotation_ref,
        translation_ref,
        mask_ref,
        proj_ref,
        spatial_out_ref,
        points_ref,
    ) = local
    frames, residues, width = x_ref.shape
    heads = gamma_ref.shape[0]
    head_dim = width // heads
    blocks = width // LANES
    block_heads = LANES // head_dim
    slot_rows = sources[-1].shape[0] // (2 * blocks)
    per_head = slot_rows // block_heads
    share = residues // groups
    fold = max(residues, LANES)
    stacked_rows = block_heads * residues
    point_scale = 0.5 * WEIGHT_LOGIT * WEIGHT_POINT

    pairs = list(zip(sources[:10], local[:10], strict=True))
    for slot in range(2 * blocks):
        pairs.append(
            (
                sources[-1].at[pl.ds(slot * slot_rows, slot_rows), :],
                points_ref.at[pl.ds(slot * SLOT, slot_rows), :],
            )
        )
    pairs += list(zip(later, later_out, strict=True))
    copies = [
        pltpu.make_async_copy(source, target, sems.at[index])
        for index, (source, target) in enumerate(pairs)
    ]
    for copy in copies:
        copy.start()
    small, wide, after = copies[:8], [copies[8]] + copies[10 : 10 + 2 * blocks], copies[9]

    for slot in range(2 * blocks):
        points_ref[slot * SLOT + slot_rows : (slot + 1) * SLOT, :] = jnp.zeros(
            (SLOT - slot_rows, width), BF16
        )
    lane = iota((1, LANES), 1)
    low = lane < SLOT
    place = lane % SLOT
    component = jnp.where(place < slot_rows, place % 3, 3)
    in_first = (place >= slot_rows) & (place < slot_rows + block_heads)
    in_second = (place >= slot_rows + block_heads) & (place < slot_rows + 2 * block_heads)
    in_norm = in_first | in_second
    member, block_member = [], []
    for part in range(block_heads):
        own = (
            ((place >= part * per_head) & (place < (part + 1) * per_head))
            | (place == slot_rows + part)
            | (place == slot_rows + block_heads + part)
        )
        member.append(own)
        block_member.append((lane >= part * head_dim) & (lane < (part + 1) * head_dim))
    both_member = [
        jnp.concatenate([left, right], axis=1).astype(F32).astype(BF16)
        for left, right in zip(block_member, member, strict=True)
    ]
    gamma_lanes = []
    for block in range(blocks):
        gamma = jnp.zeros((1, LANES), F32)
        for part in range(block_heads):
            gamma = jnp.where(member[part], gamma_ref[block * block_heads + part], gamma)
        gamma_lanes.append(gamma * point_scale)
    column = iota((LANES, LANES), 1) % SLOT - slot_rows
    column = jnp.where(column >= block_heads, column - block_heads, column)
    row_head = iota((LANES, LANES), 0) // per_head
    gather_norm = (
        ((iota((LANES, LANES), 0) < slot_rows) & (row_head == column) & in_norm)
        .astype(F32)
        .astype(BF16)
    )
    diagonal = iota((LANES, stacked_rows), 0) // head_dim == (
        iota((LANES, stacked_rows), 1) // residues
    )
    same = iota((residues, stacked_rows), 0) == iota((residues, stacked_rows), 1) % residues
    columns_ref[...] = jnp.zeros_like(columns_ref)

    for copy in small:
        copy.wait()
    kinds = table_ref.shape[0]
    onehot = (iota((kinds, residues), 0) == types_ref[...]).astype(F32).T.astype(BF16)
    conditional = matmul(onehot, table_ref[...])
    empty = as_row(null_ref).astype(F32)

    for frame in range(frames):
        state = x_ref[frame].astype(F32)
        initial = jnp.concatenate([state + conditional, state + empty], axis=0)
        normed = layer_norm(initial, as_row(gain_ref)).astype(BF16)

        columns_ref[0:9, :] = rotation_ref[:, frame, :]
        moved = translation_ref[:, frame, :]
        columns_ref[9:12, :] = moved - jnp.mean(moved, axis=1, keepdims=True)
        columns_ref[12:13, :] = mask_ref[...].astype(F32)
        columns = columns_ref[...].T
        allowed = (columns[:, 12:13] == 1.0) | same
        factors = []
        for step in range(-2, 3):
            factor = jnp.zeros((residues, LANES), F32)
            for row in range(3):
                if 0 <= row + step < 3:
                    entry = 3 * row + row + step
                    factor = jnp.where(component == row, columns[:, entry : entry + 1], factor)
            factors.append(jnp.concatenate([factor] * BRANCHES, axis=0))
        anchor = jnp.zeros((residues, LANES), F32)
        for row in range(3):
            anchor = jnp.where(component == row, columns[:, 9 + row : 10 + row], anchor)
        anchor = jnp.concatenate([anchor] * BRANCHES, axis=0)

        if frame == 0:
            for copy in wide:
                copy.wait()
        points = lax.dot_general(normed, points_ref[...], NT, preferred_element_type=F32)
        projected = matmul(normed, proj_ref[...])

        slots = []
        for pair in range(blocks):
            lanes = points[:, pair * LANES : (pair + 1) * LANES]
            placed = anchor + factors[2] * lanes
            for step in (-2, -1, 1, 2):
                placed = placed + factors[step + 2] * pltpu.roll(lanes, (-step) % LANES, 1)
            swapped = pltpu.roll(placed, SLOT, 1)
            slots += [jnp.where(low, placed, swapped), jnp.where(low, swapped, placed)]

        query_feature, key_first, key_second = [], [], []
        for block in range(blocks):
            feature = jnp.where(in_norm, 1.0, slots[block] * (2.0 * gamma_lanes[block]))
            high = feature.astype(BF16)
            rest = (feature - high.astype(F32)).astype(BF16)
            query_feature.append(jnp.where(low, high, rest))

            feature = slots[blocks + block]
            square = feature * feature
            square_high = square.astype(BF16)
            rest = square - square_high.astype(F32)
            square_middle = rest.astype(BF16)
            square_low = (rest - square_middle.astype(F32)).astype(BF16)
            norm = (
                matmul(square_high, gather_norm)
                + matmul(square_middle, gather_norm)
                + matmul(square_low, gather_norm)
            )
            feature = feature - norm * gamma_lanes[block]
            high = feature.astype(BF16)
            rest = feature - high.astype(F32)
            middle = rest.astype(BF16)
            last = (rest - middle.astype(F32)).astype(BF16)
            key_first.append(jnp.where(in_second, last, high))
            key_second.append(jnp.where(low & ~in_second, middle, jnp.zeros_like(middle)))

        queries = (
            projected[:, :width].astype(BF16) * jnp.asarray(WEIGHT_LOGIT / math.sqrt(head_dim), BF16)
        )
        keys = projected[:, width : 2 * width].astype(BF16)
        values = projected[:, 2 * width :].astype(BF16).astype(F32)
        nothing = jnp.zeros((residues, LANES), BF16)

        contexts = []
        for branch in range(BRANCHES):
            rows = slice(branch * residues, (branch + 1) * residues)
            turned = values[rows].T.astype(BF16)
            pieces = []
            for block in range(blocks):
                lanes = slice(block * LANES, (block + 1) * LANES)
                left = jnp.concatenate(
                    [
                        jnp.concatenate([keys[rows, lanes], key_first[block][rows]], axis=1),
                        jnp.concatenate([nothing, key_second[block][rows]], axis=1),
                    ],
                    axis=0,
                )
                right = jnp.concatenate([queries[rows, lanes], query_feature[block][rows]], axis=1)
                right = jnp.concatenate([right * own for own in both_member], axis=0)
                logits = lax.dot_general(left, right, NT, preferred_element_type=F32)
                attend = softmax_down(logits[:residues] + logits[residues:], allowed)
                mixed = jnp.where(diagonal, matmul(turned[lanes], attend), 0.0)
                folded = mixed[:, :fold]
                for start in range(fold, stacked_rows, fold):
                    folded = folded + mixed[:, start : start + fold]
                pieces.append(folded)
            contexts.append(jnp.concatenate(pieces, axis=0).T.astype(BF16))
        if frame == 0:
            after.wait()
        update = matmul(jnp.concatenate(contexts, axis=0), spatial_out_ref[...])
        for branch in range(BRANCHES):
            total = initial[branch * residues : (branch + 1) * residues]
            for start in range(0, fold, residues):
                first = branch * fold + start
                total = total + update[first : first + residues]
            start = (frame * BRANCHES + branch) * share
            for group in range(groups):
                rows_ref[group, start : start + share, :] = total[group * share : (group + 1) * share]
    out_ref[...] = rows_ref[...].astype(BF16)
    for copy in copies[10 + 2 * blocks :]:
        copy.wait()


def temporal_kernel(
    period,
    x_ref,
    gain_ref,
    proj_ref,
    temporal_out_ref,
    hidden_gain_ref,
    hidden_in_ref,
    hidden_out_ref,
    head_gain_ref,
    head_out_ref,
    out_ref,
):
    groups, depth, width = x_ref.shape
    rows = groups * depth
    head_dim = width // THEADS
    block_heads = LANES // head_dim
    share = period // BRANCHES

    initial = x_ref[...].astype(F32).reshape(rows, width)
    normed = layer_norm(initial, as_row(gain_ref)).astype(BF16)
    projected = matmul(normed, proj_ref[...])
    queries = projected[:, :width].astype(BF16) * jnp.asarray(1.0 / math.sqrt(head_dim), BF16)
    keys = projected[:, width : 2 * width].astype(BF16)
    turned = projected[:, 2 * width :].astype(BF16).astype(F32).T.astype(BF16)
    block_lane = iota((1, LANES), 1)
    allowed = (
        iota((rows, block_heads * rows), 0) % period == iota((rows, block_heads * rows), 1) % period
    )
    pieces = []
    for block in range(width // LANES):
        lanes = slice(block * LANES, (block + 1) * LANES)
        stacked = []
        for part in range(block_heads):
            own = (block_lane >= part * head_dim) & (block_lane < (part + 1) * head_dim)
            stacked.append(queries[:, lanes] * own.astype(F32).astype(BF16))
        logits = lax.dot_general(
            keys[:, lanes], jnp.concatenate(stacked, axis=0), NT, preferred_element_type=F32
        )
        attend = softmax_down(logits, allowed)
        mixed = matmul(turned[lanes], attend)
        for part in range(block_heads):
            pieces.append(
                mixed[part * head_dim : (part + 1) * head_dim, part * rows : (part + 1) * rows]
            )
    context = jnp.concatenate(pieces, axis=0).T.astype(BF16)
    after_time = initial + matmul(context, temporal_out_ref[...])
    second = layer_norm(after_time, as_row(hidden_gain_ref)).astype(BF16)
    hidden = jax.nn.gelu(matmul(second, hidden_in_ref[...])).astype(BF16)
    result = (after_time + matmul(hidden, hidden_out_ref[...])).astype(BF16).astype(F32)
    headed = layer_norm(result, as_row(head_gain_ref)).astype(BF16)
    branch_velocity = matmul(headed, head_out_ref[...]).reshape(rows // period, period, width)
    conditional = branch_velocity[:, :share]
    empty = branch_velocity[:, share:]
    out_ref[...] = (empty + GUIDE * (conditional - empty)).astype(BF16)


def whole(memory_space=pltpu.VMEM):
    return pl.BlockSpec(memory_space=memory_space)


def body(
    groups,
    x_state,
    noise_field,
    rotations,
    translations,
    residue_types,
    pocket_mask,
    type_table,
    null_embed,
    spatial_gain,
    spatial_proj,
    spatial_points,
    spatial_gamma,
    spatial_out,
    temporal_gain,
    temporal_proj,
    temporal_out,
    hidden_gain,
    hidden_in,
    hidden_out,
    head_gain,
    head_out,
):
    frames, residues, width = x_state.shape
    share = residues // groups
    period = BRANCHES * share
    sources = (
        x_state,
        type_table,
        residue_types[None],
        null_embed,
        spatial_gain,
        rotations,
        translations,
        pocket_mask[None],
        spatial_proj,
        spatial_out,
        spatial_points.T,
    )
    slots = 2 * (width // LANES)
    later = (temporal_proj, temporal_out, hidden_in, hidden_out, head_out)
    spatial, *later = pl.pallas_call(
        functools.partial(spatial_kernel, groups),
        out_shape=[pltpu.VMEM((groups, frames * period, width), BF16)]
        + [pltpu.VMEM(array.shape, array.dtype) for array in later],
        in_specs=[whole(pltpu.SMEM)] + [whole(pl.ANY)] * (len(sources) + len(later)),
        out_specs=[whole()] * (1 + len(later)),
        scratch_shapes=[pltpu.VMEM(array.shape, array.dtype) for array in sources[:-1]]
        + [
            pltpu.VMEM((slots * SLOT, width), BF16),
            pltpu.VMEM((16, residues), F32),
            pltpu.VMEM((groups, frames * period, width), F32),
            pltpu.SemaphoreType.DMA((len(sources) - 1 + slots + len(later),)),
        ],
        compiler_params=pltpu.CompilerParams(vmem_limit_bytes=SPATIAL_VMEM),
        name="spatial",
    )(spatial_gamma, *sources, *later)
    arrived = lax.all_to_all(spatial, "seq", split_axis=0, concat_axis=0, tiled=True)
    proj_local, out_local, in_local, hidden_local, head_local = later
    guided = pl.pallas_call(
        functools.partial(temporal_kernel, period),
        out_shape=pltpu.VMEM((groups * frames, share, width), BF16),
        in_specs=[whole()] * 9,
        out_specs=whole(),
        compiler_params=pltpu.CompilerParams(vmem_limit_bytes=TEMPORAL_VMEM),
        name="temporal",
    )(
        arrived,
        temporal_gain,
        proj_local,
        out_local,
        hidden_gain,
        in_local,
        hidden_local,
        head_gain,
        head_local,
    )
    velocity = lax.all_to_all(guided, "seq", split_axis=0, concat_axis=1, tiled=True)
    x_next = (
        x_state.astype(F32)
        + STEP_SIZE * velocity.astype(F32)
        + NOISE_SCALE * noise_field.astype(F32)
    ).astype(BF16)
    return (x_next, velocity)


def solution(mesh):
    tokens = P(("parts", "seq"), None, None)
    geometry = P(None, ("parts", "seq"), None)
    return jax.shard_map(
        functools.partial(body, mesh.shape["seq"]),
        mesh=mesh,
        in_specs=(tokens, tokens, geometry, geometry, P("parts"), P("parts")) + (P(),) * 15,
        out_specs=(tokens, tokens),
        check_vma=False,
    )
```

time: 34.2 us -> 33.1 us (0.968)
  Pallas kernels: 8.66 us -> 7.53 us
    pallas_call x1, Pallas kernels: 6.27 us -> 5.14 us  [body(): pl.pallas_call(functools.partial(spatial_kernel, groups), out_shape=[pltp...]
where the time goes in v5:
time: 33.1 us; the launch traced here: 32.9 us
  blocking collectives  23.9 us (72%)
  Pallas kernels  7.53 us (23%)
  between operations  0.72 us (2%)
  other arithmetic  0.65 us (2%)
    all_to_all x1, blocking collectives, body(): lax.all_to_all(spatial, 'seq', split_axis=0, concat_axis=0, tiled=True)  14.6 us
    all_to_all x1, blocking collectives, body(): lax.all_to_all(guided, 'seq', split_axis=0, concat_axis=1, tiled=True)  9.34 us
    pallas_call x1, Pallas kernels, body(): pl.pallas_call(functools.partial(spatial_kernel, groups), out_shape=[pltp...  5.14 us
    pallas_call x1, Pallas kernels, body(): pl.pallas_call(functools.partial(temporal_kernel, period), out_shape=pltp...  2.39 us

profile of v5, /device:TPU:0, one launch (start us, length us, event | category | flops | bytes accessed | tf_op | source)
XLA Modules:
  0.0 32.9 jit_solution(1844761195166276352)
XLA Ops:
  0.6 0.0 copy-start
  0.6 0.0 copy-start.1
  0.7 0.0 copy-start.2
  0.7 5.1 %spatial.1 = (bf16[16,8,384]{2,1,0:T(8,128)(2,1)S(1)}, bf16[384,1152]{1,0:T(8,128)(2,1)S(1)}, bf16[384,384]{1,0:T(8,128)(2,1)S(1)}, bf16[384,1536]{1,0:T(8,128)(...) custom-call(f32[12]{0:T(128)} %gamma_ref.1, bf16[1,64,384]{2,1,0:T(8,128)(2,1)} %refs_0_.1, ...), custom_call_target="tpu_custom_call" | custom-call | tf_op jit(solution)/shard_map/spatial/pallas_call | solution.py:368
  5.8 14.6 %all_to_all.17.x_ref = bf16[16,8,384]{2,1,0:T(8,128)(2,1)S(1)} all-to-all(bf16[16,8,384]{2,1,0:T(8,128)(2,1)S(1)} %get-tuple-element.8), channel_id=1, replica_groups=mesh['parts'=2,'seq'=16] {'seq'}, dimensions={0} | all-to-all | bytes 196608 | tf_op jit(solution)/shard_map/all_to_all | solution.py:384
  20.4 0.0 copy-done
  20.4 0.0 copy-done.1
  20.4 0.0 copy-done.2
  20.4 0.0 copy-start.3
  20.4 0.0 copy-start.5
  20.4 2.4 %temporal.1 = bf16[16,4,384]{2,1,0:T(4,128)(2,1)S(1)} custom-call(bf16[16,8,384]{2,1,0:T(8,128)(2,1)S(1)} %all_to_all.17.x_ref, f32[384]{0:T(512)S(1)} %copy-done, bf16[384,1152]{1,0:T(8,128)(2,1)S(1)} %get-tuple-element.9.proj_ref, bf16[384,384]{1,0:T(8,128)(2,1)S(1)} %get-tuple-element.10.temporal_out_ref, f32[384]{0:T(512)S(1)} %copy-done.1, ...), custom_call_target="tpu_custom_call" | custom-call | tf_op jit(solution)/shard_map/temporal/pallas_call | solution.py:386
  22.8 9.3 %all_to_all.18 = bf16[16,4,384]{2,1,0:T(4,128)(2,1)S(1)} all-to-all(bf16[16,4,384]{2,1,0:T(4,128)(2,1)S(1)} %temporal.1), channel_id=1, replica_groups=mesh['parts'=2,'seq'=16] {'seq'}, dimensions={0} | all-to-all | bytes 98304 | tf_op jit(solution)/shard_map/all_to_all | solution.py:404
  32.2 0.0 copy-done.3
  32.2 0.0 copy-done.5
  32.2 0.0 copy-start.4
  32.2 0.6 %add_convert_fusion = bf16[1,64,384]{2,1,0:T(8,128)(2,1)} fusion(bf16[1,64,384]{2,1,0:T(8,128)(2,1)S(1)} %copy-done.5, bf16[1,64,384]{2,1,0:T(8,128)(2,1)S(1)} %all_to_all.14, bf16[1,64,384]{2,1,0:T(8,128)(2,1)S(1)} %copy-done.3), kind=kLoop, calls=%fused_computation | loop fusion | flops 196608 | bytes 196608 | tf_op jit(solution)/shard_map/convert_element_type | solution.py:409
  32.9 0.0 copy-done.4
  (1 shorter events, 0.0 us)
Async XLA Ops:
  0.6 19.8 %copy-start = (f32[384]{0:T(512)S(1)}, f32[384]{0:T(512)}, u32[]{:S(2)}) copy-start(f32[384]{0:T(512)} %gain_ref.1) | copy-start | bytes 4612
  0.6 19.8 %copy-start.1 = (f32[384]{0:T(512)S(1)}, f32[384]{0:T(512)}, u32[]{:S(2)}) copy-start(f32[384]{0:T(512)} %hidden_gain_ref.1) | copy-start | bytes 4612
  0.7 19.8 %copy-start.2 = (f32[384]{0:T(512)S(1)}, f32[384]{0:T(512)}, u32[]{:S(2)}) copy-start(f32[384]{0:T(512)} %head_gain_ref.1) | copy-start | bytes 4612
  20.4 11.8 %copy-start.3 = (bf16[1,64,384]{2,1,0:T(8,128)(2,1)S(1)}, bf16[1,64,384]{2,1,0:T(8,128)(2,1)}, u32[]{:S(2)}) copy-start(bf16[1,64,384]{2,1,0:T(8,128)(2,1)} %refs_0_.1) | copy-start | bytes 147460
  20.4 11.8 %copy-start.5 = (bf16[1,64,384]{2,1,0:T(8,128)(2,1)S(1)}, bf16[1,64,384]{2,1,0:T(8,128)(2,1)}, u32[]{:S(2)}) copy-start(bf16[1,64,384]{2,1,0:T(8,128)(2,1)} %param.22) | copy-start | bytes 147460
  32.2 0.7 %copy-start.4 = (bf16[1,64,384]{2,1,0:T(8,128)(2,1)}, bf16[1,64,384]{2,1,0:T(8,128)(2,1)S(1)}, u32[]{:S(2)}) copy-start(bf16[1,64,384]{2,1,0:T(8,128)(2,1)S(1)} %all_to_all.14) | copy-start | bytes 147460

commit v6 on v5

--- a/solution.py
+++ b/solution.py
@@ -10,6 +10,7 @@
 
 THEADS = 6
 BRANCHES = 2
+CORES = 2
 
 WEIGHT_LOGIT = 0.7071067811865476
 WEIGHT_POINT = 0.23570226039551584
@@ -56,7 +57,7 @@
     sources, refs = refs[:11], refs[11:]
     later, refs = refs[:5], refs[5:]
     out_ref, later_out, refs = refs[0], refs[1:6], refs[6:]
-    local, (columns_ref, rows_ref, sems) = refs[:11], refs[11:]
+    local, (columns_ref, sems) = refs[:11], refs[11:]
     (
         x_ref,
         table_ref,
@@ -95,7 +96,8 @@
         pltpu.make_async_copy(source, target, sems.at[index])
         for index, (source, target) in enumerate(pairs)
     ]
-    for copy in copies:
+    first = 10 + 2 * blocks
+    for copy in copies[:first]:
         copy.start()
     small, wide, after = copies[:8], [copies[8]] + copies[10 : 10 + 2 * blocks], copies[9]
 
@@ -150,6 +152,7 @@
     conditional = matmul(onehot, table_ref[...])
     empty = as_row(null_ref).astype(F32)
 
+    tiles = []
     for frame in range(frames):
         state = x_ref[frame].astype(F32)
         initial = jnp.concatenate([state + conditional, state + empty], axis=0)
@@ -177,6 +180,8 @@
         if frame == 0:
             for copy in wide:
                 copy.wait()
+            for copy in copies[first:]:
+                copy.start()
         points = lax.dot_general(normed, points_ref[...], NT, preferred_element_type=F32)
         projected = matmul(normed, proj_ref[...])
 
@@ -249,22 +254,37 @@
         if frame == 0:
             after.wait()
         update = matmul(jnp.concatenate(contexts, axis=0), spatial_out_ref[...])
+        totals = []
         for branch in range(BRANCHES):
             total = initial[branch * residues : (branch + 1) * residues]
             for start in range(0, fold, residues):
-                first = branch * fold + start
-                total = total + update[first : first + residues]
-            start = (frame * BRANCHES + branch) * share
-            for group in range(groups):
-                rows_ref[group, start : start + share, :] = total[group * share : (group + 1) * share]
-    out_ref[...] = rows_ref[...].astype(BF16)
-    for copy in copies[10 + 2 * blocks :]:
+                begin = branch * fold + start
+                total = total + update[begin : begin + residues]
+            totals.append(total)
+        tiles.append(
+            [
+                jnp.concatenate(
+                    [total[group * share : (group + 1) * share] for total in totals], axis=0
+                )
+                for group in range(groups)
+            ]
+        )
+    first_core = lax.axis_index("seq") % CORES == 0
+    for pair in range(groups // CORES):
+        left, right = (
+            jnp.concatenate([tile[CORES * pair + core] for tile in tiles], axis=0)
+            for core in range(CORES)
+        )
+        out_ref[pair, 0] = jnp.where(first_core, left, right).astype(BF16)
+        out_ref[pair, 1] = jnp.where(first_core, right, left).astype(BF16)
+    for copy in copies[first:]:
         copy.wait()
 
 
 def temporal_kernel(
     period,
-    x_ref,
+    own_ref,
+    other_ref,
     gain_ref,
     proj_ref,
     temporal_out_ref,
@@ -275,13 +295,19 @@
     head_out_ref,
     out_ref,
 ):
-    groups, depth, width = x_ref.shape
-    rows = groups * depth
+    pairs, depth, width = other_ref.shape
+    rows = CORES * pairs * depth
     head_dim = width // THEADS
     block_heads = LANES // head_dim
     share = period // BRANCHES
 
-    initial = x_ref[...].astype(F32).reshape(rows, width)
+    initial = jnp.concatenate(
+        [
+            own_ref[:, 0].astype(F32).reshape(rows // CORES, width),
+            other_ref[...].astype(F32).reshape(rows // CORES, width),
+        ],
+        axis=0,
+    )
     normed = layer_norm(initial, as_row(gain_ref)).astype(BF16)
     projected = matmul(normed, proj_ref[...])
     queries = projected[:, :width].astype(BF16) * jnp.asarray(1.0 / math.sqrt(head_dim), BF16)
@@ -316,7 +342,24 @@
     branch_velocity = matmul(headed, head_out_ref[...]).reshape(rows // period, period, width)
     conditional = branch_velocity[:, :share]
     empty = branch_velocity[:, share:]
-    out_ref[...] = (empty + GUIDE * (conditional - empty)).astype(BF16)
+    guided = (empty + GUIDE * (conditional - empty)).astype(BF16)
+    frames = depth // period
+    for core in range(CORES):
+        for pair in range(pairs):
+            for frame in range(frames):
+                out_ref[pair, core, frame * share : (frame + 1) * share, :] = guided[
+                    (core * pairs + pair) * frames + frame
+                ]
+
+
+def exchange(array):
+    count = lax.axis_size("seq")
+    same_core = [list(range(core, count, CORES)) for core in range(CORES)]
+    array = lax.all_to_all(
+        array, "seq", split_axis=0, concat_axis=0, tiled=True, axis_index_groups=same_core
+    )
+    sibling = [(source, source + 1 if source % CORES == 0 else source - 1) for source in range(count)]
+    return array, lax.ppermute(array[:, 1], "seq", sibling)
 
 
 def whole(memory_space=pltpu.VMEM):
@@ -367,7 +410,7 @@
     later = (temporal_proj, temporal_out, hidden_in, hidden_out, head_out)
     spatial, *later = pl.pallas_call(
         functools.partial(spatial_kernel, groups),
-        out_shape=[pltpu.VMEM((groups, frames * period, width), BF16)]
+        out_shape=[pltpu.VMEM((groups // CORES, CORES, frames * period, width), BF16)]
         + [pltpu.VMEM(array.shape, array.dtype) for array in later],
         in_specs=[whole(pltpu.SMEM)] + [whole(pl.ANY)] * (len(sources) + len(later)),
         out_specs=[whole()] * (1 + len(later)),
@@ -375,23 +418,21 @@
         + [
             pltpu.VMEM((slots * SLOT, width), BF16),
             pltpu.VMEM((16, residues), F32),
-            pltpu.VMEM((groups, frames * period, width), F32),
             pltpu.SemaphoreType.DMA((len(sources) - 1 + slots + len(later),)),
         ],
         compiler_params=pltpu.CompilerParams(vmem_limit_bytes=SPATIAL_VMEM),
         name="spatial",
     )(spatial_gamma, *sources, *later)
-    arrived = lax.all_to_all(spatial, "seq", split_axis=0, concat_axis=0, tiled=True)
     proj_local, out_local, in_local, hidden_local, head_local = later
     guided = pl.pallas_call(
         functools.partial(temporal_kernel, period),
-        out_shape=pltpu.VMEM((groups * frames, share, width), BF16),
-        in_specs=[whole()] * 9,
+        out_shape=pltpu.VMEM((groups // CORES, CORES, frames * share, width), BF16),
+        in_specs=[whole()] * 10,
         out_specs=whole(),
         compiler_params=pltpu.CompilerParams(vmem_limit_bytes=TEMPORAL_VMEM),
         name="temporal",
     )(
-        arrived,
+        *exchange(spatial),
         temporal_gain,
         proj_local,
         out_local,
@@ -401,7 +442,15 @@
         head_gain,
         head_local,
     )
-    velocity = lax.all_to_all(guided, "seq", split_axis=0, concat_axis=1, tiled=True)
+    own, other = exchange(guided)
+    own = own[:, 0]
+    first_core = lax.axis_index("seq") % CORES == 0
+    velocity = jnp.stack(
+        [jnp.where(first_core, own, other), jnp.where(first_core, other, own)], axis=1
+    )
+    velocity = jnp.moveaxis(velocity.reshape(groups, frames, share, width), 1, 0).reshape(
+        x_state.shape
+    )
     x_next = (
         x_state.astype(F32)
         + STEP_SIZE * velocity.astype(F32)

time: 33.1 us -> 35.2 us (1.063)
  waiting for transfers between devices: 0 us -> 2.39 us
  blocking collectives: 23.9 us -> 23.4 us
    ppermute x0 -> x2, waiting for transfers between devices: none -> 2.39 us  [exchange(): return (array, lax.ppermute(array[:, 1], 'seq', sibling))]
    all_to_all x2, blocking collectives: 23.9 us -> 23.4 us  [exchange(): lax.all_to_all(array, 'seq', split_axis=0, concat_axis=0, tiled=True, axi...]
  transfers between devices with their start and end apart: 0 -> 2, of which waited for: 0 -> 2; matrix products, arithmetic and copies ran while one was open for 0% -> 0% of each run, Pallas kernels for 0% -> 0%
where the time goes in v6:
time: 35.2 us; the launch traced here: 35 us
  blocking collectives  23.4 us (66%)
  Pallas kernels  7.53 us (21%)
  waiting for transfers between devices  2.39 us (7%)
  between operations  0.78 us (2%)
  other arithmetic  0.71 us (2%)
    all_to_all x2, blocking collectives, exchange(): lax.all_to_all(array, 'seq', split_axis=0, concat_axis=0, tiled=True, axi...  23.4 us
    pallas_call x1, Pallas kernels, body(): pl.pallas_call(functools.partial(spatial_kernel, groups), out_shape=[pltp...  5.13 us
    pallas_call x1, Pallas kernels, body(): pl.pallas_call(functools.partial(temporal_kernel, period), out_shape=pltp...  2.4 us
    ppermute x2, waiting for transfers between devices, exchange(): return (array, lax.ppermute(array[:, 1], 'seq', sibling))  2.39 us
  transfers between devices with their start and end apart: 2, of which 2 were waited for; matrix products, arithmetic and copies ran while one was open for 0% of the time, Pallas kernels for 0%

profile of v6, /device:TPU:0, one launch (start us, length us, event | category | flops | bytes accessed | tf_op | source)
XLA Modules:
  0.0 35.0 jit_solution(14963026273920549064)
XLA Ops:
  0.6 0.0 copy-start
  0.6 0.0 copy-start.1
  0.7 0.0 copy-start.2
  0.7 5.1 %spatial.1 = (bf16[8,2,8,384]{3,2,1,0:T(8,128)(2,1)S(1)}, bf16[384,1152]{1,0:T(8,128)(2,1)S(1)}, bf16[384,384]{1,0:T(8,128)(2,1)S(1)}, bf16[384,1536]{1,0:T(8,12...) custom-call(f32[12]{0:T(128)} %gamma_ref.1, bf16[1,64,384]{2,1,0:T(8,128)(2,1)} %refs_0_.1, ...), custom_call_target="tpu_custom_call" | custom-call | tf_op jit(solution)/shard_map/spatial/pallas_call | solution.py:411
  5.8 14.2 %all_to_all.10.own_ref = bf16[8,2,8,384]{3,2,1,0:T(8,128)(2,1)S(1)} all-to-all(bf16[8,2,8,384]{3,2,1,0:T(8,128)(2,1)S(1)} %get-tuple-element.8), channel_id=1, replica_groups={{0,2,4,6,8,10,12,14},{1,3,5,7,9,11,13,15},{16,18,20,22,24,26,28,30},{17..., dimensions={0} | all-to-all | bytes 196608 | tf_op jit(solution)/shard_map/all_to_all | solution.py:358
  20.0 0.0 collective-permute-start
  20.0 1.2 %collective-permute-done.other_ref = bf16[8,8,384]{2,1,0:T(8,128)(2,1)S(1)} collective-permute-done((bf16[8,8,384]{2,1,0:T(8,128)(2,1)S(1)}, bf16[8,8,384]{2,1,0:T(8,128)(2,1)S(1)}, u32[]{:S(2)}, u32[]{:S(2)}) %collective-permute-start) | collective-permute-done | bytes 49184 | tf_op jit(solution)/shard_map/ppermute | solution.py:362
  21.2 0.0 copy-done
  21.3 0.0 copy-done.1
  21.3 0.0 copy-done.2
  21.3 0.0 copy-start.3
  21.3 0.0 copy-start.5
  21.3 2.4 %temporal.1 = bf16[8,2,4,384]{3,2,1,0:T(4,128)(2,1)S(1)} custom-call(bf16[8,2,8,384]{3,2,1,0:T(8,128)(2,1)S(1)} %all_to_all.10.own_ref, bf16[8,8,384]{2,1,0:T(8,128)(2,1)S(1)} %collective-permute-done.other_ref, f32[384]{0:T(512)S(1)} %copy-done, bf16[384,1152]{1,0:T(8,128)(2,1)S(1)} %get-tuple-element.9.proj_ref, ...), custom_call_target="tpu_custom_call" | custom-call | tf_op jit(solution)/shard_map/temporal/pallas_call | solution.py:427
  23.7 9.2 %all_to_all.11 = bf16[8,2,4,384]{3,2,1,0:T(4,128)(2,1)S(1)} all-to-all(bf16[8,2,4,384]{3,2,1,0:T(4,128)(2,1)S(1)} %temporal.1), channel_id=1, replica_groups={{0,2,4,6,8,10,12,14},{1,3,5,7,9,11,13,15},{16,18,20,22,24,26,28,30},{17..., dimensions={0} | all-to-all | bytes 98304 | tf_op jit(solution)/shard_map/all_to_all | solution.py:358
  32.9 0.1 collective-permute-start.1
  33.0 1.2 %collective-permute-done.1 = bf16[8,4,384]{2,1,0:T(4,128)(2,1)S(1)} collective-permute-done((bf16[8,4,384]{2,1,0:T(4,128)(2,1)S(1)}, bf16[8,4,384]{2,1,0:T(4,128)(2,1)S(1)}, u32[]{:S(2)}, u32[]{:S(2)}) %collective-permute-start.1) | collective-permute-done | bytes 24608 | tf_op jit(solution)/shard_map/ppermute | solution.py:362
  34.3 0.0 copy-done.3
  34.3 0.0 copy-done.5
  34.3 0.0 copy-start.4
  34.3 0.6 %add_convert_fusion = bf16[1,64,384]{2,1,0:T(8,128)(2,1)} fusion(bf16[1,64,384]{2,1,0:T(8,128)(2,1)S(1)} %copy-done.5, bf16[1,64,384]{2,1,0:T(8,128)(2,1)S(1)} %reshape_transpose_reshape.3, bf16[1,64,384]{2,1,0:T(8,128)(2,1)S(1)} %copy-done.3), kind=kLoop, calls=%fused_computation | loop fusion | flops 196608 | bytes 196608 | tf_op jit(solution)/shard_map/convert_element_type | solution.py:458
  35.0 0.0 copy-done.4
  (6 shorter events, 0.1 us)
Async XLA Ops:
  0.6 20.6 %copy-start = (f32[384]{0:T(512)S(1)}, f32[384]{0:T(512)}, u32[]{:S(2)}) copy-start(f32[384]{0:T(512)} %gain_ref.1) | copy-start | bytes 4612
  0.6 20.6 %copy-start.1 = (f32[384]{0:T(512)S(1)}, f32[384]{0:T(512)}, u32[]{:S(2)}) copy-start(f32[384]{0:T(512)} %hidden_gain_ref.1) | copy-start | bytes 4612
  0.7 20.6 %copy-start.2 = (f32[384]{0:T(512)S(1)}, f32[384]{0:T(512)}, u32[]{:S(2)}) copy-start(f32[384]{0:T(512)} %head_gain_ref.1) | copy-start | bytes 4612
  20.0 1.2 %collective-permute-start = (bf16[8,8,384]{2,1,0:T(8,128)(2,1)S(1)}, bf16[8,8,384]{2,1,0:T(8,128)(2,1)S(1)}, u32[]{:S(2)}, u32[]{:S(2)}) collective-permute-start(bf16[8,8,384]{2,1,0:T(8,128)(2,1)S(1)} %slice_bitcast_fusion), channel_id=1, source_target_pairs={{0,1},{1,0},{2,3},{3,2},{4,5},{5,4},{6,7},{7,6},{8,9},{9,8},{10,11... | collective-permute-start | bytes 147464 | tf_op jit(solution)/shard_map/ppermute | solution.py:362
  21.3 13.0 %copy-start.3 = (bf16[1,64,384]{2,1,0:T(8,128)(2,1)S(1)}, bf16[1,64,384]{2,1,0:T(8,128)(2,1)}, u32[]{:S(2)}) copy-start(bf16[1,64,384]{2,1,0:T(8,128)(2,1)} %refs_0_.1) | copy-start | bytes 147460
  21.3 13.0 %copy-start.5 = (bf16[1,64,384]{2,1,0:T(8,128)(2,1)S(1)}, bf16[1,64,384]{2,1,0:T(8,128)(2,1)}, u32[]{:S(2)}) copy-start(bf16[1,64,384]{2,1,0:T(8,128)(2,1)} %param.22) | copy-start | bytes 147460
  32.9 1.3 %collective-permute-start.1 = (bf16[8,4,384]{2,1,0:T(4,128)(2,1)S(1)}, bf16[8,4,384]{2,1,0:T(4,128)(2,1)S(1)}, u32[]{:S(2)}, u32[]{:S(2)}) collective-permute-start(bf16[8,4,384]{2,1,0:T(4,128)(2,1)S(1)} %slice_bitcast_fusion.1), channel_id=1, source_target_pairs={{0,1},{1,0},{2,3},{3,2},{4,5},{5,4},{6,7},{7,6},{8,9},{9,8},{10,11... | collective-permute-start | bytes 73736 | tf_op jit(solution)/shard_map/ppermute | solution.py:362
  34.3 0.7 %copy-start.4 = (bf16[1,64,384]{2,1,0:T(8,128)(2,1)}, bf16[1,64,384]{2,1,0:T(8,128)(2,1)S(1)}, u32[]{:S(2)}) copy-start(bf16[1,64,384]{2,1,0:T(8,128)(2,1)S(1)} %reshape_transpose_reshape.3) | copy-start | bytes 147460

commit v7 on v5

--- a/solution.py
+++ b/solution.py
@@ -49,14 +49,14 @@
 def softmax_down(logits, allowed):
     logits = jnp.where(allowed, logits, -jnp.inf)
     powers = jnp.exp(logits - jnp.max(logits, axis=0, keepdims=True))
-    return (powers * (1.0 / jnp.sum(powers, axis=0, keepdims=True))).astype(BF16)
+    return powers.astype(BF16), 1.0 / jnp.sum(powers, axis=0, keepdims=True)
 
 
 def spatial_kernel(groups, gamma_ref, *refs):
     sources, refs = refs[:11], refs[11:]
     later, refs = refs[:5], refs[5:]
     out_ref, later_out, refs = refs[0], refs[1:6], refs[6:]
-    local, (columns_ref, rows_ref, sems) = refs[:11], refs[11:]
+    local, (columns_ref, sems) = refs[:11], refs[11:]
     (
         x_ref,
         table_ref,
@@ -95,7 +95,8 @@
         pltpu.make_async_copy(source, target, sems.at[index])
         for index, (source, target) in enumerate(pairs)
     ]
-    for copy in copies:
+    first = 10 + 2 * blocks
+    for copy in copies[:first]:
         copy.start()
     small, wide, after = copies[:8], [copies[8]] + copies[10 : 10 + 2 * blocks], copies[9]
 
@@ -107,20 +108,12 @@
     low = lane < SLOT
     place = lane % SLOT
     component = jnp.where(place < slot_rows, place % 3, 3)
-    in_first = (place >= slot_rows) & (place < slot_rows + block_heads)
-    in_second = (place >= slot_rows + block_heads) & (place < slot_rows + 2 * block_heads)
-    in_norm = in_first | in_second
     member, block_member = [], []
     for part in range(block_heads):
-        own = (
-            ((place >= part * per_head) & (place < (part + 1) * per_head))
-            | (place == slot_rows + part)
-            | (place == slot_rows + block_heads + part)
-        )
-        member.append(own)
+        member.append((place >= part * per_head) & (place < (part + 1) * per_head))
         block_member.append((lane >= part * head_dim) & (lane < (part + 1) * head_dim))
     both_member = [
-        jnp.concatenate([left, right], axis=1).astype(F32).astype(BF16)
+        jnp.concatenate([left, right, right], axis=1).astype(F32).astype(BF16)
         for left, right in zip(block_member, member, strict=True)
     ]
     gamma_lanes = []
@@ -129,14 +122,6 @@
         for part in range(block_heads):
             gamma = jnp.where(member[part], gamma_ref[block * block_heads + part], gamma)
         gamma_lanes.append(gamma * point_scale)
-    column = iota((LANES, LANES), 1) % SLOT - slot_rows
-    column = jnp.where(column >= block_heads, column - block_heads, column)
-    row_head = iota((LANES, LANES), 0) // per_head
-    gather_norm = (
-        ((iota((LANES, LANES), 0) < slot_rows) & (row_head == column) & in_norm)
-        .astype(F32)
-        .astype(BF16)
-    )
     diagonal = iota((LANES, stacked_rows), 0) // head_dim == (
         iota((LANES, stacked_rows), 1) // residues
     )
@@ -150,6 +135,7 @@
     conditional = matmul(onehot, table_ref[...])
     empty = as_row(null_ref).astype(F32)
 
+    tiles = []
     for frame in range(frames):
         state = x_ref[frame].astype(F32)
         initial = jnp.concatenate([state + conditional, state + empty], axis=0)
@@ -177,6 +163,8 @@
         if frame == 0:
             for copy in wide:
                 copy.wait()
+            for copy in copies[first:]:
+                copy.start()
         points = lax.dot_general(normed, points_ref[...], NT, preferred_element_type=F32)
         projected = matmul(normed, proj_ref[...])
 
@@ -190,75 +178,83 @@
             slots += [jnp.where(low, placed, swapped), jnp.where(low, swapped, placed)]
 
         query_feature, key_first, key_second = [], [], []
+        nothing = jnp.zeros((BRANCHES * residues, LANES), BF16)
+        ones = jnp.ones((residues, LANES), BF16)
         for block in range(blocks):
-            feature = jnp.where(in_norm, 1.0, slots[block] * (2.0 * gamma_lanes[block]))
+            feature = slots[block] * (2.0 * gamma_lanes[block])
             high = feature.astype(BF16)
             rest = (feature - high.astype(F32)).astype(BF16)
             query_feature.append(jnp.where(low, high, rest))
 
             feature = slots[blocks + block]
-            square = feature * feature
-            square_high = square.astype(BF16)
-            rest = square - square_high.astype(F32)
-            square_middle = rest.astype(BF16)
-            square_low = (rest - square_middle.astype(F32)).astype(BF16)
-            norm = (
-                matmul(square_high, gather_norm)
-                + matmul(square_middle, gather_norm)
-                + matmul(square_low, gather_norm)
-            )
-            feature = feature - norm * gamma_lanes[block]
             high = feature.astype(BF16)
-            rest = feature - high.astype(F32)
+            rest = (feature - high.astype(F32)).astype(BF16)
+            key_first.append([high])
+            key_second.append([jnp.where(low, rest, nothing)])
+            square = feature * feature * (-gamma_lanes[block])
+            high = square.astype(BF16)
+            rest = square - high.astype(F32)
             middle = rest.astype(BF16)
             last = (rest - middle.astype(F32)).astype(BF16)
-            key_first.append(jnp.where(in_second, last, high))
-            key_second.append(jnp.where(low & ~in_second, middle, jnp.zeros_like(middle)))
+            key_first[block].append(jnp.where(low, high, middle))
+            key_second[block].append(jnp.where(low, last, nothing))
 
         queries = (
             projected[:, :width].astype(BF16) * jnp.asarray(WEIGHT_LOGIT / math.sqrt(head_dim), BF16)
         )
         keys = projected[:, width : 2 * width].astype(BF16)
-        values = projected[:, 2 * width :].astype(BF16).astype(F32)
-        nothing = jnp.zeros((residues, LANES), BF16)
-
+        values = projected[:, 2 * width :].astype(BF16)
         contexts = []
         for branch in range(BRANCHES):
             rows = slice(branch * residues, (branch + 1) * residues)
-            turned = values[rows].T.astype(BF16)
+            turned = values[rows].T
             pieces = []
             for block in range(blocks):
                 lanes = slice(block * LANES, (block + 1) * LANES)
                 left = jnp.concatenate(
                     [
-                        jnp.concatenate([keys[rows, lanes], key_first[block][rows]], axis=1),
-                        jnp.concatenate([nothing, key_second[block][rows]], axis=1),
+                        jnp.concatenate(
+                            [piece[rows] for piece in (keys[:, lanes], *key_first[block])], axis=1
+                        ),
+                        jnp.concatenate(
+                            [piece[rows] for piece in (nothing, *key_second[block])], axis=1
+                        ),
                     ],
                     axis=0,
                 )
-                right = jnp.concatenate([queries[rows, lanes], query_feature[block][rows]], axis=1)
+                right = jnp.concatenate(
+                    [queries[rows, lanes], query_feature[block][rows], ones], axis=1
+                )
                 right = jnp.concatenate([right * own for own in both_member], axis=0)
                 logits = lax.dot_general(left, right, NT, preferred_element_type=F32)
-                attend = softmax_down(logits[:residues] + logits[residues:], allowed)
-                mixed = jnp.where(diagonal, matmul(turned[lanes], attend), 0.0)
+                powers, scale = softmax_down(logits[:residues] + logits[residues:], allowed)
+                mixed = jnp.where(diagonal, matmul(turned[lanes], powers) * scale, 0.0)
                 folded = mixed[:, :fold]
                 for start in range(fold, stacked_rows, fold):
                     folded = folded + mixed[:, start : start + fold]
                 pieces.append(folded)
-            contexts.append(jnp.concatenate(pieces, axis=0).T.astype(BF16))
+            contexts.append(jnp.concatenate(pieces, axis=0).astype(BF16).T)
         if frame == 0:
             after.wait()
         update = matmul(jnp.concatenate(contexts, axis=0), spatial_out_ref[...])
+        totals = []
         for branch in range(BRANCHES):
             total = initial[branch * residues : (branch + 1) * residues]
             for start in range(0, fold, residues):
-                first = branch * fold + start
-                total = total + update[first : first + residues]
-            start = (frame * BRANCHES + branch) * share
-            for group in range(groups):
-                rows_ref[group, start : start + share, :] = total[group * share : (group + 1) * share]
-    out_ref[...] = rows_ref[...].astype(BF16)
-    for copy in copies[10 + 2 * blocks :]:
+                begin = branch * fold + start
+                total = total + update[begin : begin + residues]
+            totals.append(total)
+        tiles.append(
+            [
+                jnp.concatenate(
+                    [total[group * share : (group + 1) * share] for total in totals], axis=0
+                )
+                for group in range(groups)
+            ]
+        )
+    for group in range(groups):
+        out_ref[group] = jnp.concatenate([tile[group] for tile in tiles], axis=0).astype(BF16)
+    for copy in copies[first:]:
         copy.wait()
 
 
@@ -286,7 +282,7 @@
     projected = matmul(normed, proj_ref[...])
     queries = projected[:, :width].astype(BF16) * jnp.asarray(1.0 / math.sqrt(head_dim), BF16)
     keys = projected[:, width : 2 * width].astype(BF16)
-    turned = projected[:, 2 * width :].astype(BF16).astype(F32).T.astype(BF16)
+    turned = projected[:, 2 * width :].astype(BF16).T
     block_lane = iota((1, LANES), 1)
     allowed = (
         iota((rows, block_heads * rows), 0) % period == iota((rows, block_heads * rows), 1) % period
@@ -301,13 +297,13 @@
         logits = lax.dot_general(
             keys[:, lanes], jnp.concatenate(stacked, axis=0), NT, preferred_element_type=F32
         )
-        attend = softmax_down(logits, allowed)
-        mixed = matmul(turned[lanes], attend)
+        powers, scale = softmax_down(logits, allowed)
+        mixed = matmul(turned[lanes], powers) * scale
         for part in range(block_heads):
             pieces.append(
                 mixed[part * head_dim : (part + 1) * head_dim, part * rows : (part + 1) * rows]
             )
-    context = jnp.concatenate(pieces, axis=0).T.astype(BF16)
+    context = jnp.concatenate(pieces, axis=0).astype(BF16).T
     after_time = initial + matmul(context, temporal_out_ref[...])
     second = layer_norm(after_time, as_row(hidden_gain_ref)).astype(BF16)
     hidden = jax.nn.gelu(matmul(second, hidden_in_ref[...])).astype(BF16)
@@ -375,7 +371,6 @@
         + [
             pltpu.VMEM((slots * SLOT, width), BF16),
             pltpu.VMEM((16, residues), F32),
-            pltpu.VMEM((groups, frames * period, width), F32),
             pltpu.SemaphoreType.DMA((len(sources) - 1 + slots + len(later),)),
         ],
         compiler_params=pltpu.CompilerParams(vmem_limit_bytes=SPATIAL_VMEM),

time: 33.1 us -> 33 us (level)
  no operation moved by 1% of the time
where the time goes in v7:
time: 33 us; the launch traced here: 32.7 us
  blocking collectives  23.9 us (72%)
  Pallas kernels  7.38 us (22%)
  between operations  0.72 us (2%)
  other arithmetic  0.65 us (2%)
    all_to_all x1, blocking collectives, body(): lax.all_to_all(spatial, 'seq', split_axis=0, concat_axis=0, tiled=True)  14.6 us
    all_to_all x1, blocking collectives, body(): lax.all_to_all(guided, 'seq', split_axis=0, concat_axis=1, tiled=True)  9.34 us
    pallas_call x1, Pallas kernels, body(): pl.pallas_call(functools.partial(spatial_kernel, groups), out_shape=[pltp...  5.05 us
    pallas_call x1, Pallas kernels, body(): pl.pallas_call(functools.partial(temporal_kernel, period), out_shape=pltp...  2.33 us

profile of v7, /device:TPU:0, one launch (start us, length us, event | category | flops | bytes accessed | tf_op | source)
XLA Modules:
  0.0 32.7 jit_solution(3254044958966350325)
XLA Ops:
  0.6 0.0 copy-start
  0.6 0.0 copy-start.1
  0.7 0.0 copy-start.2
  0.7 5.0 %spatial.1 = (bf16[16,8,384]{2,1,0:T(8,128)(2,1)S(1)}, bf16[384,1152]{1,0:T(8,128)(2,1)S(1)}, bf16[384,384]{1,0:T(8,128)(2,1)S(1)}, bf16[384,1536]{1,0:T(8,128)(...) custom-call(f32[12]{0:T(128)} %gamma_ref.1, bf16[1,64,384]{2,1,0:T(8,128)(2,1)} %refs_0_.1, ...), custom_call_target="tpu_custom_call" | custom-call | tf_op jit(solution)/shard_map/spatial/pallas_call | solution.py:364
  5.7 14.6 %all_to_all.17.x_ref = bf16[16,8,384]{2,1,0:T(8,128)(2,1)S(1)} all-to-all(bf16[16,8,384]{2,1,0:T(8,128)(2,1)S(1)} %get-tuple-element.8), channel_id=1, replica_groups=mesh['parts'=2,'seq'=16] {'seq'}, dimensions={0} | all-to-all | bytes 196608 | tf_op jit(solution)/shard_map/all_to_all | solution.py:379
  20.3 0.0 copy-done
  20.3 0.0 copy-done.1
  20.3 0.0 copy-done.2
  20.3 0.0 copy-start.3
  20.3 0.0 copy-start.5
  20.4 2.3 %temporal.1 = bf16[16,4,384]{2,1,0:T(4,128)(2,1)S(1)} custom-call(bf16[16,8,384]{2,1,0:T(8,128)(2,1)S(1)} %all_to_all.17.x_ref, f32[384]{0:T(512)S(1)} %copy-done, bf16[384,1152]{1,0:T(8,128)(2,1)S(1)} %get-tuple-element.9.proj_ref, bf16[384,384]{1,0:T(8,128)(2,1)S(1)} %get-tuple-element.10.temporal_out_ref, f32[384]{0:T(512)S(1)} %copy-done.1, ...), custom_call_target="tpu_custom_call" | custom-call | tf_op jit(solution)/shard_map/temporal/pallas_call | solution.py:381
  22.7 9.3 %all_to_all.18 = bf16[16,4,384]{2,1,0:T(4,128)(2,1)S(1)} all-to-all(bf16[16,4,384]{2,1,0:T(4,128)(2,1)S(1)} %temporal.1), channel_id=1, replica_groups=mesh['parts'=2,'seq'=16] {'seq'}, dimensions={0} | all-to-all | bytes 98304 | tf_op jit(solution)/shard_map/all_to_all | solution.py:399
  32.0 0.0 copy-done.3
  32.1 0.0 copy-done.5
  32.1 0.0 copy-start.4
  32.1 0.6 %add_convert_fusion = bf16[1,64,384]{2,1,0:T(8,128)(2,1)} fusion(bf16[1,64,384]{2,1,0:T(8,128)(2,1)S(1)} %copy-done.5, bf16[1,64,384]{2,1,0:T(8,128)(2,1)S(1)} %all_to_all.14, bf16[1,64,384]{2,1,0:T(8,128)(2,1)S(1)} %copy-done.3), kind=kLoop, calls=%fused_computation | loop fusion | flops 196608 | bytes 196608 | tf_op jit(solution)/shard_map/convert_element_type | solution.py:404
  32.7 0.0 copy-done.4
  (1 shorter events, 0.0 us)
Async XLA Ops:
  0.6 19.7 %copy-start = (f32[384]{0:T(512)S(1)}, f32[384]{0:T(512)}, u32[]{:S(2)}) copy-start(f32[384]{0:T(512)} %gain_ref.1) | copy-start | bytes 4612
  0.6 19.7 %copy-start.1 = (f32[384]{0:T(512)S(1)}, f32[384]{0:T(512)}, u32[]{:S(2)}) copy-start(f32[384]{0:T(512)} %hidden_gain_ref.1) | copy-start | bytes 4612
  0.7 19.7 %copy-start.2 = (f32[384]{0:T(512)S(1)}, f32[384]{0:T(512)}, u32[]{:S(2)}) copy-start(f32[384]{0:T(512)} %head_gain_ref.1) | copy-start | bytes 4612
  20.3 11.7 %copy-start.3 = (bf16[1,64,384]{2,1,0:T(8,128)(2,1)S(1)}, bf16[1,64,384]{2,1,0:T(8,128)(2,1)}, u32[]{:S(2)}) copy-start(bf16[1,64,384]{2,1,0:T(8,128)(2,1)} %refs_0_.1) | copy-start | bytes 147460
  20.3 11.7 %copy-start.5 = (bf16[1,64,384]{2,1,0:T(8,128)(2,1)S(1)}, bf16[1,64,384]{2,1,0:T(8,128)(2,1)}, u32[]{:S(2)}) copy-start(bf16[1,64,384]{2,1,0:T(8,128)(2,1)} %param.22) | copy-start | bytes 147460
  32.1 0.7 %copy-start.4 = (bf16[1,64,384]{2,1,0:T(8,128)(2,1)}, bf16[1,64,384]{2,1,0:T(8,128)(2,1)S(1)}, u32[]{:S(2)}) copy-start(bf16[1,64,384]{2,1,0:T(8,128)(2,1)S(1)} %all_to_all.14) | copy-start | bytes 147460

commit v8 on v7

--- a/solution.py
+++ b/solution.py
@@ -270,6 +270,7 @@
     head_gain_ref,
     head_out_ref,
     out_ref,
+    rows_ref,
 ):
     groups, depth, width = x_ref.shape
     rows = groups * depth
@@ -312,7 +313,52 @@
     branch_velocity = matmul(headed, head_out_ref[...]).reshape(rows // period, period, width)
     conditional = branch_velocity[:, :share]
     empty = branch_velocity[:, share:]
-    out_ref[...] = (empty + GUIDE * (conditional - empty)).astype(BF16)
+    guided = empty + GUIDE * (conditional - empty)
+    frames = depth // period
+    for group in range(groups):
+        for frame in range(frames):
+            rows_ref[group, frame * share : (frame + 1) * share, :] = guided[group * frames + frame]
+    me = lax.axis_index("seq")
+    for group in range(groups):
+        out_ref[group] = rows_ref[me ^ group].astype(BF16)
+
+
+def update_kernel(x_ref, noise_ref, guided_ref, next_ref, velocity_ref, rows_ref):
+    groups = guided_ref.shape[0]
+    frames, residues, _ = x_ref.shape
+    share = residues // groups
+    me = lax.axis_index("seq")
+    even = me % 2 == 0
+    for frame in range(frames):
+        rows = slice(frame * share, (frame + 1) * share)
+        for pair in range(groups // 2):
+            first = guided_ref[2 * pair, rows].astype(F32)
+            second = guided_ref[2 * pair + 1, rows].astype(F32)
+            rows_ref[(me // 2) ^ pair] = jnp.concatenate(
+                [jnp.where(even, first, second), jnp.where(even, second, first)], axis=0
+            )
+        velocity = rows_ref[...].reshape(x_ref.shape[1:])
+        velocity_ref[frame] = velocity.astype(BF16)
+        next_ref[frame] = (
+            x_ref[frame].astype(F32)
+            + STEP_SIZE * velocity
+            + NOISE_SCALE * noise_ref[frame].astype(F32)
+        ).astype(BF16)
+
+
+def exchange(array):
+    count = array.shape[0]
+    stride = count
+    while stride > 1:
+        radix = 4 if stride % 4 == 0 else 2
+        stride //= radix
+        view = array.reshape(count // (radix * stride), radix, stride, *array.shape[1:])
+        parts = [view[:, 0]]
+        for digit in range(1, radix):
+            partners = [(source, source ^ (digit * stride)) for source in range(count)]
+            parts.append(lax.ppermute(view[:, digit], "seq", partners))
+        array = jnp.stack(parts, axis=1).reshape(array.shape)
+    return array
 
 
 def whole(memory_space=pltpu.VMEM):
@@ -380,9 +426,10 @@
     proj_local, out_local, in_local, hidden_local, head_local = later
     guided = pl.pallas_call(
         functools.partial(temporal_kernel, period),
-        out_shape=pltpu.VMEM((groups * frames, share, width), BF16),
+        out_shape=pltpu.VMEM((groups, frames * share, width), BF16),
         in_specs=[whole()] * 9,
         out_specs=whole(),
+        scratch_shapes=[pltpu.VMEM((groups, frames * share, width), F32)],
         compiler_params=pltpu.CompilerParams(vmem_limit_bytes=TEMPORAL_VMEM),
         name="temporal",
     )(
@@ -396,13 +443,17 @@
         head_gain,
         head_local,
     )
-    velocity = lax.all_to_all(guided, "seq", split_axis=0, concat_axis=1, tiled=True)
-    x_next = (
-        x_state.astype(F32)
-        + STEP_SIZE * velocity.astype(F32)
-        + NOISE_SCALE * noise_field.astype(F32)
-    ).astype(BF16)
-    return (x_next, velocity)
+    return tuple(
+        pl.pallas_call(
+            update_kernel,
+            out_shape=[jax.ShapeDtypeStruct(x_state.shape, BF16)] * 2,
+            in_specs=[whole()] * 3,
+            out_specs=[whole()] * 2,
+            scratch_shapes=[pltpu.VMEM((groups // 2, 2 * share, width), F32)],
+            compiler_params=pltpu.CompilerParams(vmem_limit_bytes=TEMPORAL_VMEM),
+            name="update",
+        )(x_state, noise_field, exchange(guided))
+    )
 
 
 def solution(mesh):

time: 33 us -> 33.7 us (1.021)
  blocking collectives: 23.9 us -> 14.6 us
  starting transfers between devices: 0 us -> 6.36 us
  waiting for transfers between devices: 0 us -> 3.58 us
  Pallas kernels: 7.38 us -> 8.07 us
  other arithmetic: 0.65 us -> 0.08 us
    all_to_all x1 -> x0, blocking collectives: 9.34 us -> none  [body(): lax.all_to_all(guided, 'seq', split_axis=0, concat_axis=1, tiled=True)]
    ppermute x0 -> x6, starting transfers between devices: none -> 6.36 us  [exchange(): parts.append(lax.ppermute(view[:, digit], 'seq', partners))]
    ppermute x0 -> x6, waiting for transfers between devices: none -> 3.58 us  [exchange(): parts.append(lax.ppermute(view[:, digit], 'seq', partners))]
    pallas_call x0 -> x1, Pallas kernels: none -> 0.68 us  [body(): pl.pallas_call(update_kernel, out_shape=[jax.ShapeDtypeStruct(x_state.sha...]
    convert_element_type x1 -> x0, other arithmetic: 0.65 us -> none  [body(): x_next = (x_state.astype(F32) + STEP_SIZE * velocity.astype(F32) + NOISE_...]
  transfers between devices with their start and end apart: 0 -> 6, of which waited for: 0 -> 4; matrix products, arithmetic and copies ran while one was open for 0% -> 0% of each run, Pallas kernels for 0% -> 0%
where the time goes in v8:
time: 33.7 us; the launch traced here: 33.5 us
  blocking collectives  14.6 us (43%)
  Pallas kernels  8.07 us (24%)
  starting transfers between devices  6.36 us (19%)
  waiting for transfers between devices  3.58 us (11%)
  between operations  0.76 us (2%)
    all_to_all x1, blocking collectives, body(): lax.all_to_all(spatial, 'seq', split_axis=0, concat_axis=0, tiled=True)  14.6 us
    ppermute x6, starting transfers between devices, exchange(): parts.append(lax.ppermute(view[:, digit], 'seq', partners))  6.36 us
    pallas_call x1, Pallas kernels, body(): pl.pallas_call(functools.partial(spatial_kernel, groups), out_shape=[pltp...  5.05 us
    ppermute x6, waiting for transfers between devices, exchange(): parts.append(lax.ppermute(view[:, digit], 'seq', partners))  3.58 us
    pallas_call x1, Pallas kernels, body(): pl.pallas_call(functools.partial(temporal_kernel, period), out_shape=pltp...  2.34 us
    pallas_call x1, Pallas kernels, body(): pl.pallas_call(update_kernel, out_shape=[jax.ShapeDtypeStruct(x_state.sha...  0.68 us
  transfers between devices with their start and end apart: 6, of which 4 were waited for; matrix products, arithmetic and copies ran while one was open for 0% of the time, Pallas kernels for 0%

profile of v8, /device:TPU:0, one launch (start us, length us, event | category | flops | bytes accessed | tf_op | source)
XLA Modules:
  0.0 33.5 jit_solution(783212052325825775)
XLA Ops:
  0.6 0.0 copy-start.2
  0.6 0.0 copy-start.3
  0.7 0.0 copy-start.4
  0.7 5.0 %spatial.1 = (bf16[16,8,384]{2,1,0:T(8,128)(2,1)S(1)}, bf16[384,1152]{1,0:T(8,128)(2,1)S(1)}, bf16[384,384]{1,0:T(8,128)(2,1)S(1)}, bf16[384,1536]{1,0:T(8,128)(...) custom-call(f32[12]{0:T(128)} %gamma_ref.1, bf16[1,64,384]{2,1,0:T(8,128)(2,1)} %x_ref.1, ...), custom_call_target="tpu_custom_call" | custom-call | tf_op jit(solution)/shard_map/spatial/pallas_call | solution.py:410
  5.7 14.6 %all_to_all.5.x_ref = bf16[16,8,384]{2,1,0:T(8,128)(2,1)S(1)} all-to-all(bf16[16,8,384]{2,1,0:T(8,128)(2,1)S(1)} %get-tuple-element.8), channel_id=1, replica_groups=mesh['parts'=2,'seq'=16] {'seq'}, dimensions={0} | all-to-all | bytes 196608 | tf_op jit(solution)/shard_map/all_to_all | solution.py:425
  20.3 0.0 copy-done.2
  20.3 0.0 copy-done.3
  20.3 0.0 copy-done.4
  20.3 0.0 copy-start
  20.3 0.0 copy-start.1
  20.4 2.3 %temporal.1 = bf16[16,4,384]{2,1,0:T(4,128)(2,1)S(1)} custom-call(bf16[16,8,384]{2,1,0:T(8,128)(2,1)S(1)} %all_to_all.5.x_ref, f32[384]{0:T(512)S(1)} %copy-done.2, bf16[384,1152]{1,0:T(8,128)(2,1)S(1)} %get-tuple-element.9.proj_ref, bf16[384,384]{1,0:T(8,128)(2,1)S(1)} %get-tuple-element.10.temporal_out_ref, f32[384]{0:T(512)S(1)} %copy-done.3, ...), custom_call_target="tpu_custom_call" | custom-call | tf_op jit(solution)/shard_map/temporal/pallas_call | solution.py:427
  22.7 0.7 %collective-permute-start.2 = (bf16[1,4,4,384]{3,2,1,0:T(4,128)(2,1)S(1)}, bf16[1,4,4,384]{3,2,1,0:T(4,128)(2,1)S(1)}, u32[]{:S(2)}, u32[]{:S(2)}) collective-permute-start(bf16[1,4,4,384]{3,2,1,0:T(4,128)(2,1)S(1)} %get-tuple-element.19), channel_id=1, source_target_pairs={{0,12},{1,13},{2,14},{3,15},{4,8},{5,9},{6,10},{7,11},{8,4},{9,5},... | collective-permute-start | bytes 36872 | tf_op jit(solution)/shard_map/ppermute | solution.py:359
  23.4 0.6 %collective-permute-start.1 = (bf16[1,4,4,384]{3,2,1,0:T(4,128)(2,1)S(1)}, bf16[1,4,4,384]{3,2,1,0:T(4,128)(2,1)S(1)}, u32[]{:S(2)}, u32[]{:S(2)}) collective-permute-start(bf16[1,4,4,384]{3,2,1,0:T(4,128)(2,1)S(1)} %get-tuple-element.20), channel_id=1, source_target_pairs={{0,8},{1,9},{2,10},{3,11},{4,12},{5,13},{6,14},{7,15},{8,0},{9,1},... | collective-permute-start | bytes 36872 | tf_op jit(solution)/shard_map/ppermute | solution.py:359
  24.0 3.2 %collective-permute-start = (bf16[1,4,4,384]{3,2,1,0:T(4,128)(2,1)S(1)}, bf16[1,4,4,384]{3,2,1,0:T(4,128)(2,1)S(1)}, u32[]{:S(2)}, u32[]{:S(2)}) collective-permute-start(bf16[1,4,4,384]{3,2,1,0:T(4,128)(2,1)S(1)} %get-tuple-element.21), channel_id=1, source_target_pairs={{0,4},{1,5},{2,6},{3,7},{4,0},{5,1},{6,2},{7,3},{8,12},{9,13},{10,... | collective-permute-start | bytes 36872 | tf_op jit(solution)/shard_map/ppermute | solution.py:359
  27.2 1.1 %collective-permute-done.2 = bf16[1,4,4,384]{3,2,1,0:T(4,128)(2,1)S(1)} collective-permute-done((bf16[1,4,4,384]{3,2,1,0:T(4,128)(2,1)S(1)}, bf16[1,4,4,384]{3,2,1,0:T(4,128)(2,1)S(1)}, u32[]{:S(2)}, u32[]{:S(2)}) %collective-permute-start.2) | collective-permute-done | bytes 12320 | tf_op jit(solution)/shard_map/ppermute | solution.py:359
  28.3 0.0 collective-permute-done.1
  28.3 0.6 %collective-permute-done = bf16[1,4,4,384]{3,2,1,0:T(4,128)(2,1)S(1)} collective-permute-done((bf16[1,4,4,384]{3,2,1,0:T(4,128)(2,1)S(1)}, bf16[1,4,4,384]{3,2,1,0:T(4,128)(2,1)S(1)}, u32[]{:S(2)}, u32[]{:S(2)}) %collective-permute-start) | collective-permute-done | bytes 12320 | tf_op jit(solution)/shard_map/ppermute | solution.py:359
  28.9 0.1 collective-permute-start.5
  29.0 0.1 collective-permute-start.4
  29.1 1.8 %collective-permute-start.3 = (bf16[4,1,4,384]{3,2,0,1:T(4,128)(2,1)S(1)}, bf16[4,1,4,384]{3,2,0,1:T(4,128)(2,1)S(1)}, u32[]{:S(2)}, u32[]{:S(2)}) collective-permute-start(bf16[4,1,4,384]{3,2,0,1:T(4,128)(2,1)S(1)} %get-tuple-element.17), channel_id=1, source_target_pairs={{0,1},{1,0},{2,3},{3,2},{4,5},{5,4},{6,7},{7,6},{8,9},{9,8},{10,11... | collective-permute-start | bytes 36872 | tf_op jit(solution)/shard_map/ppermute | solution.py:359
  30.9 1.3 %collective-permute-done.5 = bf16[4,1,4,384]{3,2,0,1:T(4,128)(2,1)S(1)} collective-permute-done((bf16[4,1,4,384]{3,2,0,1:T(4,128)(2,1)S(1)}, bf16[4,1,4,384]{3,2,0,1:T(4,128)(2,1)S(1)}, u32[]{:S(2)}, u32[]{:S(2)}) %collective-permute-start.5) | collective-permute-done | bytes 12320 | tf_op jit(solution)/shard_map/ppermute | solution.py:359
  32.1 0.7 %collective-permute-done.4 = bf16[4,1,4,384]{3,2,0,1:T(4,128)(2,1)S(1)} collective-permute-done((bf16[4,1,4,384]{3,2,0,1:T(4,128)(2,1)S(1)}, bf16[4,1,4,384]{3,2,0,1:T(4,128)(2,1)S(1)}, u32[]{:S(2)}, u32[]{:S(2)}) %collective-permute-start.4) | collective-permute-done | bytes 12320 | tf_op jit(solution)/shard_map/ppermute | solution.py:359
  32.8 0.0 collective-permute-done.3
  32.8 0.0 copy-done
  32.8 0.0 copy-done.1
  32.8 0.7 %update.1 = (bf16[1,64,384]{2,1,0:T(8,128)(2,1)}, bf16[1,64,384]{2,1,0:T(8,128)(2,1)}) custom-call(bf16[1,64,384]{2,1,0:T(8,128)(2,1)S(1)} %copy-done, bf16[1,64,384]{2,1,0:T(8,128)(2,1)S(1)} %copy-done.1, bf16[16,4,384]{2,1,0:T(4,128)(2,1)S(1)} %bitcast.38), custom_call_target="tpu_custom_call" | custom-call | tf_op jit(solution)/shard_map/update/pallas_call | solution.py:447
  (4 shorter events, 0.1 us)
Async XLA Ops:
  0.6 19.7 %copy-start.2 = (f32[384]{0:T(512)S(1)}, f32[384]{0:T(512)}, u32[]{:S(2)}) copy-start(f32[384]{0:T(512)} %gain_ref.1) | copy-start | bytes 4612
  0.6 19.7 %copy-start.3 = (f32[384]{0:T(512)S(1)}, f32[384]{0:T(512)}, u32[]{:S(2)}) copy-start(f32[384]{0:T(512)} %hidden_gain_ref.1) | copy-start | bytes 4612
  0.7 19.7 %copy-start.4 = (f32[384]{0:T(512)S(1)}, f32[384]{0:T(512)}, u32[]{:S(2)}) copy-start(f32[384]{0:T(512)} %head_gain_ref.1) | copy-start | bytes 4612
  20.3 12.5 %copy-start = (bf16[1,64,384]{2,1,0:T(8,128)(2,1)S(1)}, bf16[1,64,384]{2,1,0:T(8,128)(2,1)}, u32[]{:S(2)}) copy-start(bf16[1,64,384]{2,1,0:T(8,128)(2,1)} %x_ref.1) | copy-start | bytes 147460
  20.3 12.5 %copy-start.1 = (bf16[1,64,384]{2,1,0:T(8,128)(2,1)S(1)}, bf16[1,64,384]{2,1,0:T(8,128)(2,1)}, u32[]{:S(2)}) copy-start(bf16[1,64,384]{2,1,0:T(8,128)(2,1)} %noise_ref.1) | copy-start | bytes 147460
  22.7 5.6 %collective-permute-start.2 = (bf16[1,4,4,384]{3,2,1,0:T(4,128)(2,1)S(1)}, bf16[1,4,4,384]{3,2,1,0:T(4,128)(2,1)S(1)}, u32[]{:S(2)}, u32[]{:S(2)}) collective-permute-start(bf16[1,4,4,384]{3,2,1,0:T(4,128)(2,1)S(1)} %get-tuple-element.19), channel_id=1, source_target_pairs={{0,12},{1,13},{2,14},{3,15},{4,8},{5,9},{6,10},{7,11},{8,4},{9,5},... | collective-permute-start | bytes 36872 | tf_op jit(solution)/shard_map/ppermute | solution.py:359
  23.4 4.9 %collective-permute-start.1 = (bf16[1,4,4,384]{3,2,1,0:T(4,128)(2,1)S(1)}, bf16[1,4,4,384]{3,2,1,0:T(4,128)(2,1)S(1)}, u32[]{:S(2)}, u32[]{:S(2)}) collective-permute-start(bf16[1,4,4,384]{3,2,1,0:T(4,128)(2,1)S(1)} %get-tuple-element.20), channel_id=1, source_target_pairs={{0,8},{1,9},{2,10},{3,11},{4,12},{5,13},{6,14},{7,15},{8,0},{9,1},... | collective-permute-start | bytes 36872 | tf_op jit(solution)/shard_map/ppermute | solution.py:359
  24.0 4.8 %collective-permute-start = (bf16[1,4,4,384]{3,2,1,0:T(4,128)(2,1)S(1)}, bf16[1,4,4,384]{3,2,1,0:T(4,128)(2,1)S(1)}, u32[]{:S(2)}, u32[]{:S(2)}) collective-permute-start(bf16[1,4,4,384]{3,2,1,0:T(4,128)(2,1)S(1)} %get-tuple-element.21), channel_id=1, source_target_pairs={{0,4},{1,5},{2,6},{3,7},{4,0},{5,1},{6,2},{7,3},{8,12},{9,13},{10,... | collective-permute-start | bytes 36872 | tf_op jit(solution)/shard_map/ppermute | solution.py:359
  28.9 3.2 %collective-permute-start.5 = (bf16[4,1,4,384]{3,2,0,1:T(4,128)(2,1)S(1)}, bf16[4,1,4,384]{3,2,0,1:T(4,128)(2,1)S(1)}, u32[]{:S(2)}, u32[]{:S(2)}) collective-permute-start(bf16[4,1,4,384]{3,2,0,1:T(4,128)(2,1)S(1)} %get-tuple-element.15), channel_id=1, source_target_pairs={{0,3},{1,2},{2,1},{3,0},{4,7},{5,6},{6,5},{7,4},{8,11},{9,10},{10,... | collective-permute-start | bytes 36872 | tf_op jit(solution)/shard_map/ppermute | solution.py:359
  29.0 3.8 %collective-permute-start.4 = (bf16[4,1,4,384]{3,2,0,1:T(4,128)(2,1)S(1)}, bf16[4,1,4,384]{3,2,0,1:T(4,128)(2,1)S(1)}, u32[]{:S(2)}, u32[]{:S(2)}) collective-permute-start(bf16[4,1,4,384]{3,2,0,1:T(4,128)(2,1)S(1)} %get-tuple-element.16), channel_id=1, source_target_pairs={{0,2},{1,3},{2,0},{3,1},{4,6},{5,7},{6,4},{7,5},{8,10},{9,11},{10,... | collective-permute-start | bytes 36872 | tf_op jit(solution)/shard_map/ppermute | solution.py:359
  29.1 3.7 %collective-permute-start.3 = (bf16[4,1,4,384]{3,2,0,1:T(4,128)(2,1)S(1)}, bf16[4,1,4,384]{3,2,0,1:T(4,128)(2,1)S(1)}, u32[]{:S(2)}, u32[]{:S(2)}) collective-permute-start(bf16[4,1,4,384]{3,2,0,1:T(4,128)(2,1)S(1)} %get-tuple-element.17), channel_id=1, source_target_pairs={{0,1},{1,0},{2,3},{3,2},{4,5},{5,4},{6,7},{7,6},{8,9},{9,8},{10,11... | collective-permute-start | bytes 36872 | tf_op jit(solution)/shard_map/ppermute | solution.py:359

commit v9 on v7

--- a/solution.py
+++ b/solution.py
@@ -22,6 +22,7 @@
 F32 = jnp.float32
 LANES = 128
 SLOT = 64
+CHUNKS = 4
 SPATIAL_VMEM = 56 * 2**20
 TEMPORAL_VMEM = 40 * 2**20
 NT = (((1,), (1,)), ((), ()))
@@ -82,23 +83,34 @@
     stacked_rows = block_heads * residues
     point_scale = 0.5 * WEIGHT_LOGIT * WEIGHT_POINT
 
-    pairs = list(zip(sources[:10], local[:10], strict=True))
+    proj_source, out_source, points_source = sources[8:]
+    pairs = list(zip(sources[:8], local[:8], strict=True))
     for slot in range(2 * blocks):
         pairs.append(
             (
-                sources[-1].at[pl.ds(slot * slot_rows, slot_rows), :],
+                points_source.at[pl.ds(slot * slot_rows, slot_rows), :],
                 points_ref.at[pl.ds(slot * SLOT, slot_rows), :],
             )
         )
+    rows = width // CHUNKS
+    for chunk in range(CHUNKS):
+        taken = pl.ds(chunk * rows, rows)
+        pairs.append((proj_source.at[taken, :], proj_ref.at[taken, :]))
+    pairs.append((out_source, spatial_out_ref))
+    first = len(pairs)
     pairs += list(zip(later, later_out, strict=True))
     copies = [
         pltpu.make_async_copy(source, target, sems.at[index])
         for index, (source, target) in enumerate(pairs)
     ]
-    first = 10 + 2 * blocks
     for copy in copies[:first]:
         copy.start()
-    small, wide, after = copies[:8], [copies[8]] + copies[10 : 10 + 2 * blocks], copies[9]
+    small, narrow, wide, after = (
+        copies[:8],
+        copies[8 : 8 + 2 * blocks],
+        copies[8 + 2 * blocks : first - 1],
+        copies[first - 1],
+    )
 
     for slot in range(2 * blocks):
         points_ref[slot * SLOT + slot_rows : (slot + 1) * SLOT, :] = jnp.zeros(
@@ -161,12 +173,9 @@
         anchor = jnp.concatenate([anchor] * BRANCHES, axis=0)
 
         if frame == 0:
-            for copy in wide:
+            for copy in narrow:
                 copy.wait()
-            for copy in copies[first:]:
-                copy.start()
         points = lax.dot_general(normed, points_ref[...], NT, preferred_element_type=F32)
-        projected = matmul(normed, proj_ref[...])
 
         slots = []
         for pair in range(blocks):
@@ -199,6 +208,12 @@
             key_first[block].append(jnp.where(low, high, middle))
             key_second[block].append(jnp.where(low, last, nothing))
 
+        if frame == 0:
+            for copy in wide:
+                copy.wait()
+            for copy in copies[first:]:
+                copy.start()
+        projected = matmul(normed, proj_ref[...])
         queries = (
             projected[:, :width].astype(BF16) * jnp.asarray(WEIGHT_LOGIT / math.sqrt(head_dim), BF16)
         )
@@ -371,7 +386,7 @@
         + [
             pltpu.VMEM((slots * SLOT, width), BF16),
             pltpu.VMEM((16, residues), F32),
-            pltpu.SemaphoreType.DMA((len(sources) - 1 + slots + len(later),)),
+            pltpu.SemaphoreType.DMA((len(sources) - 2 + slots + CHUNKS + len(later),)),
         ],
         compiler_params=pltpu.CompilerParams(vmem_limit_bytes=SPATIAL_VMEM),
         name="spatial",

time: 33 us -> 33.4 us (1.012)
  Pallas kernels: 7.38 us -> 7.77 us
    pallas_call x1, Pallas kernels: 5.05 us -> 5.44 us  [body(): pl.pallas_call(functools.partial(spatial_kernel, groups), out_shape=[pltp...]
where the time goes in v9:
time: 33.4 us; the launch traced here: 33.1 us
  blocking collectives  23.9 us (72%)
  Pallas kernels  7.77 us (23%)
  between operations  0.72 us (2%)
  other arithmetic  0.65 us (2%)
    all_to_all x1, blocking collectives, body(): lax.all_to_all(spatial, 'seq', split_axis=0, concat_axis=0, tiled=True)  14.6 us
    all_to_all x1, blocking collectives, body(): lax.all_to_all(guided, 'seq', split_axis=0, concat_axis=1, tiled=True)  9.34 us
    pallas_call x1, Pallas kernels, body(): pl.pallas_call(functools.partial(spatial_kernel, groups), out_shape=[pltp...  5.44 us
    pallas_call x1, Pallas kernels, body(): pl.pallas_call(functools.partial(temporal_kernel, period), out_shape=pltp...  2.33 us

profile of v9, /device:TPU:0, one launch (start us, length us, event | category | flops | bytes accessed | tf_op | source)
XLA Modules:
  0.0 33.1 jit_solution(9328259616557154965)
XLA Ops:
  0.6 0.0 copy-start
  0.6 0.0 copy-start.1
  0.7 0.0 copy-start.2
  0.7 5.4 %spatial.1 = (bf16[16,8,384]{2,1,0:T(8,128)(2,1)S(1)}, bf16[384,1152]{1,0:T(8,128)(2,1)S(1)}, bf16[384,384]{1,0:T(8,128)(2,1)S(1)}, bf16[384,1536]{1,0:T(8,128)(...) custom-call(f32[12]{0:T(128)} %gamma_ref.1, bf16[1,64,384]{2,1,0:T(8,128)(2,1)} %refs_0_.1, ...), custom_call_target="tpu_custom_call" | custom-call | tf_op jit(solution)/shard_map/spatial/pallas_call | solution.py:379
  6.1 14.6 %all_to_all.17.x_ref = bf16[16,8,384]{2,1,0:T(8,128)(2,1)S(1)} all-to-all(bf16[16,8,384]{2,1,0:T(8,128)(2,1)S(1)} %get-tuple-element.8), channel_id=1, replica_groups=mesh['parts'=2,'seq'=16] {'seq'}, dimensions={0} | all-to-all | bytes 196608 | tf_op jit(solution)/shard_map/all_to_all | solution.py:394
  20.7 0.0 copy-done
  20.7 0.0 copy-done.1
  20.7 0.0 copy-done.2
  20.7 0.0 copy-start.3
  20.7 0.0 copy-start.5
  20.8 2.3 %temporal.1 = bf16[16,4,384]{2,1,0:T(4,128)(2,1)S(1)} custom-call(bf16[16,8,384]{2,1,0:T(8,128)(2,1)S(1)} %all_to_all.17.x_ref, f32[384]{0:T(512)S(1)} %copy-done, bf16[384,1152]{1,0:T(8,128)(2,1)S(1)} %get-tuple-element.9.proj_ref, bf16[384,384]{1,0:T(8,128)(2,1)S(1)} %get-tuple-element.10.temporal_out_ref, f32[384]{0:T(512)S(1)} %copy-done.1, ...), custom_call_target="tpu_custom_call" | custom-call | tf_op jit(solution)/shard_map/temporal/pallas_call | solution.py:396
  23.1 9.3 %all_to_all.18 = bf16[16,4,384]{2,1,0:T(4,128)(2,1)S(1)} all-to-all(bf16[16,4,384]{2,1,0:T(4,128)(2,1)S(1)} %temporal.1), channel_id=1, replica_groups=mesh['parts'=2,'seq'=16] {'seq'}, dimensions={0} | all-to-all | bytes 98304 | tf_op jit(solution)/shard_map/all_to_all | solution.py:414
  32.4 0.0 copy-done.3
  32.5 0.0 copy-done.5
  32.5 0.0 copy-start.4
  32.5 0.6 %add_convert_fusion = bf16[1,64,384]{2,1,0:T(8,128)(2,1)} fusion(bf16[1,64,384]{2,1,0:T(8,128)(2,1)S(1)} %copy-done.5, bf16[1,64,384]{2,1,0:T(8,128)(2,1)S(1)} %all_to_all.14, bf16[1,64,384]{2,1,0:T(8,128)(2,1)S(1)} %copy-done.3), kind=kLoop, calls=%fused_computation | loop fusion | flops 196608 | bytes 196608 | tf_op jit(solution)/shard_map/convert_element_type | solution.py:419
  33.1 0.0 copy-done.4
  (1 shorter events, 0.0 us)
Async XLA Ops:
  0.6 20.1 %copy-start = (f32[384]{0:T(512)S(1)}, f32[384]{0:T(512)}, u32[]{:S(2)}) copy-start(f32[384]{0:T(512)} %gain_ref.1) | copy-start | bytes 4612
  0.6 20.1 %copy-start.1 = (f32[384]{0:T(512)S(1)}, f32[384]{0:T(512)}, u32[]{:S(2)}) copy-start(f32[384]{0:T(512)} %hidden_gain_ref.1) | copy-start | bytes 4612
  0.7 20.1 %copy-start.2 = (f32[384]{0:T(512)S(1)}, f32[384]{0:T(512)}, u32[]{:S(2)}) copy-start(f32[384]{0:T(512)} %head_gain_ref.1) | copy-start | bytes 4612
  20.7 11.7 %copy-start.3 = (bf16[1,64,384]{2,1,0:T(8,128)(2,1)S(1)}, bf16[1,64,384]{2,1,0:T(8,128)(2,1)}, u32[]{:S(2)}) copy-start(bf16[1,64,384]{2,1,0:T(8,128)(2,1)} %refs_0_.1) | copy-start | bytes 147460
  20.7 11.7 %copy-start.5 = (bf16[1,64,384]{2,1,0:T(8,128)(2,1)S(1)}, bf16[1,64,384]{2,1,0:T(8,128)(2,1)}, u32[]{:S(2)}) copy-start(bf16[1,64,384]{2,1,0:T(8,128)(2,1)} %param.22) | copy-start | bytes 147460
  32.5 0.7 %copy-start.4 = (bf16[1,64,384]{2,1,0:T(8,128)(2,1)}, bf16[1,64,384]{2,1,0:T(8,128)(2,1)S(1)}, u32[]{:S(2)}) copy-start(bf16[1,64,384]{2,1,0:T(8,128)(2,1)S(1)} %all_to_all.14) | copy-start | bytes 147460

commit v10 on v7

--- a/solution.py
+++ b/solution.py
@@ -98,7 +98,7 @@
     first = 10 + 2 * blocks
     for copy in copies[:first]:
         copy.start()
-    small, wide, after = copies[:8], [copies[8]] + copies[10 : 10 + 2 * blocks], copies[9]
+    small, wide = copies[:8], copies[8:first]
 
     for slot in range(2 * blocks):
         points_ref[slot * SLOT + slot_rows : (slot + 1) * SLOT, :] = jnp.zeros(
@@ -204,11 +204,10 @@
         )
         keys = projected[:, width : 2 * width].astype(BF16)
         values = projected[:, 2 * width :].astype(BF16)
-        contexts = []
+        turned, logits = [], []
         for branch in range(BRANCHES):
             rows = slice(branch * residues, (branch + 1) * residues)
-            turned = values[rows].T
-            pieces = []
+            turned.append(values[rows].T)
             for block in range(blocks):
                 lanes = slice(block * LANES, (block + 1) * LANES)
                 left = jnp.concatenate(
@@ -226,16 +225,24 @@
                     [queries[rows, lanes], query_feature[block][rows], ones], axis=1
                 )
                 right = jnp.concatenate([right * own for own in both_member], axis=0)
-                logits = lax.dot_general(left, right, NT, preferred_element_type=F32)
-                powers, scale = softmax_down(logits[:residues] + logits[residues:], allowed)
-                mixed = jnp.where(diagonal, matmul(turned[lanes], powers) * scale, 0.0)
+                both = lax.dot_general(left, right, NT, preferred_element_type=F32)
+                logits.append(both[:residues] + both[residues:])
+        attends = [softmax_down(each, allowed) for each in logits]
+        mixes = [
+            matmul(turned[index // blocks][index % blocks * LANES :][:LANES], powers)
+            for index, (powers, _) in enumerate(attends)
+        ]
+        contexts = []
+        for branch in range(BRANCHES):
+            pieces = []
+            for block in range(blocks):
+                index = branch * blocks + block
+                mixed = jnp.where(diagonal, mixes[index] * attends[index][1], 0.0)
                 folded = mixed[:, :fold]
                 for start in range(fold, stacked_rows, fold):
                     folded = folded + mixed[:, start : start + fold]
                 pieces.append(folded)
             contexts.append(jnp.concatenate(pieces, axis=0).astype(BF16).T)
-        if frame == 0:
-            after.wait()
         update = matmul(jnp.concatenate(contexts, axis=0), spatial_out_ref[...])
         totals = []
         for branch in range(BRANCHES):
@@ -287,22 +294,28 @@
     allowed = (
         iota((rows, block_heads * rows), 0) % period == iota((rows, block_heads * rows), 1) % period
     )
-    pieces = []
+    logits = []
     for block in range(width // LANES):
         lanes = slice(block * LANES, (block + 1) * LANES)
         stacked = []
         for part in range(block_heads):
             own = (block_lane >= part * head_dim) & (block_lane < (part + 1) * head_dim)
             stacked.append(queries[:, lanes] * own.astype(F32).astype(BF16))
-        logits = lax.dot_general(
-            keys[:, lanes], jnp.concatenate(stacked, axis=0), NT, preferred_element_type=F32
+        logits.append(
+            lax.dot_general(
+                keys[:, lanes], jnp.concatenate(stacked, axis=0), NT, preferred_element_type=F32
+            )
         )
-        powers, scale = softmax_down(logits, allowed)
-        mixed = matmul(turned[lanes], powers) * scale
+    attends = [softmax_down(each, allowed) for each in logits]
+    mixes = [
+        matmul(turned[block * LANES : (block + 1) * LANES], powers)
+        for block, (powers, _) in enumerate(attends)
+    ]
+    pieces = []
+    for mixed, (_, scale) in zip(mixes, attends, strict=True):
         for part in range(block_heads):
-            pieces.append(
-                mixed[part * head_dim : (part + 1) * head_dim, part * rows : (part + 1) * rows]
-            )
+            lanes = slice(part * rows, (part + 1) * rows)
+            pieces.append(mixed[part * head_dim : (part + 1) * head_dim, lanes] * scale[:, lanes])
     context = jnp.concatenate(pieces, axis=0).astype(BF16).T
     after_time = initial + matmul(context, temporal_out_ref[...])
     second = layer_norm(after_time, as_row(hidden_gain_ref)).astype(BF16)

time: 33 us -> 32.4 us (0.982)
  Pallas kernels: 7.38 us -> 6.8 us
    pallas_call x1, Pallas kernels: 5.05 us -> 4.61 us  [body(): pl.pallas_call(functools.partial(spatial_kernel, groups), out_shape=[pltp...]
where the time goes in v10:
time: 32.4 us; the launch traced here: 32.2 us
  blocking collectives  23.9 us (74%)
  Pallas kernels  6.8 us (21%)
  between operations  0.72 us (2%)
  other arithmetic  0.65 us (2%)
    all_to_all x1, blocking collectives, body(): lax.all_to_all(spatial, 'seq', split_axis=0, concat_axis=0, tiled=True)  14.6 us
    all_to_all x1, blocking collectives, body(): lax.all_to_all(guided, 'seq', split_axis=0, concat_axis=1, tiled=True)  9.34 us
    pallas_call x1, Pallas kernels, body(): pl.pallas_call(functools.partial(spatial_kernel, groups), out_shape=[pltp...  4.61 us
    pallas_call x1, Pallas kernels, body(): pl.pallas_call(functools.partial(temporal_kernel, period), out_shape=pltp...  2.19 us
    convert_element_type x1, other arithmetic, body(): x_next = (x_state.astype(F32) + STEP_SIZE * velocity.astype(F32) + NOISE_...  0.65 us

profile of v10, /device:TPU:0, one launch (start us, length us, event | category | flops | bytes accessed | tf_op | source)
XLA Modules:
  0.0 32.2 jit_solution(10274235918975956616)
XLA Ops:
  0.6 0.0 copy-start
  0.6 0.0 copy-start.1
  0.7 0.0 copy-start.2
  0.7 4.6 %spatial.1 = (bf16[16,8,384]{2,1,0:T(8,128)(2,1)S(1)}, bf16[384,1152]{1,0:T(8,128)(2,1)S(1)}, bf16[384,384]{1,0:T(8,128)(2,1)S(1)}, bf16[384,1536]{1,0:T(8,128)(...) custom-call(f32[12]{0:T(128)} %gamma_ref.1, bf16[1,64,384]{2,1,0:T(8,128)(2,1)} %refs_0_.1, ...), custom_call_target="tpu_custom_call" | custom-call | tf_op jit(solution)/shard_map/spatial/pallas_call | solution.py:377
  5.3 14.6 %all_to_all.17.x_ref = bf16[16,8,384]{2,1,0:T(8,128)(2,1)S(1)} all-to-all(bf16[16,8,384]{2,1,0:T(8,128)(2,1)S(1)} %get-tuple-element.8), channel_id=1, replica_groups=mesh['parts'=2,'seq'=16] {'seq'}, dimensions={0} | all-to-all | bytes 196608 | tf_op jit(solution)/shard_map/all_to_all | solution.py:392
  19.9 0.0 copy-done
  19.9 0.0 copy-done.1
  19.9 0.0 copy-done.2
  19.9 0.0 copy-start.3
  19.9 0.0 copy-start.5
  19.9 2.2 %temporal.1 = bf16[16,4,384]{2,1,0:T(4,128)(2,1)S(1)} custom-call(bf16[16,8,384]{2,1,0:T(8,128)(2,1)S(1)} %all_to_all.17.x_ref, f32[384]{0:T(512)S(1)} %copy-done, bf16[384,1152]{1,0:T(8,128)(2,1)S(1)} %get-tuple-element.9.proj_ref, bf16[384,384]{1,0:T(8,128)(2,1)S(1)} %get-tuple-element.10.temporal_out_ref, f32[384]{0:T(512)S(1)} %copy-done.1, ...), custom_call_target="tpu_custom_call" | custom-call | tf_op jit(solution)/shard_map/temporal/pallas_call | solution.py:394
  22.1 9.3 %all_to_all.18 = bf16[16,4,384]{2,1,0:T(4,128)(2,1)S(1)} all-to-all(bf16[16,4,384]{2,1,0:T(4,128)(2,1)S(1)} %temporal.1), channel_id=1, replica_groups=mesh['parts'=2,'seq'=16] {'seq'}, dimensions={0} | all-to-all | bytes 98304 | tf_op jit(solution)/shard_map/all_to_all | solution.py:412
  31.5 0.0 copy-done.3
  31.5 0.0 copy-done.5
  31.5 0.0 copy-start.4
  31.5 0.6 %add_convert_fusion = bf16[1,64,384]{2,1,0:T(8,128)(2,1)} fusion(bf16[1,64,384]{2,1,0:T(8,128)(2,1)S(1)} %copy-done.5, bf16[1,64,384]{2,1,0:T(8,128)(2,1)S(1)} %all_to_all.14, bf16[1,64,384]{2,1,0:T(8,128)(2,1)S(1)} %copy-done.3), kind=kLoop, calls=%fused_computation | loop fusion | flops 196608 | bytes 196608 | tf_op jit(solution)/shard_map/convert_element_type | solution.py:417
  32.1 0.0 copy-done.4
  (1 shorter events, 0.0 us)
Async XLA Ops:
  0.6 19.2 %copy-start = (f32[384]{0:T(512)S(1)}, f32[384]{0:T(512)}, u32[]{:S(2)}) copy-start(f32[384]{0:T(512)} %gain_ref.1) | copy-start | bytes 4612
  0.6 19.2 %copy-start.1 = (f32[384]{0:T(512)S(1)}, f32[384]{0:T(512)}, u32[]{:S(2)}) copy-start(f32[384]{0:T(512)} %hidden_gain_ref.1) | copy-start | bytes 4612
  0.7 19.2 %copy-start.2 = (f32[384]{0:T(512)S(1)}, f32[384]{0:T(512)}, u32[]{:S(2)}) copy-start(f32[384]{0:T(512)} %head_gain_ref.1) | copy-start | bytes 4612
  19.9 11.6 %copy-start.3 = (bf16[1,64,384]{2,1,0:T(8,128)(2,1)S(1)}, bf16[1,64,384]{2,1,0:T(8,128)(2,1)}, u32[]{:S(2)}) copy-start(bf16[1,64,384]{2,1,0:T(8,128)(2,1)} %refs_0_.1) | copy-start | bytes 147460
  19.9 11.6 %copy-start.5 = (bf16[1,64,384]{2,1,0:T(8,128)(2,1)S(1)}, bf16[1,64,384]{2,1,0:T(8,128)(2,1)}, u32[]{:S(2)}) copy-start(bf16[1,64,384]{2,1,0:T(8,128)(2,1)} %param.22) | copy-start | bytes 147460
  31.5 0.7 %copy-start.4 = (bf16[1,64,384]{2,1,0:T(8,128)(2,1)}, bf16[1,64,384]{2,1,0:T(8,128)(2,1)S(1)}, u32[]{:S(2)}) copy-start(bf16[1,64,384]{2,1,0:T(8,128)(2,1)S(1)} %all_to_all.14) | copy-start | bytes 147460

commit v11 on v10

--- a/solution.py
+++ b/solution.py
@@ -22,6 +22,7 @@
 F32 = jnp.float32
 LANES = 128
 SLOT = 64
+FEED = 512
 SPATIAL_VMEM = 56 * 2**20
 TEMPORAL_VMEM = 40 * 2**20
 NT = (((1,), (1,)), ((), ()))
@@ -122,9 +123,9 @@
         for part in range(block_heads):
             gamma = jnp.where(member[part], gamma_ref[block * block_heads + part], gamma)
         gamma_lanes.append(gamma * point_scale)
-    diagonal = iota((LANES, stacked_rows), 0) // head_dim == (
-        iota((LANES, stacked_rows), 1) // residues
-    )
+    chunks = stacked_rows // fold
+    chunk_rows = LANES // chunks
+    diagonal = iota((chunk_rows, fold), 0) // head_dim == iota((chunk_rows, fold), 1) // residues
     same = iota((residues, stacked_rows), 0) == iota((residues, stacked_rows), 1) % residues
     columns_ref[...] = jnp.zeros_like(columns_ref)
 
@@ -228,33 +229,41 @@
                 both = lax.dot_general(left, right, NT, preferred_element_type=F32)
                 logits.append(both[:residues] + both[residues:])
         attends = [softmax_down(each, allowed) for each in logits]
-        mixes = [
-            matmul(turned[index // blocks][index % blocks * LANES :][:LANES], powers)
-            for index, (powers, _) in enumerate(attends)
-        ]
+        mixes = []
+        for index, (powers, _) in enumerate(attends):
+            block = index % blocks
+            for chunk in range(chunks):
+                start = block * LANES + chunk * chunk_rows
+                mixes.append(
+                    matmul(
+                        turned[index // blocks][start : start + chunk_rows],
+                        powers[:, chunk * fold : (chunk + 1) * fold],
+                    )
+                )
         contexts = []
         for branch in range(BRANCHES):
             pieces = []
-            for block in range(blocks):
-                index = branch * blocks + block
-                mixed = jnp.where(diagonal, mixes[index] * attends[index][1], 0.0)
-                folded = mixed[:, :fold]
-                for start in range(fold, stacked_rows, fold):
-                    folded = folded + mixed[:, start : start + fold]
-                pieces.append(folded)
-            contexts.append(jnp.concatenate(pieces, axis=0).astype(BF16).T)
+            for index in range(branch * blocks, (branch + 1) * blocks):
+                scale = attends[index][1]
+                for chunk in range(chunks):
+                    mixed = mixes[index * chunks + chunk]
+                    mixed = mixed * scale[:, chunk * fold : (chunk + 1) * fold]
+                    pieces.append(jnp.where(diagonal, mixed, 0.0))
+            context = jnp.concatenate(pieces, axis=0).astype(BF16).T
+            joined = context[:residues]
+            for start in range(residues, fold, residues):
+                joined = joined + context[start : start + residues]
+            contexts.append(joined)
         update = matmul(jnp.concatenate(contexts, axis=0), spatial_out_ref[...])
-        totals = []
-        for branch in range(BRANCHES):
-            total = initial[branch * residues : (branch + 1) * residues]
-            for start in range(0, fold, residues):
-                begin = branch * fold + start
-                total = total + update[begin : begin + residues]
-            totals.append(total)
+        total = initial + update
         tiles.append(
             [
                 jnp.concatenate(
-                    [total[group * share : (group + 1) * share] for total in totals], axis=0
+                    [
+                        total[start : start + share]
+                        for start in range(group * share, BRANCHES * residues, residues)
+                    ],
+                    axis=0,
                 )
                 for group in range(groups)
             ]
@@ -307,20 +316,29 @@
             )
         )
     attends = [softmax_down(each, allowed) for each in logits]
-    mixes = [
-        matmul(turned[block * LANES : (block + 1) * LANES], powers)
-        for block, (powers, _) in enumerate(attends)
-    ]
+    mixes = []
+    for block, (powers, _) in enumerate(attends):
+        for part in range(block_heads):
+            start = block * LANES + part * head_dim
+            lanes = slice(part * rows, (part + 1) * rows)
+            mixes.append(matmul(turned[start : start + head_dim], powers[:, lanes]))
     pieces = []
-    for mixed, (_, scale) in zip(mixes, attends, strict=True):
-        for part in range(block_heads):
-            lanes = slice(part * rows, (part + 1) * rows)
-            pieces.append(mixed[part * head_dim : (part + 1) * head_dim, lanes] * scale[:, lanes])
+    for index, mixed in enumerate(mixes):
+        part = index % block_heads
+        pieces.append(mixed * attends[index // block_heads][1][:, part * rows : (part + 1) * rows])
     context = jnp.concatenate(pieces, axis=0).astype(BF16).T
     after_time = initial + matmul(context, temporal_out_ref[...])
     second = layer_norm(after_time, as_row(hidden_gain_ref)).astype(BF16)
-    hidden = jax.nn.gelu(matmul(second, hidden_in_ref[...])).astype(BF16)
-    result = (after_time + matmul(hidden, hidden_out_ref[...])).astype(BF16).astype(F32)
+    feed = hidden_in_ref.shape[1]
+    columns = [slice(start, start + FEED) for start in range(0, feed, FEED)]
+    wide = [matmul(second, hidden_in_ref[:, columns[0]])]
+    result = after_time
+    for index, column in enumerate(columns):
+        if index + 1 < len(columns):
+            wide.append(matmul(second, hidden_in_ref[:, columns[index + 1]]))
+        hidden = jax.nn.gelu(wide[index]).astype(BF16)
+        result = result + matmul(hidden, hidden_out_ref[column, :])
+    result = result.astype(BF16).astype(F32)
     headed = layer_norm(result, as_row(head_gain_ref)).astype(BF16)
     branch_velocity = matmul(headed, head_out_ref[...]).reshape(rows // period, period, width)
     conditional = branch_velocity[:, :share]

time: 32.4 us -> 32.4 us (level)
  no operation moved by 1% of the time
where the time goes in v11:
time: 32.4 us; the launch traced here: 32.2 us
  blocking collectives  23.9 us (74%)
  Pallas kernels  6.82 us (21%)
  between operations  0.72 us (2%)
  other arithmetic  0.65 us (2%)
    all_to_all x1, blocking collectives, body(): lax.all_to_all(spatial, 'seq', split_axis=0, concat_axis=0, tiled=True)  14.6 us
    all_to_all x1, blocking collectives, body(): lax.all_to_all(guided, 'seq', split_axis=0, concat_axis=1, tiled=True)  9.34 us
    pallas_call x1, Pallas kernels, body(): pl.pallas_call(functools.partial(spatial_kernel, groups), out_shape=[pltp...  4.6 us
    pallas_call x1, Pallas kernels, body(): pl.pallas_call(functools.partial(temporal_kernel, period), out_shape=pltp...  2.22 us
    convert_element_type x1, other arithmetic, body(): x_next = (x_state.astype(F32) + STEP_SIZE * velocity.astype(F32) + NOISE_...  0.65 us

profile of v11, /device:TPU:0, one launch (start us, length us, event | category | flops | bytes accessed | tf_op | source)
XLA Modules:
  0.0 32.2 jit_solution(17236188112354165420)
XLA Ops:
  0.6 0.0 copy-start
  0.6 0.0 copy-start.1
  0.7 0.0 copy-start.2
  0.7 4.6 %spatial.1 = (bf16[16,8,384]{2,1,0:T(8,128)(2,1)S(1)}, bf16[384,1152]{1,0:T(8,128)(2,1)S(1)}, bf16[384,384]{1,0:T(8,128)(2,1)S(1)}, bf16[384,1536]{1,0:T(8,128)(...) custom-call(f32[12]{0:T(128)} %gamma_ref.1, bf16[1,64,384]{2,1,0:T(8,128)(2,1)} %refs_0_.1, ...), custom_call_target="tpu_custom_call" | custom-call | tf_op jit(solution)/shard_map/spatial/pallas_call | solution.py:395
  5.3 14.6 %all_to_all.17.x_ref = bf16[16,8,384]{2,1,0:T(8,128)(2,1)S(1)} all-to-all(bf16[16,8,384]{2,1,0:T(8,128)(2,1)S(1)} %get-tuple-element.8), channel_id=1, replica_groups=mesh['parts'=2,'seq'=16] {'seq'}, dimensions={0} | all-to-all | bytes 196608 | tf_op jit(solution)/shard_map/all_to_all | solution.py:410
  19.9 0.0 copy-done
  19.9 0.0 copy-done.1
  19.9 0.0 copy-done.2
  19.9 0.0 copy-start.3
  19.9 0.0 copy-start.5
  19.9 2.2 %temporal.1 = bf16[16,4,384]{2,1,0:T(4,128)(2,1)S(1)} custom-call(bf16[16,8,384]{2,1,0:T(8,128)(2,1)S(1)} %all_to_all.17.x_ref, f32[384]{0:T(512)S(1)} %copy-done, bf16[384,1152]{1,0:T(8,128)(2,1)S(1)} %get-tuple-element.9.proj_ref, bf16[384,384]{1,0:T(8,128)(2,1)S(1)} %get-tuple-element.10.temporal_out_ref, f32[384]{0:T(512)S(1)} %copy-done.1, ...), custom_call_target="tpu_custom_call" | custom-call | tf_op jit(solution)/shard_map/temporal/pallas_call | solution.py:412
  22.1 9.3 %all_to_all.18 = bf16[16,4,384]{2,1,0:T(4,128)(2,1)S(1)} all-to-all(bf16[16,4,384]{2,1,0:T(4,128)(2,1)S(1)} %temporal.1), channel_id=1, replica_groups=mesh['parts'=2,'seq'=16] {'seq'}, dimensions={0} | all-to-all | bytes 98304 | tf_op jit(solution)/shard_map/all_to_all | solution.py:430
  31.5 0.0 copy-done.3
  31.5 0.0 copy-done.5
  31.5 0.0 copy-start.4
  31.5 0.6 %add_convert_fusion = bf16[1,64,384]{2,1,0:T(8,128)(2,1)} fusion(bf16[1,64,384]{2,1,0:T(8,128)(2,1)S(1)} %copy-done.5, bf16[1,64,384]{2,1,0:T(8,128)(2,1)S(1)} %all_to_all.14, bf16[1,64,384]{2,1,0:T(8,128)(2,1)S(1)} %copy-done.3), kind=kLoop, calls=%fused_computation | loop fusion | flops 196608 | bytes 196608 | tf_op jit(solution)/shard_map/convert_element_type | solution.py:435
  32.2 0.0 copy-done.4
  (1 shorter events, 0.0 us)
Async XLA Ops:
  0.6 19.2 %copy-start = (f32[384]{0:T(512)S(1)}, f32[384]{0:T(512)}, u32[]{:S(2)}) copy-start(f32[384]{0:T(512)} %gain_ref.1) | copy-start | bytes 4612
  0.6 19.2 %copy-start.1 = (f32[384]{0:T(512)S(1)}, f32[384]{0:T(512)}, u32[]{:S(2)}) copy-start(f32[384]{0:T(512)} %hidden_gain_ref.1) | copy-start | bytes 4612
  0.7 19.2 %copy-start.2 = (f32[384]{0:T(512)S(1)}, f32[384]{0:T(512)}, u32[]{:S(2)}) copy-start(f32[384]{0:T(512)} %head_gain_ref.1) | copy-start | bytes 4612
  19.9 11.6 %copy-start.3 = (bf16[1,64,384]{2,1,0:T(8,128)(2,1)S(1)}, bf16[1,64,384]{2,1,0:T(8,128)(2,1)}, u32[]{:S(2)}) copy-start(bf16[1,64,384]{2,1,0:T(8,128)(2,1)} %refs_0_.1) | copy-start | bytes 147460
  19.9 11.6 %copy-start.5 = (bf16[1,64,384]{2,1,0:T(8,128)(2,1)S(1)}, bf16[1,64,384]{2,1,0:T(8,128)(2,1)}, u32[]{:S(2)}) copy-start(bf16[1,64,384]{2,1,0:T(8,128)(2,1)} %param.22) | copy-start | bytes 147460
  31.5 0.7 %copy-start.4 = (bf16[1,64,384]{2,1,0:T(8,128)(2,1)}, bf16[1,64,384]{2,1,0:T(8,128)(2,1)S(1)}, u32[]{:S(2)}) copy-start(bf16[1,64,384]{2,1,0:T(8,128)(2,1)S(1)} %all_to_all.14) | copy-start | bytes 147460

commit v12 on v11

--- a/solution.py
+++ b/solution.py
@@ -22,7 +22,6 @@
 F32 = jnp.float32
 LANES = 128
 SLOT = 64
-FEED = 512
 SPATIAL_VMEM = 56 * 2**20
 TEMPORAL_VMEM = 40 * 2**20
 NT = (((1,), (1,)), ((), ()))
@@ -113,9 +112,9 @@
     for part in range(block_heads):
         member.append((place >= part * per_head) & (place < (part + 1) * per_head))
         block_member.append((lane >= part * head_dim) & (lane < (part + 1) * head_dim))
-    both_member = [
-        jnp.concatenate([left, right, right], axis=1).astype(F32).astype(BF16)
-        for left, right in zip(block_member, member, strict=True)
+    head_lanes = [own.astype(F32).astype(BF16) for own in block_member]
+    point_lanes = [
+        jnp.concatenate([own, own], axis=1).astype(F32).astype(BF16) for own in member
     ]
     gamma_lanes = []
     for block in range(blocks):
@@ -169,6 +168,22 @@
         points = lax.dot_general(normed, points_ref[...], NT, preferred_element_type=F32)
         projected = matmul(normed, proj_ref[...])
 
+        queries = (
+            projected[:, :width].astype(BF16) * jnp.asarray(WEIGHT_LOGIT / math.sqrt(head_dim), BF16)
+        )
+        keys = projected[:, width : 2 * width].astype(BF16)
+        values = projected[:, 2 * width :].astype(BF16)
+        turned, scalar = [], []
+        for branch in range(BRANCHES):
+            rows = slice(branch * residues, (branch + 1) * residues)
+            turned.append(values[rows].T)
+            for start in range(0, width, LANES):
+                lanes = slice(start, start + LANES)
+                right = jnp.concatenate([queries[rows, lanes] * own for own in head_lanes], axis=0)
+                scalar.append(
+                    lax.dot_general(keys[rows, lanes], right, NT, preferred_element_type=F32)
+                )
+
         slots = []
         for pair in range(blocks):
             lanes = points[:, pair * LANES : (pair + 1) * LANES]
@@ -200,34 +215,21 @@
             key_first[block].append(jnp.where(low, high, middle))
             key_second[block].append(jnp.where(low, last, nothing))
 
-        queries = (
-            projected[:, :width].astype(BF16) * jnp.asarray(WEIGHT_LOGIT / math.sqrt(head_dim), BF16)
-        )
-        keys = projected[:, width : 2 * width].astype(BF16)
-        values = projected[:, 2 * width :].astype(BF16)
-        turned, logits = [], []
+        logits = []
         for branch in range(BRANCHES):
             rows = slice(branch * residues, (branch + 1) * residues)
-            turned.append(values[rows].T)
             for block in range(blocks):
-                lanes = slice(block * LANES, (block + 1) * LANES)
                 left = jnp.concatenate(
                     [
-                        jnp.concatenate(
-                            [piece[rows] for piece in (keys[:, lanes], *key_first[block])], axis=1
-                        ),
-                        jnp.concatenate(
-                            [piece[rows] for piece in (nothing, *key_second[block])], axis=1
-                        ),
+                        jnp.concatenate([piece[rows] for piece in pieces[block]], axis=1)
+                        for pieces in (key_first, key_second)
                     ],
                     axis=0,
                 )
-                right = jnp.concatenate(
-                    [queries[rows, lanes], query_feature[block][rows], ones], axis=1
-                )
-                right = jnp.concatenate([right * own for own in both_member], axis=0)
+                right = jnp.concatenate([query_feature[block][rows], ones], axis=1)
+                right = jnp.concatenate([right * own for own in point_lanes], axis=0)
                 both = lax.dot_general(left, right, NT, preferred_element_type=F32)
-                logits.append(both[:residues] + both[residues:])
+                logits.append(scalar[len(logits)] + both[:residues] + both[residues:])
         attends = [softmax_down(each, allowed) for each in logits]
         mixes = []
         for index, (powers, _) in enumerate(attends):
@@ -329,16 +331,8 @@
     context = jnp.concatenate(pieces, axis=0).astype(BF16).T
     after_time = initial + matmul(context, temporal_out_ref[...])
     second = layer_norm(after_time, as_row(hidden_gain_ref)).astype(BF16)
-    feed = hidden_in_ref.shape[1]
-    columns = [slice(start, start + FEED) for start in range(0, feed, FEED)]
-    wide = [matmul(second, hidden_in_ref[:, columns[0]])]
-    result = after_time
-    for index, column in enumerate(columns):
-        if index + 1 < len(columns):
-            wide.append(matmul(second, hidden_in_ref[:, columns[index + 1]]))
-        hidden = jax.nn.gelu(wide[index]).astype(BF16)
-        result = result + matmul(hidden, hidden_out_ref[column, :])
-    result = result.astype(BF16).astype(F32)
+    hidden = jax.nn.gelu(matmul(second, hidden_in_ref[...])).astype(BF16)
+    result = (after_time + matmul(hidden, hidden_out_ref[...])).astype(BF16).astype(F32)
     headed = layer_norm(result, as_row(head_gain_ref)).astype(BF16)
     branch_velocity = matmul(headed, head_out_ref[...]).reshape(rows // period, period, width)
     conditional = branch_velocity[:, :share]

time: 32.4 us -> 32.4 us (level)
  no operation moved by 1% of the time
where the time goes in v12:
time: 32.4 us; the launch traced here: 32.1 us
  blocking collectives  23.9 us (74%)
  Pallas kernels  6.76 us (21%)
  between operations  0.72 us (2%)
  other arithmetic  0.65 us (2%)
    all_to_all x1, blocking collectives, body(): lax.all_to_all(spatial, 'seq', split_axis=0, concat_axis=0, tiled=True)  14.6 us
    all_to_all x1, blocking collectives, body(): lax.all_to_all(guided, 'seq', split_axis=0, concat_axis=1, tiled=True)  9.34 us
    pallas_call x1, Pallas kernels, body(): pl.pallas_call(functools.partial(spatial_kernel, groups), out_shape=[pltp...  4.61 us
    pallas_call x1, Pallas kernels, body(): pl.pallas_call(functools.partial(temporal_kernel, period), out_shape=pltp...  2.15 us
    convert_element_type x1, other arithmetic, body(): x_next = (x_state.astype(F32) + STEP_SIZE * velocity.astype(F32) + NOISE_...  0.65 us

profile of v12, /device:TPU:0, one launch (start us, length us, event | category | flops | bytes accessed | tf_op | source)
XLA Modules:
  0.0 32.1 jit_solution(16812139246452176766)
XLA Ops:
  0.6 0.0 copy-start
  0.6 0.0 copy-start.1
  0.7 0.0 copy-start.2
  0.7 4.6 %spatial.1 = (bf16[16,8,384]{2,1,0:T(8,128)(2,1)S(1)}, bf16[384,1152]{1,0:T(8,128)(2,1)S(1)}, bf16[384,384]{1,0:T(8,128)(2,1)S(1)}, bf16[384,1536]{1,0:T(8,128)(...) custom-call(f32[12]{0:T(128)} %gamma_ref.1, bf16[1,64,384]{2,1,0:T(8,128)(2,1)} %refs_0_.1, ...), custom_call_target="tpu_custom_call" | custom-call | tf_op jit(solution)/shard_map/spatial/pallas_call | solution.py:389
  5.3 14.6 %all_to_all.17.x_ref = bf16[16,8,384]{2,1,0:T(8,128)(2,1)S(1)} all-to-all(bf16[16,8,384]{2,1,0:T(8,128)(2,1)S(1)} %get-tuple-element.8), channel_id=1, replica_groups=mesh['parts'=2,'seq'=16] {'seq'}, dimensions={0} | all-to-all | bytes 196608 | tf_op jit(solution)/shard_map/all_to_all | solution.py:404
  19.9 0.0 copy-done
  19.9 0.0 copy-done.1
  19.9 0.0 copy-done.2
  19.9 0.0 copy-start.3
  19.9 0.0 copy-start.5
  19.9 2.1 %temporal.1 = bf16[16,4,384]{2,1,0:T(4,128)(2,1)S(1)} custom-call(bf16[16,8,384]{2,1,0:T(8,128)(2,1)S(1)} %all_to_all.17.x_ref, f32[384]{0:T(512)S(1)} %copy-done, bf16[384,1152]{1,0:T(8,128)(2,1)S(1)} %get-tuple-element.9.proj_ref, bf16[384,384]{1,0:T(8,128)(2,1)S(1)} %get-tuple-element.10.temporal_out_ref, f32[384]{0:T(512)S(1)} %copy-done.1, ...), custom_call_target="tpu_custom_call" | custom-call | tf_op jit(solution)/shard_map/temporal/pallas_call | solution.py:406
  22.1 9.3 %all_to_all.18 = bf16[16,4,384]{2,1,0:T(4,128)(2,1)S(1)} all-to-all(bf16[16,4,384]{2,1,0:T(4,128)(2,1)S(1)} %temporal.1), channel_id=1, replica_groups=mesh['parts'=2,'seq'=16] {'seq'}, dimensions={0} | all-to-all | bytes 98304 | tf_op jit(solution)/shard_map/all_to_all | solution.py:424
  31.4 0.0 copy-done.3
  31.4 0.0 copy-done.5
  31.4 0.0 copy-start.4
  31.5 0.6 %add_convert_fusion = bf16[1,64,384]{2,1,0:T(8,128)(2,1)} fusion(bf16[1,64,384]{2,1,0:T(8,128)(2,1)S(1)} %copy-done.5, bf16[1,64,384]{2,1,0:T(8,128)(2,1)S(1)} %all_to_all.14, bf16[1,64,384]{2,1,0:T(8,128)(2,1)S(1)} %copy-done.3), kind=kLoop, calls=%fused_computation | loop fusion | flops 196608 | bytes 196608 | tf_op jit(solution)/shard_map/convert_element_type | solution.py:429
  32.1 0.0 copy-done.4
  (1 shorter events, 0.0 us)
Async XLA Ops:
  0.6 19.2 %copy-start = (f32[384]{0:T(512)S(1)}, f32[384]{0:T(512)}, u32[]{:S(2)}) copy-start(f32[384]{0:T(512)} %gain_ref.1) | copy-start | bytes 4612
  0.6 19.2 %copy-start.1 = (f32[384]{0:T(512)S(1)}, f32[384]{0:T(512)}, u32[]{:S(2)}) copy-start(f32[384]{0:T(512)} %hidden_gain_ref.1) | copy-start | bytes 4612
  0.7 19.2 %copy-start.2 = (f32[384]{0:T(512)S(1)}, f32[384]{0:T(512)}, u32[]{:S(2)}) copy-start(f32[384]{0:T(512)} %head_gain_ref.1) | copy-start | bytes 4612
  19.9 11.5 %copy-start.3 = (bf16[1,64,384]{2,1,0:T(8,128)(2,1)S(1)}, bf16[1,64,384]{2,1,0:T(8,128)(2,1)}, u32[]{:S(2)}) copy-start(bf16[1,64,384]{2,1,0:T(8,128)(2,1)} %refs_0_.1) | copy-start | bytes 147460
  19.9 11.5 %copy-start.5 = (bf16[1,64,384]{2,1,0:T(8,128)(2,1)S(1)}, bf16[1,64,384]{2,1,0:T(8,128)(2,1)}, u32[]{:S(2)}) copy-start(bf16[1,64,384]{2,1,0:T(8,128)(2,1)} %param.22) | copy-start | bytes 147460
  31.4 0.7 %copy-start.4 = (bf16[1,64,384]{2,1,0:T(8,128)(2,1)}, bf16[1,64,384]{2,1,0:T(8,128)(2,1)S(1)}, u32[]{:S(2)}) copy-start(bf16[1,64,384]{2,1,0:T(8,128)(2,1)S(1)} %all_to_all.14) | copy-start | bytes 147460

commit v13 on v12

--- a/solution.py
+++ b/solution.py
@@ -130,6 +130,8 @@
 
     for copy in small:
         copy.wait()
+    for copy in copies[first:]:
+        copy.start()
     kinds = table_ref.shape[0]
     onehot = (iota((kinds, residues), 0) == types_ref[...]).astype(F32).T.astype(BF16)
     conditional = matmul(onehot, table_ref[...])
@@ -163,8 +165,6 @@
         if frame == 0:
             for copy in wide:
                 copy.wait()
-            for copy in copies[first:]:
-                copy.start()
         points = lax.dot_general(normed, points_ref[...], NT, preferred_element_type=F32)
         projected = matmul(normed, proj_ref[...])
 

time: 32.4 us -> 31.7 us (0.978)
  Pallas kernels: 6.76 us -> 6.08 us
    pallas_call x1, Pallas kernels: 4.61 us -> 3.93 us  [body(): pl.pallas_call(functools.partial(spatial_kernel, groups), out_shape=[pltp...]
where the time goes in v13:
time: 31.7 us; the launch traced here: 31.4 us
  blocking collectives  23.9 us (75%)
  Pallas kernels  6.08 us (19%)
  between operations  0.72 us (2%)
  other arithmetic  0.65 us (2%)
    all_to_all x1, blocking collectives, body(): lax.all_to_all(spatial, 'seq', split_axis=0, concat_axis=0, tiled=True)  14.6 us
    all_to_all x1, blocking collectives, body(): lax.all_to_all(guided, 'seq', split_axis=0, concat_axis=1, tiled=True)  9.34 us
    pallas_call x1, Pallas kernels, body(): pl.pallas_call(functools.partial(spatial_kernel, groups), out_shape=[pltp...  3.93 us
    pallas_call x1, Pallas kernels, body(): pl.pallas_call(functools.partial(temporal_kernel, period), out_shape=pltp...  2.14 us
    convert_element_type x1, other arithmetic, body(): x_next = (x_state.astype(F32) + STEP_SIZE * velocity.astype(F32) + NOISE_...  0.65 us

profile of v13, /device:TPU:0, one launch (start us, length us, event | category | flops | bytes accessed | tf_op | source)
XLA Modules:
  0.0 31.4 jit_solution(2392247289474805508)
XLA Ops:
  0.6 0.0 copy-start
  0.6 0.0 copy-start.1
  0.7 0.0 copy-start.2
  0.7 3.9 %spatial.1 = (bf16[16,8,384]{2,1,0:T(8,128)(2,1)S(1)}, bf16[384,1152]{1,0:T(8,128)(2,1)S(1)}, bf16[384,384]{1,0:T(8,128)(2,1)S(1)}, bf16[384,1536]{1,0:T(8,128)(...) custom-call(f32[12]{0:T(128)} %gamma_ref.1, bf16[1,64,384]{2,1,0:T(8,128)(2,1)} %refs_0_.1, ...), custom_call_target="tpu_custom_call" | custom-call | tf_op jit(solution)/shard_map/spatial/pallas_call | solution.py:389
  4.6 14.6 %all_to_all.17.x_ref = bf16[16,8,384]{2,1,0:T(8,128)(2,1)S(1)} all-to-all(bf16[16,8,384]{2,1,0:T(8,128)(2,1)S(1)} %get-tuple-element.8), channel_id=1, replica_groups=mesh['parts'=2,'seq'=16] {'seq'}, dimensions={0} | all-to-all | bytes 196608 | tf_op jit(solution)/shard_map/all_to_all | solution.py:404
  19.2 0.0 copy-done
  19.2 0.0 copy-done.1
  19.2 0.0 copy-done.2
  19.2 0.0 copy-start.3
  19.2 0.0 copy-start.5
  19.2 2.1 %temporal.1 = bf16[16,4,384]{2,1,0:T(4,128)(2,1)S(1)} custom-call(bf16[16,8,384]{2,1,0:T(8,128)(2,1)S(1)} %all_to_all.17.x_ref, f32[384]{0:T(512)S(1)} %copy-done, bf16[384,1152]{1,0:T(8,128)(2,1)S(1)} %get-tuple-element.9.proj_ref, bf16[384,384]{1,0:T(8,128)(2,1)S(1)} %get-tuple-element.10.temporal_out_ref, f32[384]{0:T(512)S(1)} %copy-done.1, ...), custom_call_target="tpu_custom_call" | custom-call | tf_op jit(solution)/shard_map/temporal/pallas_call | solution.py:406
  21.4 9.3 %all_to_all.18 = bf16[16,4,384]{2,1,0:T(4,128)(2,1)S(1)} all-to-all(bf16[16,4,384]{2,1,0:T(4,128)(2,1)S(1)} %temporal.1), channel_id=1, replica_groups=mesh['parts'=2,'seq'=16] {'seq'}, dimensions={0} | all-to-all | bytes 98304 | tf_op jit(solution)/shard_map/all_to_all | solution.py:424
  30.7 0.0 copy-done.3
  30.8 0.0 copy-done.5
  30.8 0.0 copy-start.4
  30.8 0.6 %add_convert_fusion = bf16[1,64,384]{2,1,0:T(8,128)(2,1)} fusion(bf16[1,64,384]{2,1,0:T(8,128)(2,1)S(1)} %copy-done.5, bf16[1,64,384]{2,1,0:T(8,128)(2,1)S(1)} %all_to_all.14, bf16[1,64,384]{2,1,0:T(8,128)(2,1)S(1)} %copy-done.3), kind=kLoop, calls=%fused_computation | loop fusion | flops 196608 | bytes 196608 | tf_op jit(solution)/shard_map/convert_element_type | solution.py:429
  31.4 0.0 copy-done.4
  (1 shorter events, 0.0 us)
Async XLA Ops:
  0.6 18.6 %copy-start = (f32[384]{0:T(512)S(1)}, f32[384]{0:T(512)}, u32[]{:S(2)}) copy-start(f32[384]{0:T(512)} %gain_ref.1) | copy-start | bytes 4612
  0.6 18.6 %copy-start.1 = (f32[384]{0:T(512)S(1)}, f32[384]{0:T(512)}, u32[]{:S(2)}) copy-start(f32[384]{0:T(512)} %hidden_gain_ref.1) | copy-start | bytes 4612
  0.7 18.6 %copy-start.2 = (f32[384]{0:T(512)S(1)}, f32[384]{0:T(512)}, u32[]{:S(2)}) copy-start(f32[384]{0:T(512)} %head_gain_ref.1) | copy-start | bytes 4612
  19.2 11.5 %copy-start.3 = (bf16[1,64,384]{2,1,0:T(8,128)(2,1)S(1)}, bf16[1,64,384]{2,1,0:T(8,128)(2,1)}, u32[]{:S(2)}) copy-start(bf16[1,64,384]{2,1,0:T(8,128)(2,1)} %refs_0_.1) | copy-start | bytes 147460
  19.2 11.5 %copy-start.5 = (bf16[1,64,384]{2,1,0:T(8,128)(2,1)S(1)}, bf16[1,64,384]{2,1,0:T(8,128)(2,1)}, u32[]{:S(2)}) copy-start(bf16[1,64,384]{2,1,0:T(8,128)(2,1)} %param.22) | copy-start | bytes 147460
  30.8 0.7 %copy-start.4 = (bf16[1,64,384]{2,1,0:T(8,128)(2,1)}, bf16[1,64,384]{2,1,0:T(8,128)(2,1)S(1)}, u32[]{:S(2)}) copy-start(bf16[1,64,384]{2,1,0:T(8,128)(2,1)S(1)} %all_to_all.14) | copy-start | bytes 147460

commit v14 on v13

--- a/solution.py
+++ b/solution.py
@@ -22,6 +22,8 @@
 F32 = jnp.float32
 LANES = 128
 SLOT = 64
+PIECE = 384 * 512
+MOST_PIECES = 16
 SPATIAL_VMEM = 56 * 2**20
 TEMPORAL_VMEM = 40 * 2**20
 NT = (((1,), (1,)), ((), ()))
@@ -90,13 +92,17 @@
                 points_ref.at[pl.ds(slot * SLOT, slot_rows), :],
             )
         )
-    pairs += list(zip(later, later_out, strict=True))
+    for source, target in zip(later, later_out, strict=True):
+        rows = source.shape[0] // max(1, source.shape[0] * source.shape[1] // PIECE)
+        for start in range(0, source.shape[0], rows):
+            taken = pl.ds(start, rows)
+            pairs.append((source.at[taken, :], target.at[taken, :]))
     copies = [
         pltpu.make_async_copy(source, target, sems.at[index])
         for index, (source, target) in enumerate(pairs)
     ]
     first = 10 + 2 * blocks
-    for copy in copies[:first]:
+    for copy in copies:
         copy.start()
     small, wide = copies[:8], copies[8:first]
 
@@ -130,8 +136,6 @@
 
     for copy in small:
         copy.wait()
-    for copy in copies[first:]:
-        copy.start()
     kinds = table_ref.shape[0]
     onehot = (iota((kinds, residues), 0) == types_ref[...]).astype(F32).T.astype(BF16)
     conditional = matmul(onehot, table_ref[...])
@@ -396,7 +400,7 @@
         + [
             pltpu.VMEM((slots * SLOT, width), BF16),
             pltpu.VMEM((16, residues), F32),
-            pltpu.SemaphoreType.DMA((len(sources) - 1 + slots + len(later),)),
+            pltpu.SemaphoreType.DMA((len(sources) - 1 + slots + MOST_PIECES,)),
         ],
         compiler_params=pltpu.CompilerParams(vmem_limit_bytes=SPATIAL_VMEM),
         name="spatial",

time: 31.7 us -> 31.7 us (level)
  no operation moved by 1% of the time
where the time goes in v14:
time: 31.7 us; the launch traced here: 31.5 us
  blocking collectives  23.9 us (75%)
  Pallas kernels  6.14 us (19%)
  between operations  0.72 us (2%)
  other arithmetic  0.65 us (2%)
    all_to_all x1, blocking collectives, body(): lax.all_to_all(spatial, 'seq', split_axis=0, concat_axis=0, tiled=True)  14.6 us
    all_to_all x1, blocking collectives, body(): lax.all_to_all(guided, 'seq', split_axis=0, concat_axis=1, tiled=True)  9.34 us
    pallas_call x1, Pallas kernels, body(): pl.pallas_call(functools.partial(spatial_kernel, groups), out_shape=[pltp...  3.98 us
    pallas_call x1, Pallas kernels, body(): pl.pallas_call(functools.partial(temporal_kernel, period), out_shape=pltp...  2.16 us
    convert_element_type x1, other arithmetic, body(): x_next = (x_state.astype(F32) + STEP_SIZE * velocity.astype(F32) + NOISE_...  0.65 us

profile of v14, /device:TPU:0, one launch (start us, length us, event | category | flops | bytes accessed | tf_op | source)
XLA Modules:
  0.0 31.5 jit_solution(14507156307513326454)
XLA Ops:
  0.6 0.0 copy-start
  0.6 0.0 copy-start.1
  0.7 0.0 copy-start.2
  0.7 4.0 %spatial.1 = (bf16[16,8,384]{2,1,0:T(8,128)(2,1)S(1)}, bf16[384,1152]{1,0:T(8,128)(2,1)S(1)}, bf16[384,384]{1,0:T(8,128)(2,1)S(1)}, bf16[384,1536]{1,0:T(8,128)(...) custom-call(f32[12]{0:T(128)} %gamma_ref.1, bf16[1,64,384]{2,1,0:T(8,128)(2,1)} %refs_0_.1, ...), custom_call_target="tpu_custom_call" | custom-call | tf_op jit(solution)/shard_map/spatial/pallas_call | solution.py:393
  4.7 14.6 %all_to_all.17.x_ref = bf16[16,8,384]{2,1,0:T(8,128)(2,1)S(1)} all-to-all(bf16[16,8,384]{2,1,0:T(8,128)(2,1)S(1)} %get-tuple-element.8), channel_id=1, replica_groups=mesh['parts'=2,'seq'=16] {'seq'}, dimensions={0} | all-to-all | bytes 196608 | tf_op jit(solution)/shard_map/all_to_all | solution.py:408
  19.2 0.0 copy-done
  19.3 0.0 copy-done.1
  19.3 0.0 copy-done.2
  19.3 0.0 copy-start.3
  19.3 0.0 copy-start.5
  19.3 2.2 %temporal.1 = bf16[16,4,384]{2,1,0:T(4,128)(2,1)S(1)} custom-call(bf16[16,8,384]{2,1,0:T(8,128)(2,1)S(1)} %all_to_all.17.x_ref, f32[384]{0:T(512)S(1)} %copy-done, bf16[384,1152]{1,0:T(8,128)(2,1)S(1)} %get-tuple-element.9.proj_ref, bf16[384,384]{1,0:T(8,128)(2,1)S(1)} %get-tuple-element.10.temporal_out_ref, f32[384]{0:T(512)S(1)} %copy-done.1, ...), custom_call_target="tpu_custom_call" | custom-call | tf_op jit(solution)/shard_map/temporal/pallas_call | solution.py:410
  21.4 9.3 %all_to_all.18 = bf16[16,4,384]{2,1,0:T(4,128)(2,1)S(1)} all-to-all(bf16[16,4,384]{2,1,0:T(4,128)(2,1)S(1)} %temporal.1), channel_id=1, replica_groups=mesh['parts'=2,'seq'=16] {'seq'}, dimensions={0} | all-to-all | bytes 98304 | tf_op jit(solution)/shard_map/all_to_all | solution.py:428
  30.8 0.0 copy-done.3
  30.8 0.0 copy-done.5
  30.8 0.0 copy-start.4
  30.8 0.6 %add_convert_fusion = bf16[1,64,384]{2,1,0:T(8,128)(2,1)} fusion(bf16[1,64,384]{2,1,0:T(8,128)(2,1)S(1)} %copy-done.5, bf16[1,64,384]{2,1,0:T(8,128)(2,1)S(1)} %all_to_all.14, bf16[1,64,384]{2,1,0:T(8,128)(2,1)S(1)} %copy-done.3), kind=kLoop, calls=%fused_computation | loop fusion | flops 196608 | bytes 196608 | tf_op jit(solution)/shard_map/convert_element_type | solution.py:433
  31.5 0.0 copy-done.4
  (1 shorter events, 0.0 us)
Async XLA Ops:
  0.6 18.6 %copy-start = (f32[384]{0:T(512)S(1)}, f32[384]{0:T(512)}, u32[]{:S(2)}) copy-start(f32[384]{0:T(512)} %gain_ref.1) | copy-start | bytes 4612
  0.6 18.6 %copy-start.1 = (f32[384]{0:T(512)S(1)}, f32[384]{0:T(512)}, u32[]{:S(2)}) copy-start(f32[384]{0:T(512)} %hidden_gain_ref.1) | copy-start | bytes 4612
  0.7 18.6 %copy-start.2 = (f32[384]{0:T(512)S(1)}, f32[384]{0:T(512)}, u32[]{:S(2)}) copy-start(f32[384]{0:T(512)} %head_gain_ref.1) | copy-start | bytes 4612
  19.3 11.5 %copy-start.3 = (bf16[1,64,384]{2,1,0:T(8,128)(2,1)S(1)}, bf16[1,64,384]{2,1,0:T(8,128)(2,1)}, u32[]{:S(2)}) copy-start(bf16[1,64,384]{2,1,0:T(8,128)(2,1)} %refs_0_.1) | copy-start | bytes 147460
  19.3 11.5 %copy-start.5 = (bf16[1,64,384]{2,1,0:T(8,128)(2,1)S(1)}, bf16[1,64,384]{2,1,0:T(8,128)(2,1)}, u32[]{:S(2)}) copy-start(bf16[1,64,384]{2,1,0:T(8,128)(2,1)} %param.22) | copy-start | bytes 147460
  30.8 0.7 %copy-start.4 = (bf16[1,64,384]{2,1,0:T(8,128)(2,1)}, bf16[1,64,384]{2,1,0:T(8,128)(2,1)S(1)}, u32[]{:S(2)}) copy-start(bf16[1,64,384]{2,1,0:T(8,128)(2,1)S(1)} %all_to_all.14) | copy-start | bytes 147460

commit v15 on v13

--- a/solution.py
+++ b/solution.py
@@ -82,7 +82,7 @@
     stacked_rows = block_heads * residues
     point_scale = 0.5 * WEIGHT_LOGIT * WEIGHT_POINT
 
-    pairs = list(zip(sources[:10], local[:10], strict=True))
+    pairs = list(zip(sources[:8], local[:8], strict=True))
     for slot in range(2 * blocks):
         pairs.append(
             (
@@ -90,7 +90,7 @@
                 points_ref.at[pl.ds(slot * SLOT, slot_rows), :],
             )
         )
-    pairs += list(zip(later, later_out, strict=True))
+    pairs += list(zip(sources[8:10] + later, local[8:10] + tuple(later_out), strict=True))
     copies = [
         pltpu.make_async_copy(source, target, sems.at[index])
         for index, (source, target) in enumerate(pairs)
@@ -98,7 +98,7 @@
     first = 10 + 2 * blocks
     for copy in copies[:first]:
         copy.start()
-    small, wide = copies[:8], copies[8:first]
+    small, wide, after = copies[:8], copies[8 : first - 1], copies[first - 1]
 
     for slot in range(2 * blocks):
         points_ref[slot * SLOT + slot_rows : (slot + 1) * SLOT, :] = jnp.zeros(
@@ -256,6 +256,8 @@
             for start in range(residues, fold, residues):
                 joined = joined + context[start : start + residues]
             contexts.append(joined)
+        if frame == 0:
+            after.wait()
         update = matmul(jnp.concatenate(contexts, axis=0), spatial_out_ref[...])
         total = initial + update
         tiles.append(

time: 31.7 us -> 31.7 us (level)
  no operation moved by 1% of the time
where the time goes in v15:
time: 31.7 us; the launch traced here: 31.4 us
  blocking collectives  23.9 us (75%)
  Pallas kernels  6.09 us (19%)
  between operations  0.72 us (2%)
  other arithmetic  0.65 us (2%)
    all_to_all x1, blocking collectives, body(): lax.all_to_all(spatial, 'seq', split_axis=0, concat_axis=0, tiled=True)  14.6 us
    all_to_all x1, blocking collectives, body(): lax.all_to_all(guided, 'seq', split_axis=0, concat_axis=1, tiled=True)  9.34 us
    pallas_call x1, Pallas kernels, body(): pl.pallas_call(functools.partial(spatial_kernel, groups), out_shape=[pltp...  3.94 us
    pallas_call x1, Pallas kernels, body(): pl.pallas_call(functools.partial(temporal_kernel, period), out_shape=pltp...  2.15 us
    convert_element_type x1, other arithmetic, body(): x_next = (x_state.astype(F32) + STEP_SIZE * velocity.astype(F32) + NOISE_...  0.65 us

profile of v15, /device:TPU:0, one launch (start us, length us, event | category | flops | bytes accessed | tf_op | source)
XLA Modules:
  0.0 31.4 jit_solution(4940489420832551628)
XLA Ops:
  0.6 0.0 copy-start
  0.6 0.0 copy-start.1
  0.7 0.0 copy-start.2
  0.7 3.9 %spatial.1 = (bf16[16,8,384]{2,1,0:T(8,128)(2,1)S(1)}, bf16[384,1152]{1,0:T(8,128)(2,1)S(1)}, bf16[384,384]{1,0:T(8,128)(2,1)S(1)}, bf16[384,1536]{1,0:T(8,128)(...) custom-call(f32[12]{0:T(128)} %gamma_ref.1, bf16[1,64,384]{2,1,0:T(8,128)(2,1)} %refs_0_.1, ...), custom_call_target="tpu_custom_call" | custom-call | tf_op jit(solution)/shard_map/spatial/pallas_call | solution.py:391
  4.6 14.6 %all_to_all.17.x_ref = bf16[16,8,384]{2,1,0:T(8,128)(2,1)S(1)} all-to-all(bf16[16,8,384]{2,1,0:T(8,128)(2,1)S(1)} %get-tuple-element.8), channel_id=1, replica_groups=mesh['parts'=2,'seq'=16] {'seq'}, dimensions={0} | all-to-all | bytes 196608 | tf_op jit(solution)/shard_map/all_to_all | solution.py:406
  19.2 0.0 copy-done
  19.2 0.0 copy-done.1
  19.2 0.0 copy-done.2
  19.2 0.0 copy-start.3
  19.2 0.0 copy-start.5
  19.2 2.2 %temporal.1 = bf16[16,4,384]{2,1,0:T(4,128)(2,1)S(1)} custom-call(bf16[16,8,384]{2,1,0:T(8,128)(2,1)S(1)} %all_to_all.17.x_ref, f32[384]{0:T(512)S(1)} %copy-done, bf16[384,1152]{1,0:T(8,128)(2,1)S(1)} %get-tuple-element.9.proj_ref, bf16[384,384]{1,0:T(8,128)(2,1)S(1)} %get-tuple-element.10.temporal_out_ref, f32[384]{0:T(512)S(1)} %copy-done.1, ...), custom_call_target="tpu_custom_call" | custom-call | tf_op jit(solution)/shard_map/temporal/pallas_call | solution.py:408
  21.4 9.3 %all_to_all.18 = bf16[16,4,384]{2,1,0:T(4,128)(2,1)S(1)} all-to-all(bf16[16,4,384]{2,1,0:T(4,128)(2,1)S(1)} %temporal.1), channel_id=1, replica_groups=mesh['parts'=2,'seq'=16] {'seq'}, dimensions={0} | all-to-all | bytes 98304 | tf_op jit(solution)/shard_map/all_to_all | solution.py:426
  30.8 0.0 copy-done.3
  30.8 0.0 copy-done.5
  30.8 0.0 copy-start.4
  30.8 0.6 %add_convert_fusion = bf16[1,64,384]{2,1,0:T(8,128)(2,1)} fusion(bf16[1,64,384]{2,1,0:T(8,128)(2,1)S(1)} %copy-done.5, bf16[1,64,384]{2,1,0:T(8,128)(2,1)S(1)} %all_to_all.14, bf16[1,64,384]{2,1,0:T(8,128)(2,1)S(1)} %copy-done.3), kind=kLoop, calls=%fused_computation | loop fusion | flops 196608 | bytes 196608 | tf_op jit(solution)/shard_map/convert_element_type | solution.py:431
  31.4 0.0 copy-done.4
  (1 shorter events, 0.0 us)
Async XLA Ops:
  0.6 18.6 %copy-start = (f32[384]{0:T(512)S(1)}, f32[384]{0:T(512)}, u32[]{:S(2)}) copy-start(f32[384]{0:T(512)} %gain_ref.1) | copy-start | bytes 4612
  0.6 18.6 %copy-start.1 = (f32[384]{0:T(512)S(1)}, f32[384]{0:T(512)}, u32[]{:S(2)}) copy-start(f32[384]{0:T(512)} %hidden_gain_ref.1) | copy-start | bytes 4612
  0.7 18.6 %copy-start.2 = (f32[384]{0:T(512)S(1)}, f32[384]{0:T(512)}, u32[]{:S(2)}) copy-start(f32[384]{0:T(512)} %head_gain_ref.1) | copy-start | bytes 4612
  19.2 11.5 %copy-start.3 = (bf16[1,64,384]{2,1,0:T(8,128)(2,1)S(1)}, bf16[1,64,384]{2,1,0:T(8,128)(2,1)}, u32[]{:S(2)}) copy-start(bf16[1,64,384]{2,1,0:T(8,128)(2,1)} %refs_0_.1) | copy-start | bytes 147460
  19.2 11.5 %copy-start.5 = (bf16[1,64,384]{2,1,0:T(8,128)(2,1)S(1)}, bf16[1,64,384]{2,1,0:T(8,128)(2,1)}, u32[]{:S(2)}) copy-start(bf16[1,64,384]{2,1,0:T(8,128)(2,1)} %param.22) | copy-start | bytes 147460
  30.8 0.7 %copy-start.4 = (bf16[1,64,384]{2,1,0:T(8,128)(2,1)}, bf16[1,64,384]{2,1,0:T(8,128)(2,1)S(1)}, u32[]{:S(2)}) copy-start(bf16[1,64,384]{2,1,0:T(8,128)(2,1)S(1)} %all_to_all.14) | copy-start | bytes 147460

commit v16 on v15

--- a/solution.py
+++ b/solution.py
@@ -54,8 +54,8 @@
 
 def spatial_kernel(groups, gamma_ref, *refs):
     sources, refs = refs[:11], refs[11:]
-    later, refs = refs[:5], refs[5:]
-    out_ref, later_out, refs = refs[0], refs[1:6], refs[6:]
+    later, refs = refs[:3], refs[3:]
+    out_ref, later_out, refs = refs[0], refs[1:4], refs[4:]
     local, (columns_ref, sems) = refs[:11], refs[11:]
     (
         x_ref,
@@ -286,11 +286,20 @@
     temporal_out_ref,
     hidden_gain_ref,
     hidden_in_ref,
+    hidden_source,
+    head_gain_ref,
+    head_source,
+    out_ref,
     hidden_out_ref,
-    head_gain_ref,
     head_out_ref,
-    out_ref,
+    sems,
 ):
+    copies = [
+        pltpu.make_async_copy(hidden_source, hidden_out_ref, sems.at[0]),
+        pltpu.make_async_copy(head_source, head_out_ref, sems.at[1]),
+    ]
+    for copy in copies:
+        copy.start()
     groups, depth, width = x_ref.shape
     rows = groups * depth
     head_dim = width // THEADS
@@ -332,6 +341,8 @@
         pieces.append(mixed * attends[index // block_heads][1][:, part * rows : (part + 1) * rows])
     context = jnp.concatenate(pieces, axis=0).astype(BF16).T
     after_time = initial + matmul(context, temporal_out_ref[...])
+    for copy in copies:
+        copy.wait()
     second = layer_norm(after_time, as_row(hidden_gain_ref)).astype(BF16)
     hidden = jax.nn.gelu(matmul(second, hidden_in_ref[...])).astype(BF16)
     result = (after_time + matmul(hidden, hidden_out_ref[...])).astype(BF16).astype(F32)
@@ -387,7 +398,7 @@
         spatial_points.T,
     )
     slots = 2 * (width // LANES)
-    later = (temporal_proj, temporal_out, hidden_in, hidden_out, head_out)
+    later = (temporal_proj, temporal_out, hidden_in)
     spatial, *later = pl.pallas_call(
         functools.partial(spatial_kernel, groups),
         out_shape=[pltpu.VMEM((groups, frames * period, width), BF16)]
@@ -404,12 +415,17 @@
         name="spatial",
     )(spatial_gamma, *sources, *later)
     arrived = lax.all_to_all(spatial, "seq", split_axis=0, concat_axis=0, tiled=True)
-    proj_local, out_local, in_local, hidden_local, head_local = later
+    proj_local, out_local, in_local = later
     guided = pl.pallas_call(
         functools.partial(temporal_kernel, period),
         out_shape=pltpu.VMEM((groups * frames, share, width), BF16),
-        in_specs=[whole()] * 9,
+        in_specs=[whole()] * 6 + [whole(pl.ANY), whole(), whole(pl.ANY)],
         out_specs=whole(),
+        scratch_shapes=[
+            pltpu.VMEM(hidden_out.shape, BF16),
+            pltpu.VMEM(head_out.shape, BF16),
+            pltpu.SemaphoreType.DMA((2,)),
+        ],
         compiler_params=pltpu.CompilerParams(vmem_limit_bytes=TEMPORAL_VMEM),
         name="temporal",
     )(
@@ -419,9 +435,9 @@
         out_local,
         hidden_gain,
         in_local,
-        hidden_local,
+        hidden_out,
         head_gain,
-        head_local,
+        head_out,
     )
     velocity = lax.all_to_all(guided, "seq", split_axis=0, concat_axis=1, tiled=True)
     x_next = (

time: 31.7 us -> 32 us (level)
    pallas_call x1, Pallas kernels: 2.15 us -> 2.48 us  [body(): pl.pallas_call(functools.partial(temporal_kernel, period), out_shape=pltp...]
where the time goes in v16:
time: 32 us; the launch traced here: 31.8 us
  blocking collectives  23.9 us (75%)
  Pallas kernels  6.38 us (20%)
  between operations  0.76 us (2%)
  other arithmetic  0.65 us (2%)
    all_to_all x1, blocking collectives, body(): lax.all_to_all(spatial, 'seq', split_axis=0, concat_axis=0, tiled=True)  14.6 us
    all_to_all x1, blocking collectives, body(): lax.all_to_all(guided, 'seq', split_axis=0, concat_axis=1, tiled=True)  9.34 us
    pallas_call x1, Pallas kernels, body(): pl.pallas_call(functools.partial(spatial_kernel, groups), out_shape=[pltp...  3.9 us
    pallas_call x1, Pallas kernels, body(): pl.pallas_call(functools.partial(temporal_kernel, period), out_shape=pltp...  2.48 us
    convert_element_type x1, other arithmetic, body(): x_next = (x_state.astype(F32) + STEP_SIZE * velocity.astype(F32) + NOISE_...  0.65 us

profile of v16, /device:TPU:0, one launch (start us, length us, event | category | flops | bytes accessed | tf_op | source)
XLA Modules:
  0.0 31.8 jit_solution(5480165077066154343)
XLA Ops:
  0.6 0.0 copy-start
  0.6 0.0 copy-start.1
  0.7 0.0 copy-start.2
  0.7 0.0 copy-start.3
  0.7 0.0 copy-start.4
  0.7 3.9 %spatial.1 = (bf16[16,8,384]{2,1,0:T(8,128)(2,1)S(1)}, bf16[384,1152]{1,0:T(8,128)(2,1)S(1)}, bf16[384,384]{1,0:T(8,128)(2,1)S(1)}, bf16[384,1536]{1,0:T(8,128)(2,1)S(1)}) custom-call(f32[12]{0:T(128)} %gamma_ref.1, bf16[1,64,384]{2,1,0:T(8,128)(2,1)} %refs_0_.1, bf16[21,384]{1,0:T(8,128)(2,1)} %refs_1_.1, s32[1,64]{1,0:T(1,128)} %bitcast.4, ...), custom_call_target="tpu_custom_call" | custom-call | tf_op jit(solution)/shard_map/spatial/pallas_call | solution.py:402
  4.6 14.6 %all_to_all.17.x_ref = bf16[16,8,384]{2,1,0:T(8,128)(2,1)S(1)} all-to-all(bf16[16,8,384]{2,1,0:T(8,128)(2,1)S(1)} %get-tuple-element.6), channel_id=1, replica_groups=mesh['parts'=2,'seq'=16] {'seq'}, dimensions={0} | all-to-all | bytes 196608 | tf_op jit(solution)/shard_map/all_to_all | solution.py:417
  19.2 0.0 copy-done
  19.2 0.0 copy-done.1
  19.2 0.0 copy-done.2
  19.2 0.0 copy-done.3
  19.2 0.0 copy-done.4
  19.2 0.0 copy-start.5
  19.2 0.0 copy-start.7
  19.2 2.5 %temporal.1 = bf16[16,4,384]{2,1,0:T(4,128)(2,1)S(1)} custom-call(bf16[16,8,384]{2,1,0:T(8,128)(2,1)S(1)} %all_to_all.17.x_ref, f32[384]{0:T(512)S(1)} %copy-done.2, bf16[384,1152]{1,0:T(8,128)(2,1)S(1)} %get-tuple-element.7.proj_ref, bf16[384,384]{1,0:T(8,128)(2,1)S(1)} %get-tuple-element.8.temporal_out_ref, f32[384]{0:T(512)S(1)} %copy-done.3, ...), custom_call_target="tpu_custom_call" | custom-call | tf_op jit(solution)/shard_map/temporal/pallas_call | solution.py:419
  21.7 9.3 %all_to_all.18 = bf16[16,4,384]{2,1,0:T(4,128)(2,1)S(1)} all-to-all(bf16[16,4,384]{2,1,0:T(4,128)(2,1)S(1)} %temporal.1), channel_id=1, replica_groups=mesh['parts'=2,'seq'=16] {'seq'}, dimensions={0} | all-to-all | bytes 98304 | tf_op jit(solution)/shard_map/all_to_all | solution.py:442
  31.1 0.0 copy-done.5
  31.1 0.0 copy-done.7
  31.1 0.0 copy-start.6
  31.1 0.6 %add_convert_fusion = bf16[1,64,384]{2,1,0:T(8,128)(2,1)} fusion(bf16[1,64,384]{2,1,0:T(8,128)(2,1)S(1)} %copy-done.7, bf16[1,64,384]{2,1,0:T(8,128)(2,1)S(1)} %all_to_all.14, bf16[1,64,384]{2,1,0:T(8,128)(2,1)S(1)} %copy-done.5), kind=kLoop, calls=%fused_computation | loop fusion | flops 196608 | bytes 196608 | tf_op jit(solution)/shard_map/convert_element_type | solution.py:447
  31.8 0.0 copy-done.6
  (1 shorter events, 0.0 us)
Async XLA Ops:
  0.6 18.6 %copy-start = (bf16[1536,384]{1,0:T(8,128)(2,1)S(1)}, bf16[1536,384]{1,0:T(8,128)(2,1)}, u32[]{:S(2)}) copy-start(bf16[1536,384]{1,0:T(8,128)(2,1)} %hidden_source.1) | copy-start | bytes 3538948
  0.6 18.5 %copy-start.1 = (bf16[384,384]{1,0:T(8,128)(2,1)S(1)}, bf16[384,384]{1,0:T(8,128)(2,1)}, u32[]{:S(2)}) copy-start(bf16[384,384]{1,0:T(8,128)(2,1)} %head_source.1) | copy-start | bytes 884740
  0.7 18.5 %copy-start.2 = (f32[384]{0:T(512)S(1)}, f32[384]{0:T(512)}, u32[]{:S(2)}) copy-start(f32[384]{0:T(512)} %gain_ref.1) | copy-start | bytes 4612
  0.7 18.5 %copy-start.3 = (f32[384]{0:T(512)S(1)}, f32[384]{0:T(512)}, u32[]{:S(2)}) copy-start(f32[384]{0:T(512)} %hidden_gain_ref.1) | copy-start | bytes 4612
  0.7 18.5 %copy-start.4 = (f32[384]{0:T(512)S(1)}, f32[384]{0:T(512)}, u32[]{:S(2)}) copy-start(f32[384]{0:T(512)} %head_gain_ref.1) | copy-start | bytes 4612
  19.2 11.9 %copy-start.5 = (bf16[1,64,384]{2,1,0:T(8,128)(2,1)S(1)}, bf16[1,64,384]{2,1,0:T(8,128)(2,1)}, u32[]{:S(2)}) copy-start(bf16[1,64,384]{2,1,0:T(8,128)(2,1)} %refs_0_.1) | copy-start | bytes 147460
  19.2 11.9 %copy-start.7 = (bf16[1,64,384]{2,1,0:T(8,128)(2,1)S(1)}, bf16[1,64,384]{2,1,0:T(8,128)(2,1)}, u32[]{:S(2)}) copy-start(bf16[1,64,384]{2,1,0:T(8,128)(2,1)} %param.22) | copy-start | bytes 147460
  31.1 0.7 %copy-start.6 = (bf16[1,64,384]{2,1,0:T(8,128)(2,1)}, bf16[1,64,384]{2,1,0:T(8,128)(2,1)S(1)}, u32[]{:S(2)}) copy-start(bf16[1,64,384]{2,1,0:T(8,128)(2,1)S(1)} %all_to_all.14) | copy-start | bytes 147460

commit v17 on v15

--- a/solution.py
+++ b/solution.py
@@ -82,23 +82,30 @@
     stacked_rows = block_heads * residues
     point_scale = 0.5 * WEIGHT_LOGIT * WEIGHT_POINT
 
-    pairs = list(zip(sources[:8], local[:8], strict=True))
-    for slot in range(2 * blocks):
-        pairs.append(
-            (
-                sources[-1].at[pl.ds(slot * slot_rows, slot_rows), :],
-                points_ref.at[pl.ds(slot * SLOT, slot_rows), :],
-            )
+    whole_pairs = list(zip(sources[:10], local[:10], strict=True))
+    slot_pairs = [
+        (
+            sources[-1].at[pl.ds(slot * slot_rows, slot_rows), :],
+            points_ref.at[pl.ds(slot * SLOT, slot_rows), :],
         )
-    pairs += list(zip(sources[8:10] + later, local[8:10] + tuple(later_out), strict=True))
-    copies = [
-        pltpu.make_async_copy(source, target, sems.at[index])
-        for index, (source, target) in enumerate(pairs)
+        for slot in range(2 * blocks)
     ]
-    first = 10 + 2 * blocks
-    for copy in copies[:first]:
+    stages = [
+        [whole_pairs[2], whole_pairs[1]],
+        [whole_pairs[0], whole_pairs[3], whole_pairs[4]],
+        slot_pairs + [whole_pairs[8]] + whole_pairs[5:8],
+        [whole_pairs[9]],
+        list(zip(later, later_out, strict=True)),
+    ]
+    copies, index = [], 0
+    for stage in stages:
+        copies.append([])
+        for source, target in stage:
+            copies[-1].append(pltpu.make_async_copy(source, target, sems.at[index]))
+            index += 1
+    for_embed, for_norm, for_points, for_update, for_later = copies
+    for copy in for_embed + for_norm + for_points + for_update:
         copy.start()
-    small, wide, after = copies[:8], copies[8 : first - 1], copies[first - 1]
 
     for slot in range(2 * blocks):
         points_ref[slot * SLOT + slot_rows : (slot + 1) * SLOT, :] = jnp.zeros(
@@ -128,13 +135,15 @@
     same = iota((residues, stacked_rows), 0) == iota((residues, stacked_rows), 1) % residues
     columns_ref[...] = jnp.zeros_like(columns_ref)
 
-    for copy in small:
+    for copy in for_embed:
         copy.wait()
-    for copy in copies[first:]:
-        copy.start()
     kinds = table_ref.shape[0]
     onehot = (iota((kinds, residues), 0) == types_ref[...]).astype(F32).T.astype(BF16)
     conditional = matmul(onehot, table_ref[...])
+    for copy in for_norm:
+        copy.wait()
+    for copy in for_later:
+        copy.start()
     empty = as_row(null_ref).astype(F32)
 
     tiles = []
@@ -143,6 +152,11 @@
         initial = jnp.concatenate([state + conditional, state + empty], axis=0)
         normed = layer_norm(initial, as_row(gain_ref)).astype(BF16)
 
+        if frame == 0:
+            for copy in for_points:
+                copy.wait()
+        points = lax.dot_general(normed, points_ref[...], NT, preferred_element_type=F32)
+        projected = matmul(normed, proj_ref[...])
         columns_ref[0:9, :] = rotation_ref[:, frame, :]
         moved = translation_ref[:, frame, :]
         columns_ref[9:12, :] = moved - jnp.mean(moved, axis=1, keepdims=True)
@@ -161,12 +175,6 @@
         for row in range(3):
             anchor = jnp.where(component == row, columns[:, 9 + row : 10 + row], anchor)
         anchor = jnp.concatenate([anchor] * BRANCHES, axis=0)
-
-        if frame == 0:
-            for copy in wide:
-                copy.wait()
-        points = lax.dot_general(normed, points_ref[...], NT, preferred_element_type=F32)
-        projected = matmul(normed, proj_ref[...])
 
         queries = (
             projected[:, :width].astype(BF16) * jnp.asarray(WEIGHT_LOGIT / math.sqrt(head_dim), BF16)
@@ -257,7 +265,8 @@
                 joined = joined + context[start : start + residues]
             contexts.append(joined)
         if frame == 0:
-            after.wait()
+            for copy in for_update:
+                copy.wait()
         update = matmul(jnp.concatenate(contexts, axis=0), spatial_out_ref[...])
         total = initial + update
         tiles.append(
@@ -274,7 +283,7 @@
         )
     for group in range(groups):
         out_ref[group] = jnp.concatenate([tile[group] for tile in tiles], axis=0).astype(BF16)
-    for copy in copies[first:]:
+    for copy in for_later:
         copy.wait()
 
 

time: 31.7 us -> 31.8 us (level)
  no operation moved by 1% of the time
where the time goes in v17:
time: 31.8 us; the launch traced here: 31.5 us
  blocking collectives  23.9 us (75%)
  Pallas kernels  6.19 us (19%)
  between operations  0.72 us (2%)
  other arithmetic  0.65 us (2%)
    all_to_all x1, blocking collectives, body(): lax.all_to_all(spatial, 'seq', split_axis=0, concat_axis=0, tiled=True)  14.6 us
    all_to_all x1, blocking collectives, body(): lax.all_to_all(guided, 'seq', split_axis=0, concat_axis=1, tiled=True)  9.34 us
    pallas_call x1, Pallas kernels, body(): pl.pallas_call(functools.partial(spatial_kernel, groups), out_shape=[pltp...  4.05 us
    pallas_call x1, Pallas kernels, body(): pl.pallas_call(functools.partial(temporal_kernel, period), out_shape=pltp...  2.15 us
    convert_element_type x1, other arithmetic, body(): x_next = (x_state.astype(F32) + STEP_SIZE * velocity.astype(F32) + NOISE_...  0.65 us

profile of v17, /device:TPU:0, one launch (start us, length us, event | category | flops | bytes accessed | tf_op | source)
XLA Modules:
  0.0 31.5 jit_solution(1193574471662974416)
XLA Ops:
  0.6 0.0 copy-start
  0.6 0.0 copy-start.1
  0.7 0.0 copy-start.2
  0.7 4.0 %spatial.1 = (bf16[16,8,384]{2,1,0:T(8,128)(2,1)S(1)}, bf16[384,1152]{1,0:T(8,128)(2,1)S(1)}, bf16[384,384]{1,0:T(8,128)(2,1)S(1)}, bf16[384,1536]{1,0:T(8,128)(...) custom-call(f32[12]{0:T(128)} %gamma_ref.1, bf16[1,64,384]{2,1,0:T(8,128)(2,1)} %refs_0_.1, ...), custom_call_target="tpu_custom_call" | custom-call | tf_op jit(solution)/shard_map/spatial/pallas_call | solution.py:400
  4.7 14.6 %all_to_all.17.x_ref = bf16[16,8,384]{2,1,0:T(8,128)(2,1)S(1)} all-to-all(bf16[16,8,384]{2,1,0:T(8,128)(2,1)S(1)} %get-tuple-element.8), channel_id=1, replica_groups=mesh['parts'=2,'seq'=16] {'seq'}, dimensions={0} | all-to-all | bytes 196608 | tf_op jit(solution)/shard_map/all_to_all | solution.py:415
  19.3 0.0 copy-done
  19.3 0.0 copy-done.1
  19.3 0.0 copy-done.2
  19.3 0.0 copy-start.3
  19.3 0.0 copy-start.5
  19.4 2.1 %temporal.1 = bf16[16,4,384]{2,1,0:T(4,128)(2,1)S(1)} custom-call(bf16[16,8,384]{2,1,0:T(8,128)(2,1)S(1)} %all_to_all.17.x_ref, f32[384]{0:T(512)S(1)} %copy-done, bf16[384,1152]{1,0:T(8,128)(2,1)S(1)} %get-tuple-element.9.proj_ref, bf16[384,384]{1,0:T(8,128)(2,1)S(1)} %get-tuple-element.10.temporal_out_ref, f32[384]{0:T(512)S(1)} %copy-done.1, ...), custom_call_target="tpu_custom_call" | custom-call | tf_op jit(solution)/shard_map/temporal/pallas_call | solution.py:417
  21.5 9.3 %all_to_all.18 = bf16[16,4,384]{2,1,0:T(4,128)(2,1)S(1)} all-to-all(bf16[16,4,384]{2,1,0:T(4,128)(2,1)S(1)} %temporal.1), channel_id=1, replica_groups=mesh['parts'=2,'seq'=16] {'seq'}, dimensions={0} | all-to-all | bytes 98304 | tf_op jit(solution)/shard_map/all_to_all | solution.py:435
  30.9 0.0 copy-done.3
  30.9 0.0 copy-done.5
  30.9 0.0 copy-start.4
  30.9 0.6 %add_convert_fusion = bf16[1,64,384]{2,1,0:T(8,128)(2,1)} fusion(bf16[1,64,384]{2,1,0:T(8,128)(2,1)S(1)} %copy-done.5, bf16[1,64,384]{2,1,0:T(8,128)(2,1)S(1)} %all_to_all.14, bf16[1,64,384]{2,1,0:T(8,128)(2,1)S(1)} %copy-done.3), kind=kLoop, calls=%fused_computation | loop fusion | flops 196608 | bytes 196608 | tf_op jit(solution)/shard_map/convert_element_type | solution.py:440
  31.5 0.0 copy-done.4
  (1 shorter events, 0.0 us)
Async XLA Ops:
  0.6 18.7 %copy-start = (f32[384]{0:T(512)S(1)}, f32[384]{0:T(512)}, u32[]{:S(2)}) copy-start(f32[384]{0:T(512)} %gain_ref.1) | copy-start | bytes 4612
  0.6 18.7 %copy-start.1 = (f32[384]{0:T(512)S(1)}, f32[384]{0:T(512)}, u32[]{:S(2)}) copy-start(f32[384]{0:T(512)} %hidden_gain_ref.1) | copy-start | bytes 4612
  0.7 18.7 %copy-start.2 = (f32[384]{0:T(512)S(1)}, f32[384]{0:T(512)}, u32[]{:S(2)}) copy-start(f32[384]{0:T(512)} %head_gain_ref.1) | copy-start | bytes 4612
  19.3 11.5 %copy-start.3 = (bf16[1,64,384]{2,1,0:T(8,128)(2,1)S(1)}, bf16[1,64,384]{2,1,0:T(8,128)(2,1)}, u32[]{:S(2)}) copy-start(bf16[1,64,384]{2,1,0:T(8,128)(2,1)} %refs_0_.1) | copy-start | bytes 147460
  19.3 11.5 %copy-start.5 = (bf16[1,64,384]{2,1,0:T(8,128)(2,1)S(1)}, bf16[1,64,384]{2,1,0:T(8,128)(2,1)}, u32[]{:S(2)}) copy-start(bf16[1,64,384]{2,1,0:T(8,128)(2,1)} %param.22) | copy-start | bytes 147460
  30.9 0.7 %copy-start.4 = (bf16[1,64,384]{2,1,0:T(8,128)(2,1)}, bf16[1,64,384]{2,1,0:T(8,128)(2,1)S(1)}, u32[]{:S(2)}) copy-start(bf16[1,64,384]{2,1,0:T(8,128)(2,1)S(1)} %all_to_all.14) | copy-start | bytes 147460

commit v18 on v11

--- a/solution.py
+++ b/solution.py
@@ -22,7 +22,6 @@
 F32 = jnp.float32
 LANES = 128
 SLOT = 64
-FEED = 512
 SPATIAL_VMEM = 56 * 2**20
 TEMPORAL_VMEM = 40 * 2**20
 NT = (((1,), (1,)), ((), ()))
@@ -131,6 +130,8 @@
 
     for copy in small:
         copy.wait()
+    for copy in copies[first:]:
+        copy.start()
     kinds = table_ref.shape[0]
     onehot = (iota((kinds, residues), 0) == types_ref[...]).astype(F32).T.astype(BF16)
     conditional = matmul(onehot, table_ref[...])
@@ -164,8 +165,6 @@
         if frame == 0:
             for copy in wide:
                 copy.wait()
-            for copy in copies[first:]:
-                copy.start()
         points = lax.dot_general(normed, points_ref[...], NT, preferred_element_type=F32)
         projected = matmul(normed, proj_ref[...])
 
@@ -329,16 +328,8 @@
     context = jnp.concatenate(pieces, axis=0).astype(BF16).T
     after_time = initial + matmul(context, temporal_out_ref[...])
     second = layer_norm(after_time, as_row(hidden_gain_ref)).astype(BF16)
-    feed = hidden_in_ref.shape[1]
-    columns = [slice(start, start + FEED) for start in range(0, feed, FEED)]
-    wide = [matmul(second, hidden_in_ref[:, columns[0]])]
-    result = after_time
-    for index, column in enumerate(columns):
-        if index + 1 < len(columns):
-            wide.append(matmul(second, hidden_in_ref[:, columns[index + 1]]))
-        hidden = jax.nn.gelu(wide[index]).astype(BF16)
-        result = result + matmul(hidden, hidden_out_ref[column, :])
-    result = result.astype(BF16).astype(F32)
+    hidden = jax.nn.gelu(matmul(second, hidden_in_ref[...])).astype(BF16)
+    result = (after_time + matmul(hidden, hidden_out_ref[...])).astype(BF16).astype(F32)
     headed = layer_norm(result, as_row(head_gain_ref)).astype(BF16)
     branch_velocity = matmul(headed, head_out_ref[...]).reshape(rows // period, period, width)
     conditional = branch_velocity[:, :share]

time: 32.4 us -> 31.7 us (0.978)
  Pallas kernels: 6.82 us -> 6.08 us
    pallas_call x1, Pallas kernels: 4.6 us -> 3.93 us  [body(): pl.pallas_call(functools.partial(spatial_kernel, groups), out_shape=[pltp...]
where the time goes in v18:
time: 31.7 us; the launch traced here: 31.4 us
  blocking collectives  23.9 us (75%)
  Pallas kernels  6.08 us (19%)
  between operations  0.72 us (2%)
  other arithmetic  0.65 us (2%)
    all_to_all x1, blocking collectives, body(): lax.all_to_all(spatial, 'seq', split_axis=0, concat_axis=0, tiled=True)  14.6 us
    all_to_all x1, blocking collectives, body(): lax.all_to_all(guided, 'seq', split_axis=0, concat_axis=1, tiled=True)  9.34 us
    pallas_call x1, Pallas kernels, body(): pl.pallas_call(functools.partial(spatial_kernel, groups), out_shape=[pltp...  3.93 us
    pallas_call x1, Pallas kernels, body(): pl.pallas_call(functools.partial(temporal_kernel, period), out_shape=pltp...  2.14 us
    convert_element_type x1, other arithmetic, body(): x_next = (x_state.astype(F32) + STEP_SIZE * velocity.astype(F32) + NOISE_...  0.65 us

profile of v18, /device:TPU:0, one launch (start us, length us, event | category | flops | bytes accessed | tf_op | source)
XLA Modules:
  0.0 31.4 jit_solution(11711345504893631701)
XLA Ops:
  0.6 0.0 copy-start
  0.6 0.0 copy-start.1
  0.7 0.0 copy-start.2
  0.7 3.9 %spatial.1 = (bf16[16,8,384]{2,1,0:T(8,128)(2,1)S(1)}, bf16[384,1152]{1,0:T(8,128)(2,1)S(1)}, bf16[384,384]{1,0:T(8,128)(2,1)S(1)}, bf16[384,1536]{1,0:T(8,128)(...) custom-call(f32[12]{0:T(128)} %gamma_ref.1, bf16[1,64,384]{2,1,0:T(8,128)(2,1)} %refs_0_.1, ...), custom_call_target="tpu_custom_call" | custom-call | tf_op jit(solution)/shard_map/spatial/pallas_call | solution.py:386
  4.6 14.6 %all_to_all.17.x_ref = bf16[16,8,384]{2,1,0:T(8,128)(2,1)S(1)} all-to-all(bf16[16,8,384]{2,1,0:T(8,128)(2,1)S(1)} %get-tuple-element.8), channel_id=1, replica_groups=mesh['parts'=2,'seq'=16] {'seq'}, dimensions={0} | all-to-all | bytes 196608 | tf_op jit(solution)/shard_map/all_to_all | solution.py:401
  19.2 0.0 copy-done
  19.2 0.0 copy-done.1
  19.2 0.0 copy-done.2
  19.2 0.0 copy-start.3
  19.2 0.0 copy-start.5
  19.2 2.1 %temporal.1 = bf16[16,4,384]{2,1,0:T(4,128)(2,1)S(1)} custom-call(bf16[16,8,384]{2,1,0:T(8,128)(2,1)S(1)} %all_to_all.17.x_ref, f32[384]{0:T(512)S(1)} %copy-done, bf16[384,1152]{1,0:T(8,128)(2,1)S(1)} %get-tuple-element.9.proj_ref, bf16[384,384]{1,0:T(8,128)(2,1)S(1)} %get-tuple-element.10.temporal_out_ref, f32[384]{0:T(512)S(1)} %copy-done.1, ...), custom_call_target="tpu_custom_call" | custom-call | tf_op jit(solution)/shard_map/temporal/pallas_call | solution.py:403
  21.4 9.3 %all_to_all.18 = bf16[16,4,384]{2,1,0:T(4,128)(2,1)S(1)} all-to-all(bf16[16,4,384]{2,1,0:T(4,128)(2,1)S(1)} %temporal.1), channel_id=1, replica_groups=mesh['parts'=2,'seq'=16] {'seq'}, dimensions={0} | all-to-all | bytes 98304 | tf_op jit(solution)/shard_map/all_to_all | solution.py:421
  30.7 0.0 copy-done.3
  30.8 0.0 copy-done.5
  30.8 0.0 copy-start.4
  30.8 0.6 %add_convert_fusion = bf16[1,64,384]{2,1,0:T(8,128)(2,1)} fusion(bf16[1,64,384]{2,1,0:T(8,128)(2,1)S(1)} %copy-done.5, bf16[1,64,384]{2,1,0:T(8,128)(2,1)S(1)} %all_to_all.14, bf16[1,64,384]{2,1,0:T(8,128)(2,1)S(1)} %copy-done.3), kind=kLoop, calls=%fused_computation | loop fusion | flops 196608 | bytes 196608 | tf_op jit(solution)/shard_map/convert_element_type | solution.py:426
  31.4 0.0 copy-done.4
  (1 shorter events, 0.0 us)
Async XLA Ops:
  0.6 18.6 %copy-start = (f32[384]{0:T(512)S(1)}, f32[384]{0:T(512)}, u32[]{:S(2)}) copy-start(f32[384]{0:T(512)} %gain_ref.1) | copy-start | bytes 4612
  0.6 18.6 %copy-start.1 = (f32[384]{0:T(512)S(1)}, f32[384]{0:T(512)}, u32[]{:S(2)}) copy-start(f32[384]{0:T(512)} %hidden_gain_ref.1) | copy-start | bytes 4612
  0.7 18.6 %copy-start.2 = (f32[384]{0:T(512)S(1)}, f32[384]{0:T(512)}, u32[]{:S(2)}) copy-start(f32[384]{0:T(512)} %head_gain_ref.1) | copy-start | bytes 4612
  19.2 11.5 %copy-start.3 = (bf16[1,64,384]{2,1,0:T(8,128)(2,1)S(1)}, bf16[1,64,384]{2,1,0:T(8,128)(2,1)}, u32[]{:S(2)}) copy-start(bf16[1,64,384]{2,1,0:T(8,128)(2,1)} %refs_0_.1) | copy-start | bytes 147460
  19.2 11.5 %copy-start.5 = (bf16[1,64,384]{2,1,0:T(8,128)(2,1)S(1)}, bf16[1,64,384]{2,1,0:T(8,128)(2,1)}, u32[]{:S(2)}) copy-start(bf16[1,64,384]{2,1,0:T(8,128)(2,1)} %param.22) | copy-start | bytes 147460
  30.8 0.7 %copy-start.4 = (bf16[1,64,384]{2,1,0:T(8,128)(2,1)}, bf16[1,64,384]{2,1,0:T(8,128)(2,1)S(1)}, u32[]{:S(2)}) copy-start(bf16[1,64,384]{2,1,0:T(8,128)(2,1)S(1)} %all_to_all.14) | copy-start | bytes 147460

commit v19 on v18

--- a/solution.py
+++ b/solution.py
@@ -133,8 +133,10 @@
     for copy in copies[first:]:
         copy.start()
     kinds = table_ref.shape[0]
-    onehot = (iota((kinds, residues), 0) == types_ref[...]).astype(F32).T.astype(BF16)
-    conditional = matmul(onehot, table_ref[...])
+    onehot = (iota((kinds, residues), 0) == types_ref[...]).astype(F32).astype(BF16)
+    conditional = lax.dot_general(
+        onehot, table_ref[...], (((0,), (0,)), ((), ())), preferred_element_type=F32
+    )
     empty = as_row(null_ref).astype(F32)
 
     tiles = []

time: 31.7 us -> 31.7 us (level)
  no operation moved by 1% of the time
where the time goes in v19:
time: 31.7 us; the launch traced here: 31.4 us
  blocking collectives  23.9 us (75%)
  Pallas kernels  6.09 us (19%)
  between operations  0.72 us (2%)
  other arithmetic  0.65 us (2%)
    all_to_all x1, blocking collectives, body(): lax.all_to_all(spatial, 'seq', split_axis=0, concat_axis=0, tiled=True)  14.6 us
    all_to_all x1, blocking collectives, body(): lax.all_to_all(guided, 'seq', split_axis=0, concat_axis=1, tiled=True)  9.34 us
    pallas_call x1, Pallas kernels, body(): pl.pallas_call(functools.partial(spatial_kernel, groups), out_shape=[pltp...  3.93 us
    pallas_call x1, Pallas kernels, body(): pl.pallas_call(functools.partial(temporal_kernel, period), out_shape=pltp...  2.16 us
    convert_element_type x1, other arithmetic, body(): x_next = (x_state.astype(F32) + STEP_SIZE * velocity.astype(F32) + NOISE_...  0.65 us

profile of v19, /device:TPU:0, one launch (start us, length us, event | category | flops | bytes accessed | tf_op | source)
XLA Modules:
  0.0 31.4 jit_solution(16935107075426532343)
XLA Ops:
  0.6 0.0 copy-start
  0.6 0.0 copy-start.1
  0.7 0.0 copy-start.2
  0.7 3.9 %spatial.1 = (bf16[16,8,384]{2,1,0:T(8,128)(2,1)S(1)}, bf16[384,1152]{1,0:T(8,128)(2,1)S(1)}, bf16[384,384]{1,0:T(8,128)(2,1)S(1)}, bf16[384,1536]{1,0:T(8,128)(...) custom-call(f32[12]{0:T(128)} %gamma_ref.1, bf16[1,64,384]{2,1,0:T(8,128)(2,1)} %refs_0_.1, ...), custom_call_target="tpu_custom_call" | custom-call | tf_op jit(solution)/shard_map/spatial/pallas_call | solution.py:388
  4.6 14.6 %all_to_all.17.x_ref = bf16[16,8,384]{2,1,0:T(8,128)(2,1)S(1)} all-to-all(bf16[16,8,384]{2,1,0:T(8,128)(2,1)S(1)} %get-tuple-element.8), channel_id=1, replica_groups=mesh['parts'=2,'seq'=16] {'seq'}, dimensions={0} | all-to-all | bytes 196608 | tf_op jit(solution)/shard_map/all_to_all | solution.py:403
  19.2 0.0 copy-done
  19.2 0.0 copy-done.1
  19.2 0.0 copy-done.2
  19.2 0.0 copy-start.3
  19.2 0.0 copy-start.5
  19.2 2.2 %temporal.1 = bf16[16,4,384]{2,1,0:T(4,128)(2,1)S(1)} custom-call(bf16[16,8,384]{2,1,0:T(8,128)(2,1)S(1)} %all_to_all.17.x_ref, f32[384]{0:T(512)S(1)} %copy-done, bf16[384,1152]{1,0:T(8,128)(2,1)S(1)} %get-tuple-element.9.proj_ref, bf16[384,384]{1,0:T(8,128)(2,1)S(1)} %get-tuple-element.10.temporal_out_ref, f32[384]{0:T(512)S(1)} %copy-done.1, ...), custom_call_target="tpu_custom_call" | custom-call | tf_op jit(solution)/shard_map/temporal/pallas_call | solution.py:405
  21.4 9.3 %all_to_all.18 = bf16[16,4,384]{2,1,0:T(4,128)(2,1)S(1)} all-to-all(bf16[16,4,384]{2,1,0:T(4,128)(2,1)S(1)} %temporal.1), channel_id=1, replica_groups=mesh['parts'=2,'seq'=16] {'seq'}, dimensions={0} | all-to-all | bytes 98304 | tf_op jit(solution)/shard_map/all_to_all | solution.py:423
  30.8 0.0 copy-done.3
  30.8 0.0 copy-done.5
  30.8 0.0 copy-start.4
  30.8 0.6 %add_convert_fusion = bf16[1,64,384]{2,1,0:T(8,128)(2,1)} fusion(bf16[1,64,384]{2,1,0:T(8,128)(2,1)S(1)} %copy-done.5, bf16[1,64,384]{2,1,0:T(8,128)(2,1)S(1)} %all_to_all.14, bf16[1,64,384]{2,1,0:T(8,128)(2,1)S(1)} %copy-done.3), kind=kLoop, calls=%fused_computation | loop fusion | flops 196608 | bytes 196608 | tf_op jit(solution)/shard_map/convert_element_type | solution.py:428
  31.4 0.0 copy-done.4
  (1 shorter events, 0.0 us)
Async XLA Ops:
  0.6 18.6 %copy-start = (f32[384]{0:T(512)S(1)}, f32[384]{0:T(512)}, u32[]{:S(2)}) copy-start(f32[384]{0:T(512)} %gain_ref.1) | copy-start | bytes 4612
  0.6 18.6 %copy-start.1 = (f32[384]{0:T(512)S(1)}, f32[384]{0:T(512)}, u32[]{:S(2)}) copy-start(f32[384]{0:T(512)} %hidden_gain_ref.1) | copy-start | bytes 4612
  0.7 18.6 %copy-start.2 = (f32[384]{0:T(512)S(1)}, f32[384]{0:T(512)}, u32[]{:S(2)}) copy-start(f32[384]{0:T(512)} %head_gain_ref.1) | copy-start | bytes 4612
  19.2 11.5 %copy-start.3 = (bf16[1,64,384]{2,1,0:T(8,128)(2,1)S(1)}, bf16[1,64,384]{2,1,0:T(8,128)(2,1)}, u32[]{:S(2)}) copy-start(bf16[1,64,384]{2,1,0:T(8,128)(2,1)} %refs_0_.1) | copy-start | bytes 147460
  19.2 11.5 %copy-start.5 = (bf16[1,64,384]{2,1,0:T(8,128)(2,1)S(1)}, bf16[1,64,384]{2,1,0:T(8,128)(2,1)}, u32[]{:S(2)}) copy-start(bf16[1,64,384]{2,1,0:T(8,128)(2,1)} %param.22) | copy-start | bytes 147460
  30.8 0.7 %copy-start.4 = (bf16[1,64,384]{2,1,0:T(8,128)(2,1)}, bf16[1,64,384]{2,1,0:T(8,128)(2,1)S(1)}, u32[]{:S(2)}) copy-start(bf16[1,64,384]{2,1,0:T(8,128)(2,1)S(1)} %all_to_all.14) | copy-start | bytes 147460
